TPU v7x, 128 devices: a whole 4x4x4 slice. The times are simulated.
128 devices in a mesh: fsdp: 16 (over x, z_hi, core), replica: 8 (over y, z_lo).
Axes of the slice: x: 4, y: 4, z: 4 (z_hi: 2, z_lo: 2; z = z_hi * 2 + z_lo), core: 2. Of those that a mesh axis runs over, the one named last changes fastest.
Arguments:
- tokens: bfloat16 [131072, 4096], P(('fsdp', 'replica')), may hold values from -180 to 180
- norm_gain: float32 [4096], replicated, may hold values from 0.1 to 1.9
- key_weight: bfloat16 [4096, 512], P('fsdp'), may hold values from -0.09375 to 0.09375
- value_weight: bfloat16 [4096, 512], P('fsdp'), may hold values from -0.09375 to 0.09375
- key_cotangent: bfloat16 [131072, 512], P(('fsdp', 'replica')), may hold values from -6 to 6
- value_cotangent: bfloat16 [131072, 512], P(('fsdp', 'replica')), may hold values from -6 to 6
Outputs:
- rotated_keys: bfloat16 [131072, 512], P(('fsdp', 'replica'))
- value_rows: bfloat16 [131072, 512], P(('fsdp', 'replica'))
- input_grad: bfloat16 [131072, 4096], P(('fsdp', 'replica'))
- key_weight_grad: float32 [4096, 512], P('fsdp')
- value_weight_grad: float32 [4096, 512], P('fsdp')
- gain_grad: float32 [4096], replicated
All inputs are finite; a program needn't handle non-finite values.
Results may differ from a plain program's by a relative error of at most 0.005.
Values may be sent and summed in bfloat16 or wider, within the bound.
No kernel may reach another device: no remote copies, remote signals or barrier semaphores. Data moves between devices by JAX's collectives and lax.ppermute only.
A program may use at most 192 MiB of HBM per device.

v0:
```python
import math

import jax
import jax.numpy as jnp
from jax import lax
from jax.sharding import PartitionSpec as P

HEAD = 128


def tables(length):
    half = HEAD // 2
    places = jnp.arange(length, dtype=jnp.float32)
    inverse = jnp.exp(-(2.0 * jnp.arange(half, dtype=jnp.float32) / HEAD) * math.log(500000.0))
    angles = places[:, None] * inverse[None, :]
    return (jnp.cos(angles)[:, None, :], jnp.sin(angles)[:, None, :])


def rotate(values, cosine, sine, direction):
    length = values.shape[0]
    half = HEAD // 2
    heads = values.reshape(length, -1, HEAD)
    first = heads[..., :half]
    second = heads[..., half:]
    out_first = first * cosine - direction * second * sine
    out_second = second * cosine + direction * first * sine
    return jnp.concatenate([out_first, out_second], axis=2).reshape(length, -1)


def shards(tokens, norm_gain, key_weight, value_weight, key_cotangent, value_cotangent):
    length = tokens.shape[0]
    feats = key_weight.shape[1]
    group_size = lax.axis_size("fsdp")
    replicas = lax.axis_size("replica")
    count = group_size * replicas
    cosine, sine = tables(length)
    floats = tokens.astype(jnp.float32)
    inv_scale = lax.rsqrt(jnp.mean(floats * floats, axis=1, keepdims=True) + 1e-05)
    normed = (floats * inv_scale * norm_gain[None, :]).astype(jnp.bfloat16)
    full_key, full_value = (
        lax.all_gather(key_weight, "fsdp", axis=0, tiled=True),
        lax.all_gather(value_weight, "fsdp", axis=0, tiled=True),
    )
    key_pre = jnp.dot(normed, full_key, preferred_element_type=jnp.float32)
    value_pre = jnp.dot(normed, full_value, preferred_element_type=jnp.float32)
    rotated_keys = rotate(key_pre, cosine, sine, 1.0).astype(jnp.bfloat16)
    value_rows = value_pre.astype(jnp.bfloat16)
    key_back = rotate(key_cotangent.astype(jnp.float32), cosine, sine, -1.0).astype(jnp.bfloat16)
    contract = (((1,), (1,)), ((), ()))
    normed_grad = lax.dot_general(key_back, full_key, contract, preferred_element_type=jnp.float32)
    normed_grad = normed_grad + lax.dot_general(
        value_cotangent, full_value, contract, preferred_element_type=jnp.float32
    )
    both = jnp.concatenate([key_back, value_cotangent], axis=1)
    shard = lax.psum_scatter(
        lax.dot_general(normed, both, (((0,), (0,)), ((), ())), preferred_element_type=jnp.float32),
        "fsdp",
        scatter_dimension=0,
        tiled=True,
    )
    summed = lax.psum(shard, "replica")
    summed = summed / count
    gain_local = jnp.sum(normed_grad * floats * inv_scale, axis=0)
    gain_grad = lax.psum(gain_local, ("fsdp", "replica")) / count
    upstream = normed_grad * norm_gain[None, :]
    inner = jnp.mean(upstream * floats, axis=1, keepdims=True)
    input_grad = (inv_scale * upstream - floats * inv_scale**3 * inner).astype(jnp.bfloat16)
    return (rotated_keys, value_rows, input_grad, summed[:, :feats], summed[:, feats:], gain_grad)


def solution(mesh):
    in_specs = (
        P(("fsdp", "replica"), None),
        P(),
        P("fsdp", None),
        P("fsdp", None),
        P(("fsdp", "replica"), None),
        P(("fsdp", "replica"), None),
    )
    out_specs = (
        P(("fsdp", "replica"), None),
        P(("fsdp", "replica"), None),
        P(("fsdp", "replica"), None),
        P("fsdp", None),
        P("fsdp", None),
        P(),
    )
    return jax.shard_map(shards, mesh=mesh, in_specs=in_specs, out_specs=out_specs, check_vma=False)
```

profile of v0, /device:TPU:2, one launch (start us, length us, event | category | flops | bytes accessed | tf_op | source)
XLA Modules:
  0.0 363.3 jit_solution(2239359508696161492)
XLA Ops:
  7.2 0.0 copy-start.3
  7.2 0.0 all-gather.3.cloned.1.call-start
  7.2 0.7 all-gather.3.cloned.1.call-update
  7.9 0.0 all-gather.5.cloned.1.call-start
  8.0 0.7 all-gather.5.cloned.1.call-update
  8.7 0.0 reduce-scatter.2.cloned.1.call-start
  8.7 1.5 copy.18
  10.2 5.1 %fusion = f32[1024]{0:T(1024)S(1)} fusion(bf16[1024,4096]{1,0:T(8,128)(2,1)} %param.6), kind=kLoop, calls=%fused_computation.5 | loop fusion | flops 12581888 | bytes 8392704 | tf_op jit(solution)/shard_map/reduce_sum | solution.py:38
  15.3 1.8 broadcast_multiply_fusion.1
  17.1 51.5 %all-gather.3.cloned.1.call-done = bf16[4096,512]{1,0:T(8,128)(2,1)} async-done(((bf16[256,512]{1,0:T(8,128)(2,1)}), bf16[4096,512]{1,0:T(8,128)(2,1)}) %all-gather.3.cloned.1.call-update) | async-done | bytes 4194320 | tf_op jit(solution)/shard_map/all_gather | solution.py:41
  68.6 0.0 copy-done.3
  68.6 8.7 %fusion.18 = f32[1024,512]{0,1:T(8,128)S(1)} fusion(bf16[4096,512]{1,0:T(8,128)(2,1)} %all-gather.3.cloned.1.call-done, bf16[1024,4096]{1,0:T(8,128)(2,1)} %param.6, f32[4096]{0:T(1024)S(1)} %copy-done.3, f32[1024]{0:T(1024)S(1)} %get-tuple-element.17), kind=kOutput, calls=%fused_computation.37 | convolution fusion | flops 4311744512 | bytes 14700544 | tf_op jit(solution)/shard_map/dot_general | solution.py:44
  77.3 0.0 copy-start
  77.3 0.7 subtract_convert_fusion
  78.1 0.2 pad_maximum_fusion
  78.3 1.3 copy.17
  79.6 15.4 %fusion.9 = f32[4096,1024]{1,0:T(8,128)} fusion(bf16[1024,512]{1,0:T(8,128)(2,1)S(1)} %copy-done, bf16[1024,512]{1,0:T(8,128)(2,1)} %copy.17, bf16[1024,4096]{1,0:T(8,128)(2,1)} %param.6, f32[4096]{0:T(1024)S(1)} %copy-done.3, f32[1024]{0:T(1024)S(1)} %get-tuple-element.17), kind=kOutput, calls=%fused_computation.15 | convolution fusion | flops 8610906112 | bytes 27283456 | tf_op jit(solution)/shard_map/dot_general | solution.py:56
  95.0 0.0 reduce-scatter.2.cloned.1.call-update
  95.0 0.2 all-reduce.2.cloned.1.call-start
  95.3 1.3 copy.16
  96.6 10.3 %fusion.21 = f32[1024,4096]{1,0:T(8,128)} fusion(bf16[1024,512]{0,1:T(8,128)(2,1)S(1)} %bitcast.12, bf16[4096,512]{1,0:T(8,128)(2,1)} %all-gather.3.cloned.1.call-done), kind=kOutput, calls=%fused_computation.39 | convolution fusion | flops 4294967296 | bytes 22020096 | tf_op jit(solution)/shard_map/dot_general | solution.py:50
  106.9 18.8 %all-gather.5.cloned.1.call-done = bf16[4096,512]{1,0:T(8,128)(2,1)} async-done(((bf16[256,512]{1,0:T(8,128)(2,1)}), bf16[4096,512]{1,0:T(8,128)(2,1)}) %all-gather.5.cloned.1.call-update) | async-done | bytes 4194320 | tf_op jit(solution)/shard_map/all_gather | solution.py:42
  125.7 17.3 %fusion.8 = (f32[4096]{0:T(1024)S(1)}, f32[1024]{0:T(1024)S(1)}, f32[1024,4096]{1,0:T(8,128)}) fusion(bf16[1024,4096]{1,0:T(8,128)(2,1)} %param.6, f32[1024]{0:T(1024)S(1)} %get-tuple-element.17, f32[4096]{0:T(1024)S(1)} %copy-done.3, f32[1024,4096]{1,0:T(8,128)} %fusion.21, bf16[1024,512]{1,0:T(8,128)(2,1)S(1)} %copy-done, ...), kind=kOutput, calls=%fused_computation.13 | convolution fusion | flops 4328516608 | bytes 47226880 | tf_op jit(solution)/shard_map/dot_general | solution.py:51
  143.0 70.2 %psum.15 = f32[4096]{0:T(1024)S(1)} all-reduce(f32[4096]{0:T(1024)S(1)} %get-tuple-element.6), channel_id=1, replica_groups=mesh['fsdp'=16,'replica'=8] {'fsdp','replica'}, use_global_device_ids=true, to_apply=%region_5.0 | all-reduce | flops 4096 | bytes 32768 | tf_op jit(solution)/shard_map/psum | solution.py:64
  213.3 0.6 broadcast_multiply_fusion.2
  213.9 10.3 %convolution_convert_fusion = bf16[1024,512]{1,0:T(8,128)(2,1)} fusion(bf16[4096,512]{1,0:T(8,128)(2,1)} %all-gather.5.cloned.1.call-done, bf16[1024,4096]{1,0:T(8,128)(2,1)} %param.6, f32[4096]{0:T(1024)S(1)} %copy-done.3, f32[1024]{0:T(1024)S(1)} %get-tuple-element.17), kind=kOutput, calls=%fused_computation.19 | convolution fusion | flops 4312268800 | bytes 13651968 | tf_op jit(solution)/shard_map/dot_general | solution.py:45
  224.2 50.8 %reduce-scatter.2.cloned.1.call-done = f32[256,1024]{1,0:T(8,128)} async-done(((f32[4096,1024]{1,0:T(8,128)}), f32[256,1024]{1,0:T(8,128)}) %reduce-scatter.2.cloned.1.call-update) | async-done | bytes 1048592 | tf_op jit(solution)/shard_map/reduce_scatter | solution.py:55
  275.0 0.0 all-reduce.2.cloned.1.call-update
  275.0 13.2 %fusion.5 = bf16[1024,4096]{1,0:T(8,128)(2,1)} fusion(bf16[1024,4096]{1,0:T(8,128)(2,1)} %param.6, f32[1024,4096]{1,0:T(8,128)} %get-tuple-element.21, f32[1024]{0:T(1024)S(1)} %broadcast_multiply_fusion.3, f32[1024]{0:T(1024)S(1)} %get-tuple-element.16, f32[4096]{0:T(1024)S(1)} %copy-done.3, f32[1024]{0:T(1024)S(1)} %get-tuple-element.17), kind=kLoop, calls=%fused_computation.10 | loop fusion | flops 29360128 | bytes 33583104 | tf_op jit(solution)/shard_map/convert_element_type | solution.py:67
  288.2 66.1 %all-reduce.2.cloned.1.call-done = f32[256,1024]{1,0:T(8,128)} async-done(((f32[256,1024]{1,0:T(8,128)}), f32[256,1024]{1,0:T(8,128)}) %all-reduce.2.cloned.1.call-update) | async-done | bytes 1048592 | tf_op jit(solution)/shard_map/psum | solution.py:61
  354.4 1.3 broadcast_multiply_fusion
  355.7 1.0 fusion.20
  (8 shorter events, 0.0 us)
Async XLA Ops:
  7.2 61.4 %copy-start.3 = (f32[4096]{0:T(1024)S(1)}, f32[4096]{0:T(1024)}, u32[]{:S(2)}) copy-start(f32[4096]{0:T(1024)} %param.7) | copy-start | bytes 49156
  7.2 61.4 %all-gather.3.cloned.1.call-start = ((), (), s32[]{:S(2)}) async-start(), calls=%async_computation.1 | async-start | bytes 4456448 | tf_op jit(solution)/shard_map/all_gather | solution.py:41
  7.9 117.8 %all-gather.5.cloned.1.call-start = ((), (), s32[]{:S(2)}) async-start(), calls=%async_computation.2 | async-start | bytes 4456448 | tf_op jit(solution)/shard_map/all_gather | solution.py:42
  8.7 266.3 %reduce-scatter.2.cloned.1.call-start = ((), (), s32[]{:S(2)}) async-start(), calls=%async_computation.3 | async-start | bytes 17825792 | tf_op jit(solution)/shard_map/reduce_scatter | solution.py:55
  68.6 8.7 %copy-start.1 = (f32[1024,64]{0,1:T(8,128)S(1)}, f32[1024,64]{0,1:T(8,128)}, u32[]{:S(2)}) copy-start(f32[1024,64]{0,1:T(8,128)} %get-tuple-element.19) | copy-start | bytes 786436
  68.6 8.7 %copy-start.2 = (f32[1024,64]{0,1:T(8,128)S(1)}, f32[1024,64]{0,1:T(8,128)}, u32[]{:S(2)}) copy-start(f32[1024,64]{0,1:T(8,128)} %get-tuple-element.20) | copy-start | bytes 786436
  77.3 2.3 copy-start
  95.0 259.3 %all-reduce.2.cloned.1.call-start = ((), (), s32[]{:S(2)}) async-start(), calls=%async_computation.4 | async-start | bytes 2097152 | tf_op jit(solution)/shard_map/psum | solution.py:61
Sparse Core Ops, SparseCore 0:
  10.4 58.1 all-gather.2
  71.0 54.6 all-gather.4
  130.1 144.8 reduce-scatter.1
  277.5 76.8 all-reduce.1
where the time goes:
time: 364 us; the launch traced here: 363 us
  waiting for transfers between devices  189 us (52%)
  blocking collectives  70.2 us (19%)
  matrix products  62 us (17%)
  other arithmetic  23.1 us (6%)
  between operations  13.8 us (4%)
  local copies, waits for them, and re-layouts  5.2 us (1%)
    psum x1, blocking collectives, shards(): gain_grad = lax.psum(gain_local, ('fsdp', 'replica')) / count  70.2 us
    psum x1, waiting for transfers between devices, shards(): summed = lax.psum(shard, 'replica')  66.1 us
    all_gather x1, waiting for transfers between devices, shards(): lax.all_gather(key_weight, 'fsdp', axis=0, tiled=True)  51.5 us
    reduce_scatter x1, waiting for transfers between devices, shards(): lax.psum_scatter(lax.dot_general(normed, both, (((0,), (0,)), ((), ())),...  50.8 us
    all_gather x1, waiting for transfers between devices, shards(): lax.all_gather(value_weight, 'fsdp', axis=0, tiled=True)  18.8 us
    dot_general x1, matrix products, shards(): lax.dot_general(value_cotangent, full_value, contract, preferred_element_...  17.3 us
    dot_general x1, matrix products, shards(): lax.dot_general(normed, both, (((0,), (0,)), ((), ())), preferred_element...  15.4 us
    convert_element_type x1, other arithmetic, shards(): (inv_scale * upstream - floats * inv_scale ** 3 * inner).astype(jnp.bfloa...  13.2 us
  transfers between devices with their start and end apart: 4, of which 4 were waited for; matrix products, arithmetic and copies ran while one was open for 24% of the time, Pallas kernels for 0%

commit v1 on v0

v1 whole, which is shorter than its diff:
```python
import math

import jax
import jax.numpy as jnp
import numpy as np
from jax import lax
from jax.experimental import pallas as pl
from jax.experimental.pallas import tpu as pltpu
from jax.sharding import Mesh, PartitionSpec as P

HEAD = 128
AXES = ("x", "zh", "c", "y", "zl")
SIZES = (4, 2, 2, 4, 2)
F32 = jnp.float32
BF16 = jnp.bfloat16
MIB = 1 << 20


def send(value, move):
    pairs = []
    for i in range(math.prod(SIZES)):
        x, zh, c, y, zl = (int(v) for v in np.unravel_index(i, SIZES))
        x, y, z, c = move(x, y, zh * 2 + zl, c)
        x, y, z, c = x % 4, y % 4, z % 4, c % 2
        pairs.append((i, int(np.ravel_multi_index((x, z // 2, c, y, z % 2), SIZES))))
    return lax.ppermute(value, AXES, pairs)


def to_core(value):
    return send(value, lambda x, y, z, c: (x, y, z, c + 1))


def to_x(value, d):
    return send(value, lambda x, y, z, c: (x + d, y, z, c))


def to_y(value, d):
    return send(value, lambda x, y, z, c: (x, y + d, z, c))


def to_z(value, d):
    return send(value, lambda x, y, z, c: (x, y, z + d, c))


def to_zl(value):
    return send(value, lambda x, y, z, c: (x, y, z ^ 1, c))


def params(mib, **more):
    return pltpu.CompilerParams(vmem_limit_bytes=mib * MIB, **more)


def turn(values, cosine, sine, direction):
    parts = []
    for h in range(values.shape[1] // HEAD):
        v = values[:, h * HEAD : (h + 1) * HEAD]
        parts.append(v * cosine + direction * (pltpu.roll(v, HEAD // 2, 1) * sine))
    return jnp.concatenate(parts, axis=1)


def norm_kernel(tok_ref, gain_ref, kc_ref, cos_ref, sin_ref, normed_ref, back_ref, inv_ref):
    v = tok_ref[...].astype(F32)
    inv = lax.rsqrt(jnp.mean(v * v, axis=1, keepdims=True) + 1e-05)
    normed_ref[...] = (v * inv * gain_ref[...]).astype(BF16)
    inv_ref[...] = jnp.broadcast_to(inv, inv_ref.shape)
    back_ref[...] = turn(kc_ref[...].astype(F32), cos_ref[...], sin_ref[...], -1.0).astype(BF16)


def norm(tokens, gain, key_cot, cosine, sine):
    rows, width = tokens.shape
    feats = key_cot.shape[1]
    tb = 128
    return pl.pallas_call(
        norm_kernel,
        grid=(rows // tb,),
        in_specs=[
            pl.BlockSpec((tb, width), lambda i: (i, 0)),
            pl.BlockSpec((1, width), lambda i: (0, 0)),
            pl.BlockSpec((tb, feats), lambda i: (i, 0)),
            pl.BlockSpec((tb, HEAD), lambda i: (i, 0)),
            pl.BlockSpec((tb, HEAD), lambda i: (i, 0)),
        ],
        out_specs=[
            pl.BlockSpec((tb, width), lambda i: (i, 0)),
            pl.BlockSpec((tb, feats), lambda i: (i, 0)),
            pl.BlockSpec((tb, HEAD), lambda i: (i, 0)),
        ],
        out_shape=[
            jax.ShapeDtypeStruct((rows, width), BF16),
            jax.ShapeDtypeStruct((rows, feats), BF16),
            jax.ShapeDtypeStruct((rows, HEAD), F32),
        ],
        compiler_params=params(24),
        cost_estimate=pl.CostEstimate(flops=8 * rows * width, bytes_accessed=4 * rows * width, transcendentals=0),
        name="norm",
    )(tokens, gain, key_cot, cosine, sine)


def terms(normed_ref, cot_ref):
    return lax.dot_general(normed_ref[...], cot_ref[...], (((0,), (0,)), ((), ())), preferred_element_type=F32)


def term_cost(rows, feats):
    return pl.CostEstimate(flops=2 * rows * 2048 * feats, bytes_accessed=6 * MIB, transcendentals=0)


def sibling_kernel(order_ref, normed_ref, cot_ref, out_ref):
    out_ref[0] = terms(normed_ref, cot_ref).astype(BF16)


def sibling_terms(order, normed, cot):
    rows, feats = cot.shape
    return pl.pallas_call(
        sibling_kernel,
        grid_spec=pltpu.PrefetchScalarGridSpec(
            num_scalar_prefetch=1,
            grid=(8,),
            in_specs=[
                pl.BlockSpec((rows, 256), lambda g, order: (0, order[g])),
                pl.BlockSpec((rows, feats), lambda g, order: (0, 0)),
            ],
            out_specs=pl.BlockSpec((1, 256, feats), lambda g, order: (g, 0, 0)),
        ),
        out_shape=jax.ShapeDtypeStruct((8, 256, feats), BF16),
        compiler_params=params(16),
        cost_estimate=term_cost(rows, feats),
        name="sibling_terms",
    )(order, normed, cot)


def own_kernel(parts, order_ref, normed_ref, cot_ref, got_ref, *out_refs):
    g = pl.program_id(0)
    each = 8 // parts
    total = (terms(normed_ref, cot_ref) + got_ref[0].astype(F32)).astype(BF16)
    for p in range(parts):

        @pl.when(g // each == p)
        def _():
            out_refs[p][0] = total


def own_terms(order, normed, cot, got, parts):
    rows, feats = cot.shape
    each = 8 // parts
    return pl.pallas_call(
        lambda *refs: own_kernel(parts, *refs),
        grid_spec=pltpu.PrefetchScalarGridSpec(
            num_scalar_prefetch=1,
            grid=(8,),
            in_specs=[
                pl.BlockSpec((rows, 256), lambda g, order: (0, order[g])),
                pl.BlockSpec((rows, feats), lambda g, order: (0, 0)),
                pl.BlockSpec((1, 256, feats), lambda g, order: (g, 0, 0)),
            ],
            out_specs=[
                pl.BlockSpec((1, 256, feats), lambda g, order, p=p: (jnp.clip(g - p * each, 0, each - 1), 0, 0))
                for p in range(parts)
            ],
        ),
        out_shape=[jax.ShapeDtypeStruct((each, 256, feats), BF16) for _ in range(parts)],
        compiler_params=params(24),
        cost_estimate=term_cost(rows, feats),
        name="own_terms",
    )(order, normed, cot, got)


def forward_kernel(normed_ref, w_ref, back_ref, vc_ref, inv_ref, cos_ref, sin_ref, key_ref, value_ref, coef_ref):
    feats = back_ref.shape[1]
    pre = jnp.dot(normed_ref[...], w_ref[...], preferred_element_type=F32)
    key_pre, value_pre = pre[:, :feats], pre[:, feats:]
    key_ref[...] = turn(key_pre, cos_ref[...], sin_ref[...], 1.0).astype(BF16)
    value_ref[...] = value_pre.astype(BF16)
    inner = jnp.sum(
        key_pre * back_ref[...].astype(F32) + value_pre * vc_ref[...].astype(F32), axis=1, keepdims=True
    )
    inv = inv_ref[...]
    coef_ref[...] = inv * inv * (inner * (1.0 / normed_ref.shape[1]))


def forward(normed, weights, key_back, value_cot, inv, cosine, sine):
    rows, width = normed.shape
    feats = key_back.shape[1]
    tb = 256
    by_rows = lambda n: pl.BlockSpec((tb, n), lambda i: (i, 0))
    return pl.pallas_call(
        forward_kernel,
        grid=(rows // tb,),
        in_specs=[
            by_rows(width),
            pl.BlockSpec((width, 2 * feats), lambda i: (0, 0)),
            by_rows(feats),
            by_rows(feats),
            by_rows(HEAD),
            by_rows(HEAD),
            by_rows(HEAD),
        ],
        out_specs=[by_rows(feats), by_rows(feats), by_rows(HEAD)],
        out_shape=[
            jax.ShapeDtypeStruct((rows, feats), BF16),
            jax.ShapeDtypeStruct((rows, feats), BF16),
            jax.ShapeDtypeStruct((rows, HEAD), F32),
        ],
        compiler_params=params(36),
        cost_estimate=pl.CostEstimate(flops=4 * rows * width * feats, bytes_accessed=20 * MIB, transcendentals=0),
        name="forward",
    )(normed, weights, key_back, value_cot, inv, cosine, sine)


def backward_kernel(tok_ref, w_ref, back_ref, vc_ref, inv_ref, coef_ref, gain_ref, into_ref, out_ref):
    both = jnp.concatenate([back_ref[...], vc_ref[...]], axis=1)
    grad = lax.dot_general(both, w_ref[...], (((1,), (1,)), ((), ())), preferred_element_type=F32)
    upstream = grad * gain_ref[...]
    out_ref[...] = (inv_ref[:, :1] * upstream - tok_ref[...].astype(F32) * coef_ref[:, :1]).astype(BF16)


def backward(first, blocks, tokens, weights, key_back, value_cot, inv, coef, gain, into):
    rows, width = tokens.shape
    feats = key_back.shape[1]
    cb = 512
    whole = lambda n: pl.BlockSpec((rows, n), lambda i: (0, 0))
    columns = pl.BlockSpec((rows, cb), lambda i: (0, i + first))
    operands = [tokens, weights, key_back, value_cot, inv, coef, gain]
    specs = [
        columns,
        pl.BlockSpec((cb, 2 * feats), lambda i: (i + first, 0)),
        whole(feats),
        whole(feats),
        whole(HEAD),
        whole(HEAD),
        pl.BlockSpec((1, cb), lambda i: (0, i + first)),
    ]
    body, aliases = backward_kernel, {}
    if into is None:
        body = lambda *refs: backward_kernel(*refs[:7], None, refs[7])
    else:
        operands.append(into)
        specs.append(pl.BlockSpec(memory_space=pl.ANY))
        aliases = {7: 0}
    return pl.pallas_call(
        body,
        grid=(blocks,),
        in_specs=specs,
        out_specs=columns,
        out_shape=jax.ShapeDtypeStruct((rows, width), BF16),
        input_output_aliases=aliases,
        compiler_params=params(36),
        cost_estimate=pl.CostEstimate(
            flops=4 * rows * blocks * cb * feats, bytes_accessed=6 * rows * blocks * cb, transcendentals=0
        ),
        name="backward",
    )(*operands)


def paired(own, got):
    return (own + got[1]) + (got[0] + got[2])


def shards(tokens, norm_gain, key_weight, value_weight, key_cotangent, value_cotangent):
    length, width = tokens.shape
    feats = key_weight.shape[1]
    count = math.prod(SIZES)
    x, zh, core, y = (lax.axis_index(a) for a in ("x", "zh", "c", "y"))
    half = HEAD // 2
    angles = np.arange(length)[:, None] * np.exp(-(2.0 * np.arange(half) / HEAD) * math.log(500000.0))[None, :]
    cosine = jnp.asarray(np.concatenate([np.cos(angles), np.cos(angles)], 1).astype(np.float32))
    sine = jnp.asarray(np.concatenate([-np.sin(angles), np.sin(angles)], 1).astype(np.float32))
    gain = norm_gain.reshape(1, width)

    shard = jnp.concatenate([key_weight, value_weight], axis=1)
    weights = lax.all_gather(shard, ("x", "zh", "c"), axis=0, tiled=True)

    normed, key_back, inv = norm(tokens, gain, key_cotangent, cosine, sine)

    i4, j2 = jnp.arange(4, dtype=jnp.int32), jnp.arange(2, dtype=jnp.int32)
    base = ((x + i4) % 4)[:, None] * 4 + ((zh + j2) % 2)[None, :] * 2
    x_major, z_major = base.reshape(8), base.T.reshape(8)
    sib_value = to_core(sibling_terms(x_major + 1 - core, normed, value_cotangent))
    sib_key = to_core(sibling_terms(z_major + 1 - core, normed, key_back))
    value_terms = own_terms(x_major + core, normed, value_cotangent, sib_value, 4)
    key_terms = own_terms(z_major + core, normed, key_back, sib_key, 2)

    got_x = [to_x(value_terms[d], d) for d in (1, 2, 3)]
    got_z = to_z(key_terms[1], 2)
    value_sum = value_terms[0].astype(F32) + sum(g.astype(F32) for g in got_x)
    key_sum = key_terms[0].astype(F32) + got_z.astype(F32)
    got_z = to_z(value_sum[1].astype(BF16), 2)
    got_x = [to_x(key_sum[d].astype(BF16), d) for d in (1, 2, 3)]
    value_part = value_sum[0] + got_z.astype(F32)
    key_part = key_sum[0] + sum(g.astype(F32) for g in got_x)

    parts = jnp.stack([key_part, value_part]).reshape(2, 4, 64, feats)
    piece = lambda d: lax.dynamic_index_in_dim(parts, (y + d) % 4, 1, keepdims=False)
    got_y = [to_y(piece(d).astype(BF16), d) for d in (1, 2, 3)]
    mine = (piece(0) + sum(g.astype(F32) for g in got_y)).astype(BF16)
    mine = ((mine.astype(F32) + to_zl(mine).astype(F32)) / count).astype(BF16)
    pieces = [mine] + [to_y(mine, d) for d in (1, 2, 3)]
    grads = jnp.zeros((2, 4, 64, feats), F32)
    for d, piece_d in enumerate(pieces):
        grads = lax.dynamic_update_slice(grads, piece_d.astype(F32)[:, None], (0, (y - d) % 4, 0, 0))
    key_grad, value_grad = grads[0].reshape(256, feats), grads[1].reshape(256, feats)

    first_row = (x * 4 + zh * 2 + core) * 256
    own_gain = lax.dynamic_slice(norm_gain, (first_row,), (256,))
    local = jnp.sum(key_part * key_weight.astype(F32) + value_part * value_weight.astype(F32), axis=1)
    total = lax.dynamic_update_slice(jnp.zeros((width,), F32), local / own_gain / count, (first_row,)).reshape(32, 128)
    total = total + to_core(total)
    total = paired(total, [to_x(total, d) for d in (1, 2, 3)])
    total = paired(total, [to_y(total, d) for d in (1, 2, 3)])
    total = paired(total, [to_z(total, d) for d in (1, 2, 3)])
    gain_grad = total.reshape(width)

    rotated_keys, value_rows, coef = forward(normed, weights, key_back, value_cotangent, inv, cosine, sine)
    input_grad = None
    for q in range(4):
        input_grad = backward(
            2 * q, 2, tokens, weights, key_back, value_cotangent, inv, coef, gain, input_grad
        )
    return rotated_keys, value_rows, input_grad, key_grad, value_grad, gain_grad


def solution(mesh):
    fine = Mesh(mesh.devices.reshape(SIZES), AXES)
    fsdp, replica = ("x", "zh", "c"), ("y", "zl")
    in_specs = (P(fsdp + replica, None), P(), P(fsdp, None), P(fsdp, None), P(fsdp + replica, None), P(fsdp + replica, None))
    out_specs = (P(fsdp + replica, None), P(fsdp + replica, None), P(fsdp + replica, None), P(fsdp, None), P(fsdp, None), P())
    return jax.shard_map(shards, mesh=fine, in_specs=in_specs, out_specs=out_specs, check_vma=False)
```

time: 364 us -> 202 us (0.55)
  waiting for transfers between devices: 189 us -> 48 us
  blocking collectives: 70.2 us -> 0 us
  Pallas kernels: 0 us -> 64.7 us
  matrix products: 62 us -> 0 us
  starting transfers between devices: 0.34 us -> 38.6 us
  local copies, waits for them, and re-layouts: 5.2 us -> 24.4 us
  other arithmetic: 23.1 us -> 9.63 us
    all_gather x2 -> x1, waiting for transfers between devices: 70.3 us -> 0.01 us  [shards(): weights = lax.all_gather(shard, ('x', 'zh', 'c'), axis=0, tiled=True)]
    psum x1 -> x0, blocking collectives: 70.2 us -> none  [shards(): gain_grad = lax.psum(gain_local, ('fsdp', 'replica')) / count]
    psum x1 -> x0, waiting for transfers between devices: 66.1 us -> none  [shards(): summed = lax.psum(shard, 'replica')]
    pallas_call x0 -> x10, Pallas kernels: none -> 64.7 us  [the longest x4 19.5 us: backward(): pl.pallas_call(body, grid=(blocks,), in_specs=specs, out_specs=columns, o...]
    dot_general x5 -> x0, matrix products: 62 us -> none  [the longest x1 17.3 us: shards(): lax.dot_general(value_cotangent, full_value, contract, preferred_element_...]
    reduce_scatter x1 -> x0, waiting for transfers between devices: 50.8 us -> none  [shards(): lax.psum_scatter(lax.dot_general(normed, both, (((0,), (0,)), ((), ())),...]
    ppermute x0 -> x27, waiting for transfers between devices: none -> 47.9 us  [send(): return lax.ppermute(value, AXES, pairs)]
    ppermute x0 -> x27, starting transfers between devices: none -> 38.6 us  [send(): return lax.ppermute(value, AXES, pairs)]
  transfers between devices with their start and end apart: 4 -> 28, of which waited for: 4 -> 16; matrix products, arithmetic and copies ran while one was open for 24% -> 5% of each run, Pallas kernels for 0% -> 16%
where the time goes in v1:
time: 202 us; the launch traced here: 200 us
  Pallas kernels  64.7 us (32%)
  waiting for transfers between devices  48 us (24%)
  starting transfers between devices  38.6 us (19%)
  local copies, waits for them, and re-layouts  24.4 us (12%)
  between operations  14.3 us (7%)
  other arithmetic  9.63 us (5%)
    ppermute x27, waiting for transfers between devices, send(): return lax.ppermute(value, AXES, pairs)  47.9 us
    ppermute x27, starting transfers between devices, send(): return lax.ppermute(value, AXES, pairs)  38.6 us
    unnamed x32, local copies, waits for them, and re-layouts  22 us
    pallas_call x4, Pallas kernels, backward(): pl.pallas_call(body, grid=(blocks,), in_specs=specs, out_specs=columns, o...  19.5 us
    pallas_call x2, Pallas kernels, own_terms(): pl.pallas_call(lambda *refs: own_kernel(parts, *refs), grid_spec=pltpu.Pr...  14.7 us
    pallas_call x1, Pallas kernels, forward(): pl.pallas_call(forward_kernel, grid=(rows // tb,), in_specs=[by_rows(widt...  13.7 us
    pallas_call x2, Pallas kernels, sibling_terms(): pl.pallas_call(sibling_kernel, grid_spec=pltpu.PrefetchScalarGridSpec(num...  12.9 us
  transfers between devices with their start and end apart: 28, of which 16 were waited for; matrix products, arithmetic and copies ran while one was open for 5% of the time, Pallas kernels for 16%

profile of v1, /device:TPU:2, one launch (start us, length us, event | category | flops | bytes accessed | tf_op | source)
XLA Modules:
  0.0 199.7 jit_solution(5429443448597246499)
XLA Ops:
  7.2 1.9 pad_maximum_fusion
  9.3 3.4 %copy-done = bf16[1024,4096]{1,0:T(8,128)(2,1)S(1)} copy-done((bf16[1024,4096]{1,0:T(8,128)(2,1)S(1)}, bf16[1024,4096]{1,0:T(8,128)(2,1)}, u32[]{:S(2)}) %copy-start) | copy-done | bytes 8388632
  16.7 3.9 %norm.1 = (bf16[1024,4096]{1,0:T(8,128)(2,1)S(1)}, bf16[1024,512]{1,0:T(8,128)(2,1)S(1)}, f32[1024,128]{1,0:T(8,128)S(1)}) custom-call(bf16[1024,4096]{1,0:T(8,128)(2,1)S(1)} %copy-done, f32[1,4096]{1,0:T(1,128)S(1)} %bitcast.77, bf16[1024,512]{1,0:T(8,128)(2,1)S(1)} %copy-done.7, f32[1024,128]{1,0:T(8,128)S(1)} %copy-done.10, f32[1024,128]{1,0:T(8,128)S(1)} %copy-done.8), custom_call_target="tpu_custom_call" | custom-call | flops 33554432 | bytes 16777216 | tf_op jit(solution)/shard_map/norm/pallas_call | solution.py:73
  20.6 6.8 %sibling_terms.3 = bf16[8,256,512]{2,1,0:T(8,128)(2,1)} custom-call(s32[8]{0:T(128)S(1)} %sub.24.order_ref, bf16[1024,4096]{1,0:T(8,128)(2,1)S(1)} %get-tuple-element.18.normed_ref.refs_1_, bf16[1024,512]{1,0:T(8,128)(2,1)S(1)} %copy-done.6), custom_call_target="tpu_custom_call" | custom-call | flops 2147483648 | bytes 6291456 | tf_op jit(solution)/shard_map/sibling_terms/pallas_call | solution.py:113
  27.6 3.4 %copy-done.3 = bf16[1024,4096]{1,0:T(8,128)(2,1)S(1)} copy-done((bf16[1024,4096]{1,0:T(8,128)(2,1)S(1)}, bf16[1024,4096]{1,0:T(8,128)(2,1)}, u32[]{:S(2)}) %copy-start.3) | copy-done | bytes 8388632
  30.9 6.1 %sibling_terms.2 = bf16[8,256,512]{2,1,0:T(8,128)(2,1)} custom-call(s32[8]{0:T(128)S(1)} %sub.22.order_ref, bf16[1024,4096]{1,0:T(8,128)(2,1)S(1)} %copy-done.3, bf16[1024,512]{1,0:T(8,128)(2,1)S(1)} %get-tuple-element.19.back_ref.refs_2_.cot_ref), custom_call_target="tpu_custom_call" | custom-call | flops 2147483648 | bytes 6291456 | tf_op jit(solution)/shard_map/sibling_terms/pallas_call | solution.py:113
  37.8 3.4 %copy-done.4 = bf16[1024,4096]{1,0:T(8,128)(2,1)S(1)} copy-done((bf16[1024,4096]{1,0:T(8,128)(2,1)S(1)}, bf16[1024,4096]{1,0:T(8,128)(2,1)}, u32[]{:S(2)}) %copy-start.4) | copy-done | bytes 8388632
  41.2 7.4 %own_terms.3 = (bf16[2,256,512]{2,1,0:T(8,128)(2,1)S(1)}, bf16[2,256,512]{2,1,0:T(8,128)(2,1)S(1)}, bf16[2,256,512]{2,1,0:T(8,128)(2,1)S(1)}, bf16[2,256,512]{2,1,0:T(8,128)(2,1)S(1)}) custom-call(s32[8]{0:T(128)S(1)} %add.247.refs_0_, bf16[1024,4096]{1,0:T(8,128)(2,1)S(1)} %copy-done.4, bf16[1024,512]{1,0:T(8,128)(2,1)S(1)} %copy-done.6, ...), custom_call_target="tpu_custom_call" | custom-call | flops 2147483648 | bytes 6291456 | tf_op jit(solution)/shard_map/own_terms/pallas_call | solution.py:145
  51.2 2.2 %collective-permute-start.8 = (bf16[2,256,512]{2,1,0:T(8,128)(2,1)S(1)}, bf16[2,256,512]{2,1,0:T(8,128)(2,1)S(1)}, u32[]{:S(2)}, u32[]{:S(2)}) collective-permute-start(bf16[2,256,512]{2,1,0:T(8,128)(2,1)S(1)} %get-tuple-element.29), channel_id=1, source_target_pairs={{0,96},{1,97},{2,98},{3,99},{4,100},{5,101},{6,102},{7,103},{8,104... | collective-permute-start | bytes 1572872 | tf_op jit(solution)/shard_map/ppermute | solution.py:26
  53.4 7.3 %own_terms.2 = (bf16[4,256,512]{2,1,0:T(8,128)(2,1)S(1)}, bf16[4,256,512]{2,1,0:T(8,128)(2,1)S(1)}) custom-call(s32[8]{0:T(128)S(1)} %add.236.refs_0_, bf16[1024,4096]{1,0:T(8,128)(2,1)S(1)} %copy-done.4, bf16[1024,512]{1,0:T(8,128)(2,1)S(1)} %get-tuple-element.19.back_ref.refs_2_.cot_ref, bf16[8,256,512]{2,1,0:T(8,128)(2,1)} %collective-permute-done.refs_3_), custom_call_target="tpu_custom_call" | custom-call | flops 2147483648 | bytes 6291456 | tf_op jit(solution)/shard_map/own_terms/pallas_call | solution.py:145
  60.7 3.9 %collective-permute-start.1 = (bf16[4,256,512]{2,1,0:T(8,128)(2,1)S(1)}, bf16[4,256,512]{2,1,0:T(8,128)(2,1)S(1)}, u32[]{:S(2)}, u32[]{:S(2)}) collective-permute-start(bf16[4,256,512]{2,1,0:T(8,128)(2,1)S(1)} %get-tuple-element.25), channel_id=1, source_target_pairs={{0,16},{1,17},{2,18},{3,19},{4,20},{5,21},{6,22},{7,23},{8,24},{9,... | collective-permute-start | bytes 3145736 | tf_op jit(solution)/shard_map/ppermute | solution.py:26
  64.7 3.6 %collective-permute-done.6 = bf16[2,256,512]{2,1,0:T(8,128)(2,1)S(1)} collective-permute-done((bf16[2,256,512]{2,1,0:T(8,128)(2,1)S(1)}, bf16[2,256,512]{2,1,0:T(8,128)(2,1)S(1)}, u32[]{:S(2)}, u32[]{:S(2)}) %collective-permute-start.6) | collective-permute-done | bytes 524320 | tf_op jit(solution)/shard_map/ppermute | solution.py:26
  68.3 1.9 collective-permute-done.7
  70.2 11.6 %collective-permute-done.8 = bf16[2,256,512]{2,1,0:T(8,128)(2,1)S(1)} collective-permute-done((bf16[2,256,512]{2,1,0:T(8,128)(2,1)S(1)}, bf16[2,256,512]{2,1,0:T(8,128)(2,1)S(1)}, u32[]{:S(2)}, u32[]{:S(2)}) %collective-permute-start.8) | collective-permute-done | bytes 524320 | tf_op jit(solution)/shard_map/ppermute | solution.py:26
  82.1 4.8 %collective-permute-start.9 = (bf16[256,512]{1,0:T(8,128)(2,1)S(1)}, bf16[256,512]{1,0:T(8,128)(2,1)}, u32[]{:S(2)}, u32[]{:S(2)}) collective-permute-start(bf16[256,512]{1,0:T(8,128)(2,1)S(1)} %fusion.2), channel_id=1, source_target_pairs={{0,16},{1,17},{2,18},{3,19},{4,20},{5,21},{6,22},{7,23},{8,24},{9,... | collective-permute-start | bytes 786440 | tf_op jit(solution)/shard_map/ppermute | solution.py:26
  86.9 9.7 %collective-permute-done.1 = bf16[4,256,512]{2,1,0:T(8,128)(2,1)S(1)} collective-permute-done((bf16[4,256,512]{2,1,0:T(8,128)(2,1)S(1)}, bf16[4,256,512]{2,1,0:T(8,128)(2,1)S(1)}, u32[]{:S(2)}, u32[]{:S(2)}) %collective-permute-start.1) | collective-permute-done | bytes 1048608 | tf_op jit(solution)/shard_map/ppermute | solution.py:26
  101.2 2.0 collective-permute-start.3
  103.2 5.5 %collective-permute-done.2 = bf16[256,512]{1,0:T(8,128)(2,1)} collective-permute-done((bf16[256,512]{1,0:T(8,128)(2,1)}, bf16[256,512]{1,0:T(8,128)(2,1)}, u32[]{:S(2)}, u32[]{:S(2)}) %collective-permute-start.2) | collective-permute-done | bytes 262176 | tf_op jit(solution)/shard_map/ppermute | solution.py:26
  109.3 5.0 %collective-permute-done.3 = bf16[256,512]{1,0:T(8,128)(2,1)} collective-permute-done((bf16[256,512]{1,0:T(8,128)(2,1)S(1)}, bf16[256,512]{1,0:T(8,128)(2,1)}, u32[]{:S(2)}, u32[]{:S(2)}) %collective-permute-start.3) | collective-permute-done | bytes 262176 | tf_op jit(solution)/shard_map/ppermute | solution.py:26
  114.3 2.6 %add_reduce_fusion = (f32[256]{0:T(256)S(1)}, f32[256,512]{1,0:T(8,128)S(1)}, f32[256,512]{1,0:T(8,128)}) fusion(bf16[256,512]{1,0:T(8,128)(2,1)S(1)} %copy-done.15, bf16[256,512]{1,0:T(8,128)(2,1)} %param.10, bf16[256,512]{1,0:T(8,128)(2,1)} %collective-permute-done.9, f32[2,256,512]{2,1,0:T(8,128)} %copy-done.14, ...), kind=kLoop, calls=%fused_computation.16 | loop fusion | flops 1834752 | bytes 3671040 | tf_op jit(solution)/shard_map/reduce_sum | solution.py:304
  118.3 2.0 %collective-permute-start.20 = (f32[32,128]{1,0:T(8,128)S(1)}, f32[32,128]{1,0:T(8,128)S(1)}, u32[]{:S(2)}, u32[]{:S(2)}) collective-permute-start(f32[32,128]{1,0:T(8,128)S(1)} %bitcast_add_fusion), channel_id=1, source_target_pairs={{0,96},{1,97},{2,98},{3,99},{4,100},{5,101},{6,102},{7,103},{8,104... | collective-permute-start | bytes 49160 | tf_op jit(solution)/shard_map/ppermute | solution.py:26
  124.6 2.7 %collective-permute-start.11 = (bf16[2,64,512]{2,1,0:T(8,128)(2,1)S(1)}, bf16[2,64,512]{2,1,0:T(8,128)(2,1)S(1)}, u32[]{:S(2)}, u32[]{:S(2)}) collective-permute-start(bf16[2,64,512]{2,1,0:T(8,128)(2,1)S(1)} %get-tuple-element.40), channel_id=1, source_target_pairs={{0,4},{1,5},{2,6},{3,7},{4,0},{5,1},{6,2},{7,3},{8,12},{9,13},{10,... | collective-permute-start | bytes 393224 | tf_op jit(solution)/shard_map/ppermute | solution.py:26
  128.9 2.0 %collective-permute-start.22 = (f32[32,128]{1,0:T(8,128)S(1)}, f32[32,128]{1,0:T(8,128)S(1)}, u32[]{:S(2)}, u32[]{:S(2)}) collective-permute-start(f32[32,128]{1,0:T(8,128)S(1)} %add_add_fusion.2), channel_id=1, source_target_pairs={{0,2},{1,3},{2,4},{3,5},{4,6},{5,7},{6,0},{7,1},{8,10},{9,11},{10,... | collective-permute-start | bytes 49160 | tf_op jit(solution)/shard_map/ppermute | solution.py:26
  145.5 1.9 collective-permute-start.16
  147.4 3.2 %collective-permute-done.15 = bf16[2,64,512]{2,1,0:T(8,128)(2,1)S(1)} collective-permute-done((bf16[2,64,512]{2,1,0:T(8,128)(2,1)S(1)}, bf16[2,64,512]{2,1,0:T(8,128)(2,1)S(1)}, u32[]{:S(2)}, u32[]{:S(2)}) %collective-permute-start.15) | collective-permute-done | bytes 131104 | tf_op jit(solution)/shard_map/ppermute | solution.py:26
  151.8 3.4 %copy-done.5 = bf16[1024,4096]{1,0:T(8,128)(2,1)S(1)} copy-done((bf16[1024,4096]{1,0:T(8,128)(2,1)S(1)}, bf16[1024,4096]{1,0:T(8,128)(2,1)}, u32[]{:S(2)}) %copy-start.5) | copy-done | bytes 8388632
  156.2 13.7 %forward.1 = (bf16[1024,512]{1,0:T(8,128)(2,1)}, bf16[1024,512]{1,0:T(8,128)(2,1)}, f32[1024,128]{1,0:T(8,128)S(1)}) custom-call(bf16[1024,4096]{1,0:T(8,128)(2,1)S(1)} %copy-done.5, bf16[4096,1024]{1,0:T(8,128)(2,1)} %all-gather.2.cloned.1.call-done.w_ref.refs_1_, bf16[1024,512]{1,0:T(8,128)(2,1)S(1)} %get-tuple-element.19.back_ref.refs_2_.cot_ref, ...), custom_call_target="tpu_custom_call" | custom-call | flops 8589934592 | bytes 20971520 | tf_op jit(solution)/shard_map/forward/pallas_call | solution.py:185
  169.9 3.4 %copy-done.1 = bf16[1024,4096]{1,0:T(8,128)(2,1)S(1)} copy-done((bf16[1024,4096]{1,0:T(8,128)(2,1)S(1)}, bf16[1024,4096]{1,0:T(8,128)(2,1)}, u32[]{:S(2)}) %copy-start.1) | copy-done | bytes 8388632
  173.3 4.9 %backward.4.into_ref = bf16[1024,4096]{1,0:T(8,128)(2,1)} custom-call(bf16[1024,4096]{1,0:T(8,128)(2,1)S(1)} %copy-done.1, bf16[4096,1024]{1,0:T(8,128)(2,1)} %all-gather.2.cloned.1.call-done.w_ref.refs_1_, bf16[1024,512]{1,0:T(8,128)(2,1)S(1)} %get-tuple-element.19.back_ref.refs_2_.cot_ref, bf16[1024,512]{1,0:T(8,128)(2,1)S(1)} %copy-done.6, ...), custom_call_target="tpu_custom_call" | custom-call | flops 2147483648 | bytes 6291456 | tf_op jit(solution)/shard_map/backward/pallas_call | solution.py:239
  178.2 4.9 %backward.5.into_ref = bf16[1024,4096]{1,0:T(8,128)(2,1)} custom-call(bf16[1024,4096]{1,0:T(8,128)(2,1)S(1)} %copy-done.1, bf16[4096,1024]{1,0:T(8,128)(2,1)} %all-gather.2.cloned.1.call-done.w_ref.refs_1_, bf16[1024,512]{1,0:T(8,128)(2,1)S(1)} %get-tuple-element.19.back_ref.refs_2_.cot_ref, ...), custom_call_target="tpu_custom_call", output_to_operand_aliasing={{}: (7, {})} | custom-call | flops 2147483648 | bytes 6291456 | tf_op jit(solution)/shard_map/backward/pallas_call | solution.py:239
  183.1 4.9 %backward.6.into_ref = bf16[1024,4096]{1,0:T(8,128)(2,1)} custom-call(bf16[1024,4096]{1,0:T(8,128)(2,1)S(1)} %copy-done.1, bf16[4096,1024]{1,0:T(8,128)(2,1)} %all-gather.2.cloned.1.call-done.w_ref.refs_1_, bf16[1024,512]{1,0:T(8,128)(2,1)S(1)} %get-tuple-element.19.back_ref.refs_2_.cot_ref, ...), custom_call_target="tpu_custom_call", output_to_operand_aliasing={{}: (7, {})} | custom-call | flops 2147483648 | bytes 6291456 | tf_op jit(solution)/shard_map/backward/pallas_call | solution.py:239
  188.0 4.9 %backward.7 = bf16[1024,4096]{1,0:T(8,128)(2,1)} custom-call(bf16[1024,4096]{1,0:T(8,128)(2,1)S(1)} %copy-done.1, bf16[4096,1024]{1,0:T(8,128)(2,1)} %all-gather.2.cloned.1.call-done.w_ref.refs_1_, bf16[1024,512]{1,0:T(8,128)(2,1)S(1)} %get-tuple-element.19.back_ref.refs_2_.cot_ref, bf16[1024,512]{1,0:T(8,128)(2,1)S(1)} %copy-done.6, ...), custom_call_target="tpu_custom_call", output_to_operand_aliasing={{}: (7, {})} | custom-call | flops 2147483648 | bytes 6291456 | tf_op jit(solution)/shard_map/backward/pallas_call | solution.py:239
  (95 shorter events, 37.1 us)
Async XLA Ops:
  7.2 144.6 %all-gather.2.cloned.1.call-start = ((), (), s32[]{:S(2)}) async-start(), calls=%async_computation | async-start | bytes 8912896 | tf_op jit(solution)/shard_map/all_gather | solution.py:270
  27.4 10.4 %collective-permute-start.5 = (bf16[8,256,512]{2,1,0:T(8,128)(2,1)}, bf16[8,256,512]{2,1,0:T(8,128)(2,1)}, u32[]{:S(2)}, u32[]{:S(2)}) collective-permute-start(bf16[8,256,512]{2,1,0:T(8,128)(2,1)} %sibling_terms.3), channel_id=1, source_target_pairs={{0,8},{1,9},{2,10},{3,11},{4,12},{5,13},{6,14},{7,15},{8,0},{9,1},... | collective-permute-start | bytes 6291464 | tf_op jit(solution)/shard_map/ppermute | solution.py:26
  37.1 16.3 %collective-permute-start = (bf16[8,256,512]{2,1,0:T(8,128)(2,1)}, bf16[8,256,512]{2,1,0:T(8,128)(2,1)}, u32[]{:S(2)}, u32[]{:S(2)}) collective-permute-start(bf16[8,256,512]{2,1,0:T(8,128)(2,1)} %sibling_terms.2), channel_id=1, source_target_pairs={{0,8},{1,9},{2,10},{3,11},{4,12},{5,13},{6,14},{7,15},{8,0},{9,1},... | collective-permute-start | bytes 6291464 | tf_op jit(solution)/shard_map/ppermute | solution.py:26
  48.6 19.7 %collective-permute-start.6 = (bf16[2,256,512]{2,1,0:T(8,128)(2,1)S(1)}, bf16[2,256,512]{2,1,0:T(8,128)(2,1)S(1)}, u32[]{:S(2)}, u32[]{:S(2)}) collective-permute-start(bf16[2,256,512]{2,1,0:T(8,128)(2,1)S(1)} %get-tuple-element.27), channel_id=1, source_target_pairs={{0,32},{1,33},{2,34},{3,35},{4,36},{5,37},{6,38},{7,39},{8,40},{9,... | collective-permute-start | bytes 1572872 | tf_op jit(solution)/shard_map/ppermute | solution.py:26
  50.1 20.1 %collective-permute-start.7 = (bf16[2,256,512]{2,1,0:T(8,128)(2,1)S(1)}, bf16[2,256,512]{2,1,0:T(8,128)(2,1)S(1)}, u32[]{:S(2)}, u32[]{:S(2)}) collective-permute-start(bf16[2,256,512]{2,1,0:T(8,128)(2,1)S(1)} %get-tuple-element.28), channel_id=1, source_target_pairs={{0,64},{1,65},{2,66},{3,67},{4,68},{5,69},{6,70},{7,71},{8,72},{9,... | collective-permute-start | bytes 1572872 | tf_op jit(solution)/shard_map/ppermute | solution.py:26
  51.2 30.6 %collective-permute-start.8 = (bf16[2,256,512]{2,1,0:T(8,128)(2,1)S(1)}, bf16[2,256,512]{2,1,0:T(8,128)(2,1)S(1)}, u32[]{:S(2)}, u32[]{:S(2)}) collective-permute-start(bf16[2,256,512]{2,1,0:T(8,128)(2,1)S(1)} %get-tuple-element.29), channel_id=1, source_target_pairs={{0,96},{1,97},{2,98},{3,99},{4,100},{5,101},{6,102},{7,103},{8,104... | collective-permute-start | bytes 1572872 | tf_op jit(solution)/shard_map/ppermute | solution.py:26
  60.7 35.8 %collective-permute-start.1 = (bf16[4,256,512]{2,1,0:T(8,128)(2,1)S(1)}, bf16[4,256,512]{2,1,0:T(8,128)(2,1)S(1)}, u32[]{:S(2)}, u32[]{:S(2)}) collective-permute-start(bf16[4,256,512]{2,1,0:T(8,128)(2,1)S(1)} %get-tuple-element.25), channel_id=1, source_target_pairs={{0,16},{1,17},{2,18},{3,19},{4,20},{5,21},{6,22},{7,23},{8,24},{9,... | collective-permute-start | bytes 3145736 | tf_op jit(solution)/shard_map/ppermute | solution.py:26
  82.0 16.3 %copy-start.14 = (f32[2,256,512]{2,1,0:T(8,128)}, f32[2,256,512]{2,1,0:T(8,128)S(1)}, u32[]{:S(2)}) copy-start(f32[2,256,512]{2,1,0:T(8,128)S(1)} %add_add_fusion) | copy-start | bytes 3145732
  82.1 21.1 %collective-permute-start.9 = (bf16[256,512]{1,0:T(8,128)(2,1)S(1)}, bf16[256,512]{1,0:T(8,128)(2,1)}, u32[]{:S(2)}, u32[]{:S(2)}) collective-permute-start(bf16[256,512]{1,0:T(8,128)(2,1)S(1)} %fusion.2), channel_id=1, source_target_pairs={{0,16},{1,17},{2,18},{3,19},{4,20},{5,21},{6,22},{7,23},{8,24},{9,... | collective-permute-start | bytes 786440 | tf_op jit(solution)/shard_map/ppermute | solution.py:26
  96.6 17.7 %copy-start.15 = (bf16[256,512]{1,0:T(8,128)(2,1)S(1)}, bf16[256,512]{1,0:T(8,128)(2,1)}, u32[]{:S(2)}) copy-start(bf16[256,512]{1,0:T(8,128)(2,1)} %param.11) | copy-start | bytes 786436
  99.1 17.8 %copy-start.13 = (f32[4096]{0:T(1024)S(1)}, f32[4096]{0:T(1024)}, u32[]{:S(2)}) copy-start(f32[4096]{0:T(1024)} %param.9) | copy-start | bytes 49156
  99.1 9.6 %collective-permute-start.2 = (bf16[256,512]{1,0:T(8,128)(2,1)}, bf16[256,512]{1,0:T(8,128)(2,1)}, u32[]{:S(2)}, u32[]{:S(2)}) collective-permute-start(bf16[256,512]{1,0:T(8,128)(2,1)} %get-tuple-element.42), channel_id=1, source_target_pairs={{0,32},{1,33},{2,34},{3,35},{4,36},{5,37},{6,38},{7,39},{8,40},{9,... | collective-permute-start | bytes 786440 | tf_op jit(solution)/shard_map/ppermute | solution.py:26
  100.6 8.7 %collective-permute-start.4 = (bf16[256,512]{1,0:T(8,128)(2,1)}, bf16[256,512]{1,0:T(8,128)(2,1)}, u32[]{:S(2)}, u32[]{:S(2)}) collective-permute-start(bf16[256,512]{1,0:T(8,128)(2,1)} %get-tuple-element.43), channel_id=1, source_target_pairs={{0,96},{1,97},{2,98},{3,99},{4,100},{5,101},{6,102},{7,103},{8,104... | collective-permute-start | bytes 786440 | tf_op jit(solution)/shard_map/ppermute | solution.py:26
  101.2 13.1 %collective-permute-start.3 = (bf16[256,512]{1,0:T(8,128)(2,1)S(1)}, bf16[256,512]{1,0:T(8,128)(2,1)}, u32[]{:S(2)}, u32[]{:S(2)}) collective-permute-start(bf16[256,512]{1,0:T(8,128)(2,1)S(1)} %get-tuple-element.44), channel_id=1, source_target_pairs={{0,64},{1,65},{2,66},{3,67},{4,68},{5,69},{6,70},{7,71},{8,72},{9,... | collective-permute-start | bytes 786440 | tf_op jit(solution)/shard_map/ppermute | solution.py:26
  117.1 1.2 collective-permute-start.17
  118.3 9.1 %collective-permute-start.19 = (f32[32,128]{1,0:T(8,128)S(1)}, f32[32,128]{1,0:T(8,128)S(1)}, u32[]{:S(2)}, u32[]{:S(2)}) collective-permute-start(f32[32,128]{1,0:T(8,128)S(1)} %bitcast_add_fusion), channel_id=1, source_target_pairs={{0,32},{1,33},{2,34},{3,35},{4,36},{5,37},{6,38},{7,39},{8,40},{9,... | collective-permute-start | bytes 49160 | tf_op jit(solution)/shard_map/ppermute | solution.py:26
  118.3 10.5 %collective-permute-start.20 = (f32[32,128]{1,0:T(8,128)S(1)}, f32[32,128]{1,0:T(8,128)S(1)}, u32[]{:S(2)}, u32[]{:S(2)}) collective-permute-start(f32[32,128]{1,0:T(8,128)S(1)} %bitcast_add_fusion), channel_id=1, source_target_pairs={{0,96},{1,97},{2,98},{3,99},{4,100},{5,101},{6,102},{7,103},{8,104... | collective-permute-start | bytes 49160 | tf_op jit(solution)/shard_map/ppermute | solution.py:26
  120.3 8.5 %collective-permute-start.18 = (f32[32,128]{1,0:T(8,128)S(1)}, f32[32,128]{1,0:T(8,128)S(1)}, u32[]{:S(2)}, u32[]{:S(2)}) collective-permute-start(f32[32,128]{1,0:T(8,128)S(1)} %bitcast_add_fusion), channel_id=1, source_target_pairs={{0,64},{1,65},{2,66},{3,67},{4,68},{5,69},{6,70},{7,71},{8,72},{9,... | collective-permute-start | bytes 49160 | tf_op jit(solution)/shard_map/ppermute | solution.py:26
  123.1 7.9 %collective-permute-start.10 = (bf16[2,64,512]{2,1,0:T(8,128)(2,1)S(1)}, bf16[2,64,512]{2,1,0:T(8,128)(2,1)S(1)}, u32[]{:S(2)}, u32[]{:S(2)}) collective-permute-start(bf16[2,64,512]{2,1,0:T(8,128)(2,1)S(1)} %get-tuple-element.39), channel_id=1, source_target_pairs={{0,2},{1,3},{2,4},{3,5},{4,6},{5,7},{6,0},{7,1},{8,10},{9,11},{10,... | collective-permute-start | bytes 393224 | tf_op jit(solution)/shard_map/ppermute | solution.py:26
  124.6 8.5 %collective-permute-start.11 = (bf16[2,64,512]{2,1,0:T(8,128)(2,1)S(1)}, bf16[2,64,512]{2,1,0:T(8,128)(2,1)S(1)}, u32[]{:S(2)}, u32[]{:S(2)}) collective-permute-start(bf16[2,64,512]{2,1,0:T(8,128)(2,1)S(1)} %get-tuple-element.40), channel_id=1, source_target_pairs={{0,4},{1,5},{2,6},{3,7},{4,0},{5,1},{6,2},{7,3},{8,12},{9,13},{10,... | collective-permute-start | bytes 393224 | tf_op jit(solution)/shard_map/ppermute | solution.py:26
  127.4 5.9 %collective-permute-start.12 = (bf16[2,64,512]{2,1,0:T(8,128)(2,1)S(1)}, bf16[2,64,512]{2,1,0:T(8,128)(2,1)S(1)}, u32[]{:S(2)}, u32[]{:S(2)}) collective-permute-start(bf16[2,64,512]{2,1,0:T(8,128)(2,1)S(1)} %get-tuple-element.41), channel_id=1, source_target_pairs={{0,6},{1,7},{2,0},{3,1},{4,2},{5,3},{6,4},{7,5},{8,14},{9,15},{10,... | collective-permute-start | bytes 393224 | tf_op jit(solution)/shard_map/ppermute | solution.py:26
  128.8 6.1 %collective-permute-start.23 = (f32[32,128]{1,0:T(8,128)S(1)}, f32[32,128]{1,0:T(8,128)S(1)}, u32[]{:S(2)}, u32[]{:S(2)}) collective-permute-start(f32[32,128]{1,0:T(8,128)S(1)} %add_add_fusion.2), channel_id=1, source_target_pairs={{0,6},{1,7},{2,0},{3,1},{4,2},{5,3},{6,4},{7,5},{8,14},{9,15},{10,... | collective-permute-start | bytes 49160 | tf_op jit(solution)/shard_map/ppermute | solution.py:26
  128.9 6.0 %collective-permute-start.22 = (f32[32,128]{1,0:T(8,128)S(1)}, f32[32,128]{1,0:T(8,128)S(1)}, u32[]{:S(2)}, u32[]{:S(2)}) collective-permute-start(f32[32,128]{1,0:T(8,128)S(1)} %add_add_fusion.2), channel_id=1, source_target_pairs={{0,2},{1,3},{2,4},{3,5},{4,6},{5,7},{6,0},{7,1},{8,10},{9,11},{10,... | collective-permute-start | bytes 49160 | tf_op jit(solution)/shard_map/ppermute | solution.py:26
  130.9 5.2 %collective-permute-start.21 = (f32[32,128]{1,0:T(8,128)S(1)}, f32[32,128]{1,0:T(8,128)S(1)}, u32[]{:S(2)}, u32[]{:S(2)}) collective-permute-start(f32[32,128]{1,0:T(8,128)S(1)} %add_add_fusion.2), channel_id=1, source_target_pairs={{0,4},{1,5},{2,6},{3,7},{4,0},{5,1},{6,2},{7,3},{8,12},{9,13},{10,... | collective-permute-start | bytes 49160 | tf_op jit(solution)/shard_map/ppermute | solution.py:26
  134.3 5.2 %collective-permute-start.13 = (bf16[2,64,512]{2,1,0:T(8,128)(2,1)S(1)}, bf16[2,64,512]{2,1,0:T(8,128)(2,1)S(1)}, u32[]{:S(2)}, u32[]{:S(2)}) collective-permute-start(bf16[2,64,512]{2,1,0:T(8,128)(2,1)S(1)} %fusion.8), channel_id=1, source_target_pairs={{0,1},{1,0},{2,3},{3,2},{4,5},{5,4},{6,7},{7,6},{8,9},{9,8},{10,11... | collective-permute-start | bytes 393224 | tf_op jit(solution)/shard_map/ppermute | solution.py:26
  136.2 4.8 %collective-permute-start.26 = (f32[32,128]{1,0:T(8,128)S(1)}, f32[32,128]{1,0:T(8,128)S(1)}, u32[]{:S(2)}, u32[]{:S(2)}) collective-permute-start(f32[32,128]{1,0:T(8,128)S(1)} %add_add_fusion.1), channel_id=1, source_target_pairs={{0,17},{1,0},{2,19},{3,2},{4,21},{5,4},{6,23},{7,6},{8,25},{9,8},{... | collective-permute-start | bytes 49160 | tf_op jit(solution)/shard_map/ppermute | solution.py:26
  137.2 4.9 %collective-permute-start.25 = (f32[32,128]{1,0:T(8,128)S(1)}, f32[32,128]{1,0:T(8,128)S(1)}, u32[]{:S(2)}, u32[]{:S(2)}) collective-permute-start(f32[32,128]{1,0:T(8,128)S(1)} %add_add_fusion.1), channel_id=1, source_target_pairs={{0,1},{1,16},{2,3},{3,18},{4,5},{5,20},{6,7},{7,22},{8,9},{9,24},{... | collective-permute-start | bytes 49160 | tf_op jit(solution)/shard_map/ppermute | solution.py:26
  138.3 5.2 %collective-permute-start.24 = (f32[32,128]{1,0:T(8,128)S(1)}, f32[32,128]{1,0:T(8,128)S(1)}, u32[]{:S(2)}, u32[]{:S(2)}) collective-permute-start(f32[32,128]{1,0:T(8,128)S(1)} %add_add_fusion.1), channel_id=1, source_target_pairs={{0,16},{1,17},{2,18},{3,19},{4,20},{5,21},{6,22},{7,23},{8,24},{9,... | collective-permute-start | bytes 49160 | tf_op jit(solution)/shard_map/ppermute | solution.py:26
  139.6 12.2 %copy-start.9 = (f32[1024,128]{1,0:T(8,128)S(1)}, f32[1024,128]{1,0:T(8,128)}, u32[]{:S(2)}) copy-start(f32[1024,128]{1,0:T(8,128)} %constant.118.clone.sin_ref) | copy-start | bytes 1572868
  139.7 7.7 %collective-permute-start.14 = (bf16[2,64,512]{2,1,0:T(8,128)(2,1)S(1)}, bf16[2,64,512]{2,1,0:T(8,128)(2,1)S(1)}, u32[]{:S(2)}, u32[]{:S(2)}) collective-permute-start(bf16[2,64,512]{2,1,0:T(8,128)(2,1)S(1)} %get-tuple-element.34), channel_id=1, source_target_pairs={{0,2},{1,3},{2,4},{3,5},{4,6},{5,7},{6,0},{7,1},{8,10},{9,11},{10,... | collective-permute-start | bytes 393224 | tf_op jit(solution)/shard_map/ppermute | solution.py:26
  144.1 6.5 %collective-permute-start.15 = (bf16[2,64,512]{2,1,0:T(8,128)(2,1)S(1)}, bf16[2,64,512]{2,1,0:T(8,128)(2,1)S(1)}, u32[]{:S(2)}, u32[]{:S(2)}) collective-permute-start(bf16[2,64,512]{2,1,0:T(8,128)(2,1)S(1)} %get-tuple-element.34), channel_id=1, source_target_pairs={{0,4},{1,5},{2,6},{3,7},{4,0},{5,1},{6,2},{7,3},{8,12},{9,13},{10,... | collective-permute-start | bytes 393224 | tf_op jit(solution)/shard_map/ppermute | solution.py:26
  145.5 5.2 %collective-permute-start.16 = (bf16[2,64,512]{2,1,0:T(8,128)(2,1)S(1)}, bf16[2,64,512]{2,1,0:T(8,128)(2,1)S(1)}, u32[]{:S(2)}, u32[]{:S(2)}) collective-permute-start(bf16[2,64,512]{2,1,0:T(8,128)(2,1)S(1)} %get-tuple-element.34), channel_id=1, source_target_pairs={{0,6},{1,7},{2,0},{3,1},{4,2},{5,3},{6,4},{7,5},{8,14},{9,15},{10,... | collective-permute-start | bytes 393224 | tf_op jit(solution)/shard_map/ppermute | solution.py:26
  (12 other events, 32.7 us)
Sparse Core Ops, SparseCore 0:
  11.0 83.5 all-gather.1

commit v2 on v0

v2 whole, which is shorter than its diff:
```python
import math

import jax
import jax.numpy as jnp
import numpy as np
from jax import lax
from jax.experimental import pallas as pl
from jax.experimental.pallas import tpu as pltpu
from jax.sharding import Mesh, PartitionSpec as P

HEAD = 128
AXES = ("x", "zh", "c", "y", "zl")
SIZES = (4, 2, 2, 4, 2)
F32 = jnp.float32
BF16 = jnp.bfloat16
MIB = 1 << 20


def send(value, move):
    pairs = []
    for i in range(math.prod(SIZES)):
        x, zh, c, y, zl = (int(v) for v in np.unravel_index(i, SIZES))
        x, y, z, c = move(x, y, zh * 2 + zl, c)
        x, y, z, c = x % 4, y % 4, z % 4, c % 2
        pairs.append((i, int(np.ravel_multi_index((x, z // 2, c, y, z % 2), SIZES))))
    return lax.ppermute(value, AXES, pairs)


def to_core(value):
    return send(value, lambda x, y, z, c: (x, y, z, c + 1))


def to_x(value, d):
    return send(value, lambda x, y, z, c: (x + d, y, z, c))


def to_y(value, d):
    return send(value, lambda x, y, z, c: (x, y + d, z, c))


def to_z(value, d):
    return send(value, lambda x, y, z, c: (x, y, z + d, c))


def to_zl(value):
    return send(value, lambda x, y, z, c: (x, y, z ^ 1, c))


def params(mib, **more):
    return pltpu.CompilerParams(vmem_limit_bytes=mib * MIB, **more)


def turn(values, cosine, sine, direction):
    parts = []
    for h in range(values.shape[1] // HEAD):
        v = values[:, h * HEAD : (h + 1) * HEAD]
        parts.append(v * cosine + direction * (pltpu.roll(v, HEAD // 2, 1) * sine))
    return jnp.concatenate(parts, axis=1)


RESIDENT = pl.BlockSpec(memory_space=pltpu.VMEM)
UNREAD = pl.BlockSpec(memory_space=pl.ANY)


def in_hbm(value):
    return pltpu.with_memory_space_constraint(value, pltpu.HBM)


def norm_kernel(
    order_ref, tok_ref, gain_ref, kc_ref, vc_ref, cos_ref, sin_ref, after_ref,
    both_out_ref, inv_ref, stored_ref, sib_v_ref, sib_k_ref, own_v_ref, own_k_ref, normed_ref, both_ref, done,
):
    i = pl.program_id(0)
    tb, feats = kc_ref.shape
    store = pltpu.make_async_copy(normed_ref, stored_ref, done)

    @pl.when(i < 4)
    def _():
        def rows(r, carry):
            at = pl.ds(pl.multiple_of(r * 16, 16), 16)
            v = tok_ref[at, :].astype(F32)
            inv = lax.rsqrt(jnp.mean(v * v, axis=1, keepdims=True) + 1e-05)
            inv_ref[at, :] = jnp.broadcast_to(inv, (16, HEAD))
            to = pl.ds(pl.multiple_of(i * tb + r * 16, 16), 16)
            normed_ref[to, :] = (tok_ref[at, :].astype(F32) * inv * gain_ref[...]).astype(BF16)
            return carry

        lax.fori_loop(0, tb // 16, rows, 0, unroll=2)
        here = pl.ds(pl.multiple_of(i * tb, tb), tb)
        back = turn(kc_ref[...].astype(F32), cos_ref[...], sin_ref[...], -1.0).astype(BF16)
        both_ref[here, :feats] = back
        both_ref[here, feats:] = vc_ref[...]
        both_out_ref[:, :feats] = back
        both_out_ref[:, feats:] = vc_ref[...]

    @pl.when(i == 4)
    def _():
        store.start()

    def part(value_ref, key_ref):
        for j in range(2):
            columns = pl.ds(pl.multiple_of(order_ref[(i - 4) * 2 + j] * 256, 256), 256)
            total = lax.dot_general(
                normed_ref[:, columns], both_ref[...], (((0,), (0,)), ((), ())), preferred_element_type=F32
            )
            key_ref[j] = total[:, :feats].astype(BF16)
            value_ref[j] = total[:, feats:].astype(BF16)

    pl.when((i >= 4) & (i < 8))(lambda: part(sib_v_ref, sib_k_ref))
    pl.when(i >= 8)(lambda: part(own_v_ref, own_k_ref))

    @pl.when(i == 11)
    def _():
        store.wait()


def norm_and_terms(order, tokens, gain, key_cot, value_cot, cosine, sine, after):
    rows, width = tokens.shape
    feats = key_cot.shape[1]
    tb = rows // 4
    by_rows = lambda n: pl.BlockSpec((tb, n), lambda i, order: (jnp.minimum(i, 3), 0))
    pairs = lambda first: pl.BlockSpec((2, 256, feats), lambda i, order: (jnp.clip(i - first, 0, 3), 0, 0))
    return pl.pallas_call(
        norm_kernel,
        grid_spec=pltpu.PrefetchScalarGridSpec(
            num_scalar_prefetch=1,
            grid=(12,),
            in_specs=[
                by_rows(width),
                pl.BlockSpec((1, width), lambda i, order: (0, 0)),
                by_rows(feats),
                by_rows(feats),
                by_rows(HEAD),
                by_rows(HEAD),
                UNREAD,
            ],
            out_specs=[by_rows(2 * feats), by_rows(HEAD), pl.BlockSpec(memory_space=pltpu.HBM)]
            + [pairs(4), pairs(4), pairs(8), pairs(8)],
            scratch_shapes=[
                pltpu.VMEM((rows, width), BF16),
                pltpu.VMEM((rows, 2 * feats), BF16),
                pltpu.SemaphoreType.DMA,
            ],
        ),
        out_shape=[
            pltpu.HBM((rows, 2 * feats), BF16),
            pltpu.HBM((rows, HEAD), F32),
            pltpu.HBM((rows, width), BF16),
        ]
        + [pltpu.HBM((8, 256, feats), BF16)] * 4,
        compiler_params=params(56),
        cost_estimate=pl.CostEstimate(flops=16000 * MIB, bytes_accessed=20 * MIB, transcendentals=0),
        name="norm_and_terms",
    )(order, in_hbm(tokens), gain, in_hbm(key_cot), in_hbm(value_cot), cosine, sine, in_hbm(after))


def add_values_kernel(y_ref, own_ref, got_ref, after_ref, *refs):
    out_refs, total_ref = refs[:4], refs[4]
    for j in range(own_ref.shape[0]):
        total_ref[...] = own_ref[j].astype(F32) + got_ref[j].astype(F32)
        for d in range(4):
            first = pl.multiple_of(lax.rem(y_ref[0] + d, 4) * 64, 64)
            out_refs[d][j] = total_ref[pl.ds(first, 64), :].astype(BF16)


def add_values(y, own, got, after):
    feats = own.shape[2]
    block = pl.BlockSpec((2, 256, feats), lambda g, y: (g, 0, 0))
    return pl.pallas_call(
        add_values_kernel,
        grid_spec=pltpu.PrefetchScalarGridSpec(
            num_scalar_prefetch=1,
            grid=(4,),
            in_specs=[block, block, UNREAD],
            out_specs=[pl.BlockSpec((2, 64, feats), lambda g, y: (g, 0, 0))] * 4,
            scratch_shapes=[pltpu.VMEM((256, feats), F32)],
        ),
        out_shape=[pltpu.HBM((8, 64, feats), BF16)] * 4,
        compiler_params=params(56),
        cost_estimate=pl.CostEstimate(flops=MIB, bytes_accessed=6 * MIB, transcendentals=0),
        name="add_values",
    )(y.reshape(1), in_hbm(own), in_hbm(got), in_hbm(after))


def add_keys_kernel(own_ref, got_ref, after_ref, near_ref, far_ref):
    for j, out_ref in enumerate((near_ref, far_ref)):
        out_ref[0] = (own_ref[j].astype(F32) + got_ref[j].astype(F32)).astype(BF16)


def add_keys(own, got, after):
    feats = own.shape[2]
    block = pl.BlockSpec((2, 256, feats), lambda g: (g, 0, 0))
    return pl.pallas_call(
        add_keys_kernel,
        grid=(4,),
        in_specs=[block, block, UNREAD],
        out_specs=[pl.BlockSpec((1, 256, feats), lambda g: (g, 0, 0))] * 2,
        out_shape=[pltpu.HBM((4, 256, feats), BF16)] * 2,
        compiler_params=params(56),
        cost_estimate=pl.CostEstimate(flops=MIB, bytes_accessed=6 * MIB, transcendentals=0),
        name="add_keys",
    )(in_hbm(own), in_hbm(got), in_hbm(after))


def forward_kernel(normed_ref, both_ref, inv_ref, cos_ref, sin_ref, w_ref, after_ref, key_ref, value_ref, coef_ref, held_ref, done):
    feats = key_ref.shape[1]
    parts = done.shape[0]
    depth = w_ref.shape[0] // parts
    first_step = pl.program_id(0) == 0
    at = [pl.ds(p * depth, depth) for p in range(parts)]
    copies = [pltpu.make_async_copy(w_ref.at[at[p], :], held_ref.at[at[p], :], done.at[p]) for p in range(parts)]

    @pl.when(first_step)
    def _():
        for copy in copies:
            copy.start()

    pre = None
    for p in range(parts):
        pl.when(first_step)(copies[p].wait)
        term = jnp.dot(normed_ref[:, at[p]], held_ref[at[p], :], preferred_element_type=F32)
        pre = term if pre is None else pre + term
    key_pre, value_pre = pre[:, :feats], pre[:, feats:]
    key_ref[...] = turn(key_pre, cos_ref[...], sin_ref[...], 1.0).astype(BF16)
    value_ref[...] = value_pre.astype(BF16)
    inner = jnp.sum(
        key_pre * both_ref[:, :feats].astype(F32) + value_pre * both_ref[:, feats:].astype(F32), axis=1, keepdims=True
    )
    inv = inv_ref[...]
    coef_ref[...] = inv * inv * (inner * (1.0 / normed_ref.shape[1]))


def forward(normed, both, inv, cosine, sine, weights, after):
    rows, width = normed.shape
    feats = both.shape[1] // 2
    tb = 256
    by_rows = lambda n: pl.BlockSpec((tb, n), lambda i: (i, 0))
    return pl.pallas_call(
        forward_kernel,
        grid=(rows // tb,),
        in_specs=[by_rows(width), by_rows(2 * feats), by_rows(HEAD), by_rows(HEAD), by_rows(HEAD), UNREAD, UNREAD],
        out_specs=[by_rows(feats), by_rows(feats), by_rows(HEAD)],
        scratch_shapes=[pltpu.VMEM(weights.shape, BF16), pltpu.SemaphoreType.DMA((4,))],
        out_shape=[
            pltpu.HBM((rows, feats), BF16),
            pltpu.HBM((rows, feats), BF16),
            pltpu.HBM((rows, HEAD), F32),
        ],
        compiler_params=params(56),
        cost_estimate=pl.CostEstimate(flops=4 * rows * width * feats, bytes_accessed=20 * MIB, transcendentals=0),
        name="forward",
    )(in_hbm(normed), in_hbm(both), in_hbm(inv), cosine, sine, in_hbm(weights), in_hbm(after))


def backward_kernel(tok_ref, both_ref, inv_ref, coef_ref, gain_ref, w_ref, after_ref, *refs):
    out_ref = refs[-1]
    for h in range(w_ref.shape[0] // 256):
        s = slice(h * 256, h * 256 + 256)
        grad = lax.dot_general(both_ref[...], w_ref[s], (((1,), (1,)), ((), ())), preferred_element_type=F32)
        out = inv_ref[:, :1] * (grad * gain_ref[:, s]) - tok_ref[:, s].astype(F32) * coef_ref[:, :1]
        out_ref[:, s] = out.astype(BF16)


def backward(first, blocks, tokens, both, inv, coef, gain, weights, into, after):
    rows, width = tokens.shape
    feats = both.shape[1] // 2
    cb = 512
    whole = lambda n: pl.BlockSpec((rows, n), lambda i: (0, 0))
    columns = pl.BlockSpec((rows, cb), lambda i: (0, i + first))
    operands = [in_hbm(tokens), in_hbm(both), in_hbm(inv), in_hbm(coef), gain, in_hbm(weights), in_hbm(after)]
    specs = [
        columns,
        whole(2 * feats),
        whole(HEAD),
        whole(HEAD),
        pl.BlockSpec((1, cb), lambda i: (0, i + first)),
        pl.BlockSpec((cb, 2 * feats), lambda i: (i + first, 0)),
        UNREAD,
    ]
    aliases = {}
    if into is not None:
        aliases = {len(operands): 0}
        operands.append(in_hbm(into))
        specs.append(UNREAD)
    return pl.pallas_call(
        backward_kernel,
        grid=(blocks,),
        in_specs=specs,
        out_specs=columns,
        out_shape=pltpu.HBM((rows, width), BF16),
        input_output_aliases=aliases,
        compiler_params=params(56),
        cost_estimate=pl.CostEstimate(
            flops=4 * blocks * rows * cb * feats, bytes_accessed=6 * blocks * rows * cb, transcendentals=0
        ),
        name="backward",
    )(*operands)


def total_of(refs):
    total = refs[0][...].astype(F32)
    for ref in refs[1:]:
        total += ref[...].astype(F32)
    return total


def join(kernel, name, operands, shapes, after=(), scalars=(), place=in_hbm):
    specs = [pl.BlockSpec(memory_space=pltpu.SMEM)] * len(scalars) + [RESIDENT] * len(operands) + [UNREAD] * len(after)
    return pl.pallas_call(
        kernel,
        in_specs=specs,
        out_specs=[RESIDENT] * len(shapes),
        out_shape=shapes,
        compiler_params=params(56),
        cost_estimate=pl.CostEstimate(flops=2 * MIB, bytes_accessed=4 * MIB, transcendentals=0),
        name=name,
    )(*scalars, *(place(o) for o in operands), *(in_hbm(a) for a in after))


def join_first_kernel(v0, v1, v2, v3, k0, k1, own_ref, *out_refs):
    for d in range(4):
        values = v0[2 * d : 2 * d + 2].astype(F32)
        for v in (v1, v2, v3):
            values += v[2 * d : 2 * d + 2].astype(F32)
        keys = k0[d].astype(F32) + k1[d].astype(F32)
        out_ref = own_ref if d == 0 else out_refs[d - 1]
        out_ref[:2] = values.astype(out_ref.dtype)
        for q in range(4):
            out_ref[2 + q] = keys[q * 64 : q * 64 + 64].astype(out_ref.dtype)


def join_x_kernel(y_ref, own, x1, x2, x3, value_ref, key_ref, to_z_ref, *to_y_refs):
    def sum_of(i):
        return own[i] + (x1[i].astype(F32) + x2[i].astype(F32) + x3[i].astype(F32))

    value_ref[...] = sum_of(0)
    to_z_ref[...] = sum_of(1).astype(BF16)
    for d in range(4):
        part = sum_of(2 + lax.rem(y_ref[0] + d, 4))
        if d == 0:
            key_ref[...] = part
        else:
            to_y_refs[d - 1][...] = part.astype(BF16)


def join_zy_kernel(value, z1, key, y1, y2, y3, after_ref, out_ref):
    out_ref[0] = total_of([key, y1, y2, y3]).astype(BF16)
    out_ref[1] = total_of([value, z1]).astype(BF16)


def join_zl_kernel(count, mine, other, out_ref):
    out_ref[...] = (total_of([mine, other]) * (1.0 / count)).astype(BF16)


def finish_kernel(y_ref, p0_ref, p1_ref, p2_ref, p3_ref, kw_ref, vw_ref, gain_ref, after_ref, key_ref, value_ref, g_ref):
    for d, p_ref in enumerate((p0_ref, p1_ref, p2_ref, p3_ref)):
        first = pl.multiple_of(lax.rem(y_ref[0] + 4 - d, 4) * 64, 64)
        key_ref[pl.ds(first, 64), :] = p_ref[0].astype(F32)
        value_ref[pl.ds(first, 64), :] = p_ref[1].astype(F32)
    products = key_ref[...] * kw_ref[...].astype(F32) + value_ref[...] * vw_ref[...].astype(F32)
    sums = jnp.broadcast_to(jnp.sum(products, axis=1, keepdims=True), (products.shape[0], HEAD))
    g_ref[...] = jnp.broadcast_to(sums.T[:1] / gain_ref[...], g_ref.shape)


def finish(y, pieces, key_weight, value_weight, own_gain, after):
    rows, feats = key_weight.shape
    return pl.pallas_call(
        finish_kernel,
        in_specs=[pl.BlockSpec(memory_space=pltpu.SMEM)] + [RESIDENT] * 7 + [UNREAD],
        out_specs=[RESIDENT] * 3,
        out_shape=[
            jax.ShapeDtypeStruct((rows, feats), F32),
            jax.ShapeDtypeStruct((rows, feats), F32),
            jax.ShapeDtypeStruct((16, rows), F32),
        ],
        compiler_params=params(56),
        cost_estimate=pl.CostEstimate(flops=4 * rows * feats, bytes_accessed=8 * rows * feats, transcendentals=0),
        name="finish",
    )(y.reshape(1), *pieces, key_weight, value_weight, own_gain, in_hbm(after))


def shards(tokens, norm_gain, key_weight, value_weight, key_cotangent, value_cotangent):
    length, width = tokens.shape
    feats = key_weight.shape[1]
    count = math.prod(SIZES)
    x, zh, core, y = (lax.axis_index(a).astype(jnp.int32) for a in ("x", "zh", "c", "y"))
    half = HEAD // 2
    angles = np.arange(length)[:, None] * np.exp(-(2.0 * np.arange(half) / HEAD) * math.log(500000.0))[None, :]
    cosine = jnp.asarray(np.concatenate([np.cos(angles), np.cos(angles)], 1).astype(np.float32))
    sine = jnp.asarray(np.concatenate([-np.sin(angles), np.sin(angles)], 1).astype(np.float32))
    gain = norm_gain.reshape(1, width)

    shard = jnp.concatenate([key_weight, value_weight], axis=1)
    weights = lax.all_gather(shard, ("x", "zh", "c"), axis=0, tiled=True)

    shape = pltpu.HBM
    i4, j2 = jnp.arange(4, dtype=jnp.int32), jnp.arange(2, dtype=jnp.int32)
    order = (((x + i4) % 4)[:, None] * 4 + ((zh + j2) % 2)[None, :] * 2).reshape(8)
    order = jnp.concatenate([order + 1 - core, order + core])
    both, inv, normed, sib_v, sib_k, own_v, own_k = norm_and_terms(
        order, tokens, gain, key_cotangent, value_cotangent, cosine, sine, shard
    )
    got_v, got_k = to_core(sib_v), to_core(sib_k)
    value_terms = add_values(y, own_v, got_v, inv)
    key_near, key_far = add_keys(own_k, got_k, value_terms[0])
    ring = lambda value: send(value, lambda x, y, z, c: (x + 1 - 2 * c, y, z, c))
    piece = shape((64, feats), BF16)
    got_y = [to_y(value_terms[d], d) for d in (1, 2, 3)]
    got_z = to_z(key_far, 2)
    own, *for_x = join(
        join_first_kernel,
        "join_first",
        [value_terms[0], *got_y, key_near, got_z],
        [shape((6, 64, feats), F32)] + [shape((6, 64, feats), BF16)] * 3,
    )
    got_x = [to_x(for_x[d - 1], d) for d in (1, 2, 3)]
    value_part, key_part, for_z, *for_y = join(
        join_x_kernel,
        "join_x",
        [own, *got_x],
        [shape((64, feats), F32)] * 2 + [piece] * 4,
        [],
        [y.reshape(1)],
    )
    got_z = to_z(for_z, 2)
    got_y = [to_y(for_y[d - 1], d) for d in (1, 2, 3)]
    rotated_keys, value_rows, coef = forward(normed, both, inv, cosine, sine, weights, for_z)
    pair = [shape((2, 64, feats), BF16)]
    (mine,) = join(join_zy_kernel, "join_zy", [value_part, got_z, key_part, *got_y], pair, [coef])
    (mine,) = join(lambda *refs: join_zl_kernel(count, *refs), "join_zl", [mine, to_zl(mine)], pair)
    parts = [mine] + [to_y(mine, d) for d in (1, 2, 3)]
    input_grad = backward(0, 4, tokens, both, inv, coef, gain, weights, None, mine)

    own_gain = lax.dynamic_slice(gain, (0, (x * 4 + zh * 2 + core) * 256), (1, 256))
    key_grad, value_grad, gain_rows = finish(y, parts, key_weight, value_weight, own_gain, input_grad)
    gain_grad = lax.all_to_all(gain_rows, ("x", "zh", "c"), 0, 0, tiled=True).reshape(width)
    input_grad = backward(4, 4, tokens, both, inv, coef, gain, weights, input_grad, gain_rows)
    return rotated_keys, value_rows, input_grad, key_grad, value_grad, gain_grad


def solution(mesh):
    fine = Mesh(mesh.devices.reshape(SIZES), AXES)
    fsdp, replica = ("x", "zh", "c"), ("y", "zl")
    in_specs = (P(fsdp + replica, None), P(), P(fsdp, None), P(fsdp, None), P(fsdp + replica, None), P(fsdp + replica, None))
    out_specs = (P(fsdp + replica, None), P(fsdp + replica, None), P(fsdp + replica, None), P(fsdp, None), P(fsdp, None), P())
    return jax.shard_map(shards, mesh=fine, in_specs=in_specs, out_specs=out_specs, check_vma=False)
```

time: 364 us -> 200 us (0.55)
  waiting for transfers between devices: 189 us -> 60.2 us
  Pallas kernels: 0 us -> 79.7 us
  blocking collectives: 70.2 us -> 0 us
  matrix products: 62 us -> 0 us
  starting transfers between devices: 0.34 us -> 32 us
  other arithmetic: 23.1 us -> 0.69 us
  local copies, waits for them, and re-layouts: 5.2 us -> 11.2 us
    pallas_call x0 -> x11, Pallas kernels: none -> 79.7 us  [the longest x1 24 us: norm_and_terms(): pl.pallas_call(norm_kernel, grid_spec=pltpu.PrefetchScalarGridSpec(num_sc...]
    all_gather x2 -> x1, waiting for transfers between devices: 70.3 us -> 0.01 us  [shards(): weights = lax.all_gather(shard, ('x', 'zh', 'c'), axis=0, tiled=True)]
    psum x1 -> x0, blocking collectives: 70.2 us -> none  [shards(): gain_grad = lax.psum(gain_local, ('fsdp', 'replica')) / count]
    psum x1 -> x0, waiting for transfers between devices: 66.1 us -> none  [shards(): summed = lax.psum(shard, 'replica')]
    dot_general x5 -> x0, matrix products: 62 us -> none  [the longest x1 17.3 us: shards(): lax.dot_general(value_cotangent, full_value, contract, preferred_element_...]
    ppermute x0 -> x17, waiting for transfers between devices: none -> 60.1 us  [send(): return lax.ppermute(value, AXES, pairs)]
    reduce_scatter x1 -> x0, waiting for transfers between devices: 50.8 us -> none  [shards(): lax.psum_scatter(lax.dot_general(normed, both, (((0,), (0,)), ((), ())),...]
    ppermute x0 -> x17, starting transfers between devices: none -> 24.7 us  [send(): return lax.ppermute(value, AXES, pairs)]
  transfers between devices with their start and end apart: 4 -> 19, of which waited for: 4 -> 8; matrix products, arithmetic and copies ran while one was open for 24% -> 1% of each run, Pallas kernels for 0% -> 37%
where the time goes in v2:
time: 200 us; the launch traced here: 198 us
  Pallas kernels  79.7 us (40%)
  waiting for transfers between devices  60.2 us (30%)
  starting transfers between devices  32 us (16%)
  between operations  14.3 us (7%)
  local copies, waits for them, and re-layouts  11.2 us (6%)
    ppermute x17, waiting for transfers between devices, send(): return lax.ppermute(value, AXES, pairs)  60.1 us
    ppermute x17, starting transfers between devices, send(): return lax.ppermute(value, AXES, pairs)  24.7 us
    pallas_call x1, Pallas kernels, norm_and_terms(): pl.pallas_call(norm_kernel, grid_spec=pltpu.PrefetchScalarGridSpec(num_sc...  24 us
    pallas_call x2, Pallas kernels, backward(): pl.pallas_call(backward_kernel, grid=(blocks,), in_specs=specs, out_specs...  19.1 us
    pallas_call x1, Pallas kernels, forward(): pl.pallas_call(forward_kernel, grid=(rows // tb,), in_specs=[by_rows(widt...  15.7 us
    pallas_call x4, Pallas kernels, join(): pl.pallas_call(kernel, in_specs=specs, out_specs=[RESIDENT] * len(shapes)...  9.4 us
    unnamed x42, local copies, waits for them, and re-layouts  7.42 us
    all_to_all x1, starting transfers between devices, shards(): lax.all_to_all(gain_rows, ('x', 'zh', 'c'), 0, 0, tiled=True).reshape(width)  7.27 us
  transfers between devices with their start and end apart: 19, of which 8 were waited for; matrix products, arithmetic and copies ran while one was open for 1% of the time, Pallas kernels for 37%

profile of v2, /device:TPU:2, one launch (start us, length us, event | category | flops | bytes accessed | tf_op | source)
XLA Modules:
  0.0 197.9 jit_solution(243568773462986899)
XLA Ops:
  10.9 24.0 %norm_and_terms.1 = (bf16[1024,1024]{1,0:T(8,128)(2,1)}, f32[1024,128]{1,0:T(8,128)}, bf16[1024,4096]{1,0:T(8,128)(2,1)}, bf16[8,256,512]{2,1,0:T(8,128)(2,1)}, ...) custom-call(s32[16]{0:T(128)} %pad_add_fusion.order_ref, ...), custom_call_target="tpu_custom_call" | custom-call | flops 16777216000 | bytes 20971520 | tf_op jit(solution)/shard_map/norm_and_terms/pallas_call | solution.py:123
  35.5 5.9 %collective-permute-done.got_ref = bf16[8,256,512]{2,1,0:T(8,128)(2,1)S(1)} collective-permute-done((bf16[8,256,512]{2,1,0:T(8,128)(2,1)}, bf16[8,256,512]{2,1,0:T(8,128)(2,1)S(1)}, u32[]{:S(2)}, u32[]{:S(2)}) %collective-permute-start) | collective-permute-done | bytes 2097184 | tf_op jit(solution)/shard_map/ppermute | solution.py:26
  42.8 4.4 %add_values.1 = (bf16[8,64,512]{2,1,0:T(8,128)(2,1)}, bf16[8,64,512]{2,1,0:T(8,128)(2,1)}, bf16[8,64,512]{2,1,0:T(8,128)(2,1)}, bf16[8,64,512]{2,1,0:T(8,128)(2,1)}) custom-call(s32[1]{0:T(128)} %bitcast.1.y_ref, bf16[8,256,512]{2,1,0:T(8,128)(2,1)} %get-tuple-element.38.own_ref, bf16[8,256,512]{2,1,0:T(8,128)(2,1)} %copy-done, ...), custom_call_target="tpu_custom_call" | custom-call | flops 1048576 | bytes 6291456 | tf_op jit(solution)/shard_map/add_values/pallas_call | solution.py:169
  47.2 4.7 %add_keys.1 = (bf16[4,256,512]{2,1,0:T(8,128)(2,1)}, bf16[4,256,512]{2,1,0:T(8,128)(2,1)}) custom-call(bf16[8,256,512]{2,1,0:T(8,128)(2,1)} %get-tuple-element.44.own_ref, bf16[8,256,512]{2,1,0:T(8,128)(2,1)} %collective-permute-done.4.got_ref, bf16[8,64,512]{2,1,0:T(8,128)(2,1)} %get-tuple-element.40.after_ref.v0), custom_call_target="tpu_custom_call" | custom-call | flops 1048576 | bytes 6291456 | tf_op jit(solution)/shard_map/add_keys/pallas_call | solution.py:193
  51.9 3.7 %collective-permute-start.5 = (bf16[4,256,512]{2,1,0:T(8,128)(2,1)}, bf16[4,256,512]{2,1,0:T(8,128)(2,1)S(1)}, u32[]{:S(2)}, u32[]{:S(2)}) collective-permute-start(bf16[4,256,512]{2,1,0:T(8,128)(2,1)} %get-tuple-element.47), channel_id=1, source_target_pairs={{0,16},{1,17},{2,18},{3,19},{4,20},{5,21},{6,22},{7,23},{8,24},{9,... | collective-permute-start | bytes 3145736 | tf_op jit(solution)/shard_map/ppermute | solution.py:26
  55.6 1.5 collective-permute-start.1
  57.1 2.9 %collective-permute-start.2 = (bf16[8,64,512]{2,1,0:T(8,128)(2,1)S(1)}, bf16[8,64,512]{2,1,0:T(8,128)(2,1)S(1)}, u32[]{:S(2)}, u32[]{:S(2)}) collective-permute-start(bf16[8,64,512]{2,1,0:T(8,128)(2,1)S(1)} %copy-done.18), channel_id=1, source_target_pairs={{0,4},{1,5},{2,6},{3,7},{4,0},{5,1},{6,2},{7,3},{8,12},{9,13},{10,... | collective-permute-start | bytes 1572872 | tf_op jit(solution)/shard_map/ppermute | solution.py:26
  60.0 1.4 collective-permute-start.3
  61.3 9.2 %collective-permute-done.1.v1 = bf16[8,64,512]{2,1,0:T(8,128)(2,1)S(1)} collective-permute-done((bf16[8,64,512]{2,1,0:T(8,128)(2,1)S(1)}, bf16[8,64,512]{2,1,0:T(8,128)(2,1)S(1)}, u32[]{:S(2)}, u32[]{:S(2)}) %collective-permute-start.1) | collective-permute-done | bytes 524320 | tf_op jit(solution)/shard_map/ppermute | solution.py:26
  70.6 12.3 %collective-permute-done.2.v2 = bf16[8,64,512]{2,1,0:T(8,128)(2,1)S(1)} collective-permute-done((bf16[8,64,512]{2,1,0:T(8,128)(2,1)S(1)}, bf16[8,64,512]{2,1,0:T(8,128)(2,1)S(1)}, u32[]{:S(2)}, u32[]{:S(2)}) %collective-permute-start.2) | collective-permute-done | bytes 524320 | tf_op jit(solution)/shard_map/ppermute | solution.py:26
  82.9 13.2 %collective-permute-done.5.k1 = bf16[4,256,512]{2,1,0:T(8,128)(2,1)S(1)} collective-permute-done((bf16[4,256,512]{2,1,0:T(8,128)(2,1)}, bf16[4,256,512]{2,1,0:T(8,128)(2,1)S(1)}, u32[]{:S(2)}, u32[]{:S(2)}) %collective-permute-start.5) | collective-permute-done | bytes 1048608 | tf_op jit(solution)/shard_map/ppermute | solution.py:26
  97.0 3.7 %join_first.1 = (f32[6,64,512]{2,1,0:T(8,128)}, bf16[6,64,512]{2,1,0:T(8,128)(2,1)}, bf16[6,64,512]{2,1,0:T(8,128)(2,1)}, bf16[6,64,512]{2,1,0:T(8,128)(2,1)}) custom-call(bf16[8,64,512]{2,1,0:T(8,128)(2,1)} %get-tuple-element.40.after_ref.v0, bf16[8,64,512]{2,1,0:T(8,128)(2,1)} %copy-done.3, bf16[8,64,512]{2,1,0:T(8,128)(2,1)} %copy-done.4, ...), custom_call_target="tpu_custom_call" | custom-call | flops 2097152 | bytes 4194304 | tf_op jit(solution)/shard_map/join_first/pallas_call | solution.py:309
  100.7 1.5 collective-permute-start.6
  103.4 2.1 %collective-permute-start.8 = (bf16[6,64,512]{2,1,0:T(8,128)(2,1)}, bf16[6,64,512]{2,1,0:T(8,128)(2,1)S(1)}, u32[]{:S(2)}, u32[]{:S(2)}) collective-permute-start(bf16[6,64,512]{2,1,0:T(8,128)(2,1)} %get-tuple-element.51), channel_id=1, source_target_pairs={{0,96},{1,97},{2,98},{3,99},{4,100},{5,101},{6,102},{7,103},{8,104... | collective-permute-start | bytes 1179656 | tf_op jit(solution)/shard_map/ppermute | solution.py:26
  105.4 7.5 %collective-permute-done.6.x1 = bf16[6,64,512]{2,1,0:T(8,128)(2,1)S(1)} collective-permute-done((bf16[6,64,512]{2,1,0:T(8,128)(2,1)}, bf16[6,64,512]{2,1,0:T(8,128)(2,1)S(1)}, u32[]{:S(2)}, u32[]{:S(2)}) %collective-permute-start.6) | collective-permute-done | bytes 393248 | tf_op jit(solution)/shard_map/ppermute | solution.py:26
  112.9 3.0 %collective-permute-done.7.x2 = bf16[6,64,512]{2,1,0:T(8,128)(2,1)S(1)} collective-permute-done((bf16[6,64,512]{2,1,0:T(8,128)(2,1)}, bf16[6,64,512]{2,1,0:T(8,128)(2,1)S(1)}, u32[]{:S(2)}, u32[]{:S(2)}) %collective-permute-start.7) | collective-permute-done | bytes 393248 | tf_op jit(solution)/shard_map/ppermute | solution.py:26
  115.9 6.5 %collective-permute-done.8.x3 = bf16[6,64,512]{2,1,0:T(8,128)(2,1)S(1)} collective-permute-done((bf16[6,64,512]{2,1,0:T(8,128)(2,1)}, bf16[6,64,512]{2,1,0:T(8,128)(2,1)S(1)}, u32[]{:S(2)}, u32[]{:S(2)}) %collective-permute-start.8) | collective-permute-done | bytes 393248 | tf_op jit(solution)/shard_map/ppermute | solution.py:26
  123.1 2.3 %join_x.1 = (f32[64,512]{1,0:T(8,128)}, f32[64,512]{1,0:T(8,128)}, bf16[64,512]{1,0:T(8,128)(2,1)}, bf16[64,512]{1,0:T(8,128)(2,1)}, bf16[64,512]{1,0:T(8,128)(2,1)}, /*index=5*/bf16[64,512]{1,0:T(8,128)(2,1)}) custom-call(s32[1]{0:T(128)} %bitcast.1.y_ref, f32[6,64,512]{2,1,0:T(8,128)} %get-tuple-element.48.own, bf16[6,64,512]{2,1,0:T(8,128)(2,1)} %copy-done.6, ...), custom_call_target="tpu_custom_call" | custom-call | flops 2097152 | bytes 4194304 | tf_op jit(solution)/shard_map/join_x/pallas_call | solution.py:309
  125.5 1.5 collective-permute-start.10
  126.9 2.7 %collective-permute-start.11 = (bf16[64,512]{1,0:T(8,128)(2,1)}, bf16[64,512]{1,0:T(8,128)(2,1)S(1)}, u32[]{:S(2)}, u32[]{:S(2)}) collective-permute-start(bf16[64,512]{1,0:T(8,128)(2,1)} %get-tuple-element.59), channel_id=1, source_target_pairs={{0,4},{1,5},{2,6},{3,7},{4,0},{5,1},{6,2},{7,3},{8,12},{9,13},{10,... | collective-permute-start | bytes 196616 | tf_op jit(solution)/shard_map/ppermute | solution.py:26
  129.6 1.5 collective-permute-start.12
  131.4 15.7 %forward.1 = (bf16[1024,512]{1,0:T(8,128)(2,1)}, bf16[1024,512]{1,0:T(8,128)(2,1)}, f32[1024,128]{1,0:T(8,128)}) custom-call(bf16[1024,4096]{1,0:T(8,128)(2,1)} %get-tuple-element.35.normed_ref, bf16[1024,1024]{1,0:T(8,128)(2,1)} %get-tuple-element.36.both_ref, f32[1024,128]{1,0:T(8,128)} %get-tuple-element.37.after_ref.inv_ref, ...), custom_call_target="tpu_custom_call" | custom-call | flops 8589934592 | bytes 20971520 | tf_op jit(solution)/shard_map/forward/pallas_call | solution.py:238
  147.8 1.8 join_zy.1.refs_0_
  149.5 1.4 collective-permute-start.13
  152.3 2.5 %collective-permute-done.13.refs_1_ = bf16[2,64,512]{2,1,0:T(8,128)(2,1)S(1)} collective-permute-done((bf16[2,64,512]{2,1,0:T(8,128)(2,1)}, bf16[2,64,512]{2,1,0:T(8,128)(2,1)S(1)}, u32[]{:S(2)}, u32[]{:S(2)}) %collective-permute-start.13) | collective-permute-done | bytes 131104 | tf_op jit(solution)/shard_map/ppermute | solution.py:26
  155.4 1.7 join_zl.1.after_ref.p0_ref
  157.0 2.6 %collective-permute-start.15 = (bf16[2,64,512]{2,1,0:T(8,128)(2,1)}, bf16[2,64,512]{2,1,0:T(8,128)(2,1)S(1)}, u32[]{:S(2)}, u32[]{:S(2)}) collective-permute-start(bf16[2,64,512]{2,1,0:T(8,128)(2,1)} %join_zl.1.after_ref.p0_ref), channel_id=1, source_target_pairs={{0,4},{1,5},{2,6},{3,7},{4,0},{5,1},{6,2},{7,3},{8,12},{9,13},{10,... | collective-permute-start | bytes 393224 | tf_op jit(solution)/shard_map/ppermute | solution.py:26
  159.7 9.5 %backward.2.after_ref.refs_0_ = bf16[1024,4096]{1,0:T(8,128)(2,1)} custom-call(bf16[1024,4096]{1,0:T(8,128)(2,1)} %tok_ref.5, bf16[1024,1024]{1,0:T(8,128)(2,1)} %get-tuple-element.36.both_ref, f32[1024,128]{1,0:T(8,128)} %get-tuple-element.37.after_ref.inv_ref, f32[1024,128]{1,0:T(8,128)} %get-tuple-element.55.after_ref.coef_ref, f32[1,4096]{1,0:T(1,128)} %bitcast.6, ...), custom_call_target="tpu_custom_call" | custom-call | flops 4294967296 | bytes 12582912 | tf_op jit(solution)/shard_map/backward/pallas_call | solution.py:285
  170.0 2.3 %finish.1 = (f32[256,512]{1,0:T(8,128)}, f32[256,512]{1,0:T(8,128)}, f32[16,256]{1,0:T(8,128)}) custom-call(s32[1]{0:T(128)} %bitcast.1.y_ref, bf16[2,64,512]{2,1,0:T(8,128)(2,1)} %join_zl.1.after_ref.p0_ref, bf16[2,64,512]{2,1,0:T(8,128)(2,1)} %copy-done.11, bf16[2,64,512]{2,1,0:T(8,128)(2,1)} %copy-done.10, bf16[2,64,512]{2,1,0:T(8,128)(2,1)} %copy-done.9, ...), custom_call_target="tpu_custom_call" | custom-call | flops 524288 | bytes 1048576 | tf_op jit(solution)/shard_map/finish/pallas_call | solution.py:367
  172.3 1.3 copy.15
  173.6 7.3 %all-to-all-start = ((f32[16,1,256]{2,1,0:T(1,128)}), f32[16,1,256]{2,1,0:T(1,128)S(1)}, u32[]{:S(2)}, u32[]{:S(2)}) async-start(f32[16,1,256]{2,1,0:T(1,128)} %copy.15), calls=%async_computation | async-start | bytes 32768 | tf_op jit(solution)/shard_map/all_to_all | solution.py:436
  180.9 9.6 %backward.3 = bf16[1024,4096]{1,0:T(8,128)(2,1)} custom-call(bf16[1024,4096]{1,0:T(8,128)(2,1)} %tok_ref.5, bf16[1024,1024]{1,0:T(8,128)(2,1)} %get-tuple-element.36.both_ref, f32[1024,128]{1,0:T(8,128)} %get-tuple-element.37.after_ref.inv_ref, f32[1024,128]{1,0:T(8,128)} %get-tuple-element.55.after_ref.coef_ref, ...), custom_call_target="tpu_custom_call", output_to_operand_aliasing={{}: (7, {})} | custom-call | flops 4294967296 | bytes 12582912 | tf_op jit(solution)/shard_map/backward/pallas_call | solution.py:285
  (69 shorter events, 12.7 us)
Async XLA Ops:
  7.2 124.2 %all-gather.2.cloned.1.call-start = ((), (), s32[]{:S(2)}) async-start(), calls=%async_computation.1 | async-start | bytes 8912896 | tf_op jit(solution)/shard_map/all_gather | solution.py:394
  9.2 0.8 copy-start.1
  34.9 6.5 %collective-permute-start = (bf16[8,256,512]{2,1,0:T(8,128)(2,1)}, bf16[8,256,512]{2,1,0:T(8,128)(2,1)S(1)}, u32[]{:S(2)}, u32[]{:S(2)}) collective-permute-start(bf16[8,256,512]{2,1,0:T(8,128)(2,1)} %get-tuple-element.39), channel_id=1, source_target_pairs={{0,8},{1,9},{2,10},{3,11},{4,12},{5,13},{6,14},{7,15},{8,0},{9,1},... | collective-permute-start | bytes 6291464 | tf_op jit(solution)/shard_map/ppermute | solution.py:26
  35.0 12.2 %collective-permute-start.4 = (bf16[8,256,512]{2,1,0:T(8,128)(2,1)}, bf16[8,256,512]{2,1,0:T(8,128)(2,1)}, u32[]{:S(2)}, u32[]{:S(2)}) collective-permute-start(bf16[8,256,512]{2,1,0:T(8,128)(2,1)} %get-tuple-element.45), channel_id=1, source_target_pairs={{0,8},{1,9},{2,10},{3,11},{4,12},{5,13},{6,14},{7,15},{8,0},{9,1},... | collective-permute-start | bytes 6291464 | tf_op jit(solution)/shard_map/ppermute | solution.py:26
  41.4 1.3 copy-start
  47.2 8.4 %copy-start.19 = (bf16[8,64,512]{2,1,0:T(8,128)(2,1)S(1)}, bf16[8,64,512]{2,1,0:T(8,128)(2,1)}, u32[]{:S(2)}) copy-start(bf16[8,64,512]{2,1,0:T(8,128)(2,1)} %get-tuple-element.41) | copy-start | bytes 1572868
  47.2 9.9 %copy-start.18 = (bf16[8,64,512]{2,1,0:T(8,128)(2,1)S(1)}, bf16[8,64,512]{2,1,0:T(8,128)(2,1)}, u32[]{:S(2)}) copy-start(bf16[8,64,512]{2,1,0:T(8,128)(2,1)} %get-tuple-element.42) | copy-start | bytes 1572868
  47.2 12.7 %copy-start.17 = (bf16[8,64,512]{2,1,0:T(8,128)(2,1)S(1)}, bf16[8,64,512]{2,1,0:T(8,128)(2,1)}, u32[]{:S(2)}) copy-start(bf16[8,64,512]{2,1,0:T(8,128)(2,1)} %get-tuple-element.43) | copy-start | bytes 1572868
  51.9 44.2 %collective-permute-start.5 = (bf16[4,256,512]{2,1,0:T(8,128)(2,1)}, bf16[4,256,512]{2,1,0:T(8,128)(2,1)S(1)}, u32[]{:S(2)}, u32[]{:S(2)}) collective-permute-start(bf16[4,256,512]{2,1,0:T(8,128)(2,1)} %get-tuple-element.47), channel_id=1, source_target_pairs={{0,16},{1,17},{2,18},{3,19},{4,20},{5,21},{6,22},{7,23},{8,24},{9,... | collective-permute-start | bytes 3145736 | tf_op jit(solution)/shard_map/ppermute | solution.py:26
  55.6 15.0 %collective-permute-start.1 = (bf16[8,64,512]{2,1,0:T(8,128)(2,1)S(1)}, bf16[8,64,512]{2,1,0:T(8,128)(2,1)S(1)}, u32[]{:S(2)}, u32[]{:S(2)}) collective-permute-start(bf16[8,64,512]{2,1,0:T(8,128)(2,1)S(1)} %copy-done.19), channel_id=1, source_target_pairs={{0,2},{1,3},{2,4},{3,5},{4,6},{5,7},{6,0},{7,1},{8,10},{9,11},{10,... | collective-permute-start | bytes 1572872 | tf_op jit(solution)/shard_map/ppermute | solution.py:26
  57.1 25.8 %collective-permute-start.2 = (bf16[8,64,512]{2,1,0:T(8,128)(2,1)S(1)}, bf16[8,64,512]{2,1,0:T(8,128)(2,1)S(1)}, u32[]{:S(2)}, u32[]{:S(2)}) collective-permute-start(bf16[8,64,512]{2,1,0:T(8,128)(2,1)S(1)} %copy-done.18), channel_id=1, source_target_pairs={{0,4},{1,5},{2,6},{3,7},{4,0},{5,1},{6,2},{7,3},{8,12},{9,13},{10,... | collective-permute-start | bytes 1572872 | tf_op jit(solution)/shard_map/ppermute | solution.py:26
  60.0 22.9 %collective-permute-start.3 = (bf16[8,64,512]{2,1,0:T(8,128)(2,1)S(1)}, bf16[8,64,512]{2,1,0:T(8,128)(2,1)S(1)}, u32[]{:S(2)}, u32[]{:S(2)}) collective-permute-start(bf16[8,64,512]{2,1,0:T(8,128)(2,1)S(1)} %copy-done.17), channel_id=1, source_target_pairs={{0,6},{1,7},{2,0},{3,1},{4,2},{5,3},{6,4},{7,5},{8,14},{9,15},{10,... | collective-permute-start | bytes 1572872 | tf_op jit(solution)/shard_map/ppermute | solution.py:26
  70.5 25.5 %copy-start.3 = (bf16[8,64,512]{2,1,0:T(8,128)(2,1)}, bf16[8,64,512]{2,1,0:T(8,128)(2,1)S(1)}, u32[]{:S(2)}) copy-start(bf16[8,64,512]{2,1,0:T(8,128)(2,1)S(1)} %collective-permute-done.1.v1) | copy-start | bytes 1572868
  82.9 13.2 %copy-start.4 = (bf16[8,64,512]{2,1,0:T(8,128)(2,1)}, bf16[8,64,512]{2,1,0:T(8,128)(2,1)S(1)}, u32[]{:S(2)}) copy-start(bf16[8,64,512]{2,1,0:T(8,128)(2,1)S(1)} %collective-permute-done.2.v2) | copy-start | bytes 1572868
  82.9 13.2 %copy-start.5 = (bf16[8,64,512]{2,1,0:T(8,128)(2,1)}, bf16[8,64,512]{2,1,0:T(8,128)(2,1)S(1)}, u32[]{:S(2)}) copy-start(bf16[8,64,512]{2,1,0:T(8,128)(2,1)S(1)} %collective-permute-done.3.v3) | copy-start | bytes 1572868
  96.1 1.0 copy-start.2
  100.7 12.2 %collective-permute-start.6 = (bf16[6,64,512]{2,1,0:T(8,128)(2,1)}, bf16[6,64,512]{2,1,0:T(8,128)(2,1)S(1)}, u32[]{:S(2)}, u32[]{:S(2)}) collective-permute-start(bf16[6,64,512]{2,1,0:T(8,128)(2,1)} %get-tuple-element.49), channel_id=1, source_target_pairs={{0,32},{1,33},{2,34},{3,35},{4,36},{5,37},{6,38},{7,39},{8,40},{9,... | collective-permute-start | bytes 1179656 | tf_op jit(solution)/shard_map/ppermute | solution.py:26
  102.2 13.7 %collective-permute-start.7 = (bf16[6,64,512]{2,1,0:T(8,128)(2,1)}, bf16[6,64,512]{2,1,0:T(8,128)(2,1)S(1)}, u32[]{:S(2)}, u32[]{:S(2)}) collective-permute-start(bf16[6,64,512]{2,1,0:T(8,128)(2,1)} %get-tuple-element.50), channel_id=1, source_target_pairs={{0,64},{1,65},{2,66},{3,67},{4,68},{5,69},{6,70},{7,71},{8,72},{9,... | collective-permute-start | bytes 1179656 | tf_op jit(solution)/shard_map/ppermute | solution.py:26
  103.4 19.0 %collective-permute-start.8 = (bf16[6,64,512]{2,1,0:T(8,128)(2,1)}, bf16[6,64,512]{2,1,0:T(8,128)(2,1)S(1)}, u32[]{:S(2)}, u32[]{:S(2)}) collective-permute-start(bf16[6,64,512]{2,1,0:T(8,128)(2,1)} %get-tuple-element.51), channel_id=1, source_target_pairs={{0,96},{1,97},{2,98},{3,99},{4,100},{5,101},{6,102},{7,103},{8,104... | collective-permute-start | bytes 1179656 | tf_op jit(solution)/shard_map/ppermute | solution.py:26
  112.9 9.5 %copy-start.6 = (bf16[6,64,512]{2,1,0:T(8,128)(2,1)}, bf16[6,64,512]{2,1,0:T(8,128)(2,1)S(1)}, u32[]{:S(2)}) copy-start(bf16[6,64,512]{2,1,0:T(8,128)(2,1)S(1)} %collective-permute-done.6.x1) | copy-start | bytes 1179652
  115.9 6.5 %copy-start.7 = (bf16[6,64,512]{2,1,0:T(8,128)(2,1)}, bf16[6,64,512]{2,1,0:T(8,128)(2,1)S(1)}, u32[]{:S(2)}) copy-start(bf16[6,64,512]{2,1,0:T(8,128)(2,1)S(1)} %collective-permute-done.7.x2) | copy-start | bytes 1179652
  122.4 0.7 copy-start.8
  125.5 21.6 %collective-permute-start.10 = (bf16[64,512]{1,0:T(8,128)(2,1)}, bf16[64,512]{1,0:T(8,128)(2,1)S(1)}, u32[]{:S(2)}, u32[]{:S(2)}) collective-permute-start(bf16[64,512]{1,0:T(8,128)(2,1)} %get-tuple-element.58), channel_id=1, source_target_pairs={{0,2},{1,3},{2,4},{3,5},{4,6},{5,7},{6,0},{7,1},{8,10},{9,11},{10,... | collective-permute-start | bytes 196616 | tf_op jit(solution)/shard_map/ppermute | solution.py:26
  126.9 20.2 %collective-permute-start.11 = (bf16[64,512]{1,0:T(8,128)(2,1)}, bf16[64,512]{1,0:T(8,128)(2,1)S(1)}, u32[]{:S(2)}, u32[]{:S(2)}) collective-permute-start(bf16[64,512]{1,0:T(8,128)(2,1)} %get-tuple-element.59), channel_id=1, source_target_pairs={{0,4},{1,5},{2,6},{3,7},{4,0},{5,1},{6,2},{7,3},{8,12},{9,13},{10,... | collective-permute-start | bytes 196616 | tf_op jit(solution)/shard_map/ppermute | solution.py:26
  129.6 17.5 %collective-permute-start.12 = (bf16[64,512]{1,0:T(8,128)(2,1)}, bf16[64,512]{1,0:T(8,128)(2,1)S(1)}, u32[]{:S(2)}, u32[]{:S(2)}) collective-permute-start(bf16[64,512]{1,0:T(8,128)(2,1)} %get-tuple-element.60), channel_id=1, source_target_pairs={{0,6},{1,7},{2,0},{3,1},{4,2},{5,3},{6,4},{7,5},{8,14},{9,15},{10,... | collective-permute-start | bytes 196616 | tf_op jit(solution)/shard_map/ppermute | solution.py:26
  131.1 16.1 %collective-permute-start.9 = (bf16[64,512]{1,0:T(8,128)(2,1)}, bf16[64,512]{1,0:T(8,128)(2,1)S(1)}, u32[]{:S(2)}, u32[]{:S(2)}) collective-permute-start(bf16[64,512]{1,0:T(8,128)(2,1)} %get-tuple-element.52.after_ref), channel_id=1, source_target_pairs={{0,16},{1,17},{2,18},{3,19},{4,20},{5,21},{6,22},{7,23},{8,24},{9,... | collective-permute-start | bytes 196616 | tf_op jit(solution)/shard_map/ppermute | solution.py:26
  149.5 5.2 %collective-permute-start.13 = (bf16[2,64,512]{2,1,0:T(8,128)(2,1)}, bf16[2,64,512]{2,1,0:T(8,128)(2,1)S(1)}, u32[]{:S(2)}, u32[]{:S(2)}) collective-permute-start(bf16[2,64,512]{2,1,0:T(8,128)(2,1)} %join_zy.1.refs_0_), channel_id=1, source_target_pairs={{0,1},{1,0},{2,3},{3,2},{4,5},{5,4},{6,7},{7,6},{8,9},{9,8},{10,11... | collective-permute-start | bytes 393224 | tf_op jit(solution)/shard_map/ppermute | solution.py:26
  157.0 12.2 %collective-permute-start.16 = (bf16[2,64,512]{2,1,0:T(8,128)(2,1)}, bf16[2,64,512]{2,1,0:T(8,128)(2,1)S(1)}, u32[]{:S(2)}, u32[]{:S(2)}) collective-permute-start(bf16[2,64,512]{2,1,0:T(8,128)(2,1)} %join_zl.1.after_ref.p0_ref), channel_id=1, source_target_pairs={{0,6},{1,7},{2,0},{3,1},{4,2},{5,3},{6,4},{7,5},{8,14},{9,15},{10,... | collective-permute-start | bytes 393224 | tf_op jit(solution)/shard_map/ppermute | solution.py:26
  157.0 12.2 %collective-permute-start.15 = (bf16[2,64,512]{2,1,0:T(8,128)(2,1)}, bf16[2,64,512]{2,1,0:T(8,128)(2,1)S(1)}, u32[]{:S(2)}, u32[]{:S(2)}) collective-permute-start(bf16[2,64,512]{2,1,0:T(8,128)(2,1)} %join_zl.1.after_ref.p0_ref), channel_id=1, source_target_pairs={{0,4},{1,5},{2,6},{3,7},{4,0},{5,1},{6,2},{7,3},{8,12},{9,13},{10,... | collective-permute-start | bytes 393224 | tf_op jit(solution)/shard_map/ppermute | solution.py:26
  159.7 9.6 %collective-permute-start.14 = (bf16[2,64,512]{2,1,0:T(8,128)(2,1)}, bf16[2,64,512]{2,1,0:T(8,128)(2,1)S(1)}, u32[]{:S(2)}, u32[]{:S(2)}) collective-permute-start(bf16[2,64,512]{2,1,0:T(8,128)(2,1)} %join_zl.1.after_ref.p0_ref), channel_id=1, source_target_pairs={{0,2},{1,3},{2,4},{3,5},{4,6},{5,7},{6,0},{7,1},{8,10},{9,11},{10,... | collective-permute-start | bytes 393224 | tf_op jit(solution)/shard_map/ppermute | solution.py:26
  169.3 0.7 copy-start.11
  173.6 16.8 %all-to-all-start = ((f32[16,1,256]{2,1,0:T(1,128)}), f32[16,1,256]{2,1,0:T(1,128)S(1)}, u32[]{:S(2)}, u32[]{:S(2)}) async-start(f32[16,1,256]{2,1,0:T(1,128)} %copy.15), calls=%async_computation | async-start | bytes 32768 | tf_op jit(solution)/shard_map/all_to_all | solution.py:436
  (7 other events, 4.5 us)
Sparse Core Ops, SparseCore 0:
  11.0 90.2 all-gather.1

commit v3 on v2

v3 whole, which is shorter than its diff:
```python
import math

import jax
import jax.numpy as jnp
import numpy as np
from jax import lax
from jax.experimental import pallas as pl
from jax.experimental.pallas import tpu as pltpu
from jax.sharding import Mesh, PartitionSpec as P

HEAD = 128
AXES = ("x", "zh", "c", "y", "zl")
SIZES = (4, 2, 2, 4, 2)
F32 = jnp.float32
BF16 = jnp.bfloat16
MIB = 1 << 20


def send(value, move):
    pairs = []
    for i in range(math.prod(SIZES)):
        x, zh, c, y, zl = (int(v) for v in np.unravel_index(i, SIZES))
        x, y, z, c = move(x, y, zh * 2 + zl, c)
        x, y, z, c = x % 4, y % 4, z % 4, c % 2
        pairs.append((i, int(np.ravel_multi_index((x, z // 2, c, y, z % 2), SIZES))))
    return lax.ppermute(value, AXES, pairs)


def to_core(value):
    return send(value, lambda x, y, z, c: (x, y, z, c + 1))


def params(mib, **more):
    return pltpu.CompilerParams(vmem_limit_bytes=mib * MIB, **more)


def turn(values, cosine, sine, direction):
    parts = []
    for h in range(values.shape[1] // HEAD):
        v = values[:, h * HEAD : (h + 1) * HEAD]
        parts.append(v * cosine + direction * (pltpu.roll(v, HEAD // 2, 1) * sine))
    return jnp.concatenate(parts, axis=1)


RESIDENT = pl.BlockSpec(memory_space=pltpu.VMEM)
UNREAD = pl.BlockSpec(memory_space=pl.ANY)


def in_hbm(value):
    return pltpu.with_memory_space_constraint(value, pltpu.HBM)


COLUMNS = (((0,), (0,)), ((), ()))


def norm_kernel(
    order_ref, tok_ref, gain_ref, kc_ref, vc_ref, cos_ref, sin_ref, after_ref,
    both_out_ref, inv_ref, stored_ref, t0_ref, t1_ref, t2_ref, t3_ref, normed_ref, both_ref, done,
):
    i = pl.program_id(0)
    tb, feats = kc_ref.shape
    store = pltpu.make_async_copy(normed_ref, stored_ref, done)

    @pl.when(i < 4)
    def _():
        def rows(r, carry):
            at = pl.ds(pl.multiple_of(r * 16, 16), 16)
            v = tok_ref[at, :].astype(F32)
            inv = lax.rsqrt(jnp.mean(v * v, axis=1, keepdims=True) + 1e-05)
            inv_ref[at, :] = jnp.broadcast_to(inv, (16, HEAD))
            to = pl.ds(pl.multiple_of(i * tb + r * 16, 16), 16)
            normed_ref[to, :] = (tok_ref[at, :].astype(F32) * inv * gain_ref[...]).astype(BF16)
            return carry

        lax.fori_loop(0, tb // 16, rows, 0, unroll=2)
        here = pl.ds(pl.multiple_of(i * tb, tb), tb)
        back = turn(kc_ref[...].astype(F32), cos_ref[...], sin_ref[...], -1.0).astype(BF16)
        both_ref[here, :feats] = back
        both_ref[here, feats:] = vc_ref[...]
        both_out_ref[:, :feats] = back
        both_out_ref[:, feats:] = vc_ref[...]

    @pl.when(i == 4)
    def _():
        store.start()

    def part(p, terms_ref):
        for j in range(2):
            columns = pl.ds(pl.multiple_of(order_ref[p * 2 + j] * 256, 256), 256)
            term = lax.dot_general(normed_ref[:, columns], both_ref[...], COLUMNS, preferred_element_type=F32)
            terms_ref[j] = term.astype(BF16)

    for p, terms_ref in enumerate((t0_ref, t1_ref, t2_ref, t3_ref)):
        pl.when(i == 4 + p)(lambda p=p, terms_ref=terms_ref: part(p, terms_ref))

    @pl.when(i == 7)
    def _():
        store.wait()


def norm_and_terms(order, tokens, gain, key_cot, value_cot, cosine, sine, after):
    rows, width = tokens.shape
    feats = key_cot.shape[1]
    tb = rows // 4
    by_rows = lambda n: pl.BlockSpec((tb, n), lambda i, order: (jnp.minimum(i, 3), 0))
    return pl.pallas_call(
        norm_kernel,
        grid_spec=pltpu.PrefetchScalarGridSpec(
            num_scalar_prefetch=1,
            grid=(8,),
            in_specs=[
                by_rows(width),
                pl.BlockSpec((1, width), lambda i, order: (0, 0)),
                by_rows(feats),
                by_rows(feats),
                by_rows(HEAD),
                by_rows(HEAD),
                UNREAD,
            ],
            out_specs=[
                by_rows(2 * feats),
                by_rows(HEAD),
                pl.BlockSpec(memory_space=pltpu.HBM),
            ]
            + [pl.BlockSpec((2, 256, 2 * feats), lambda i, order: (0, 0, 0))] * 4,
            scratch_shapes=[
                pltpu.VMEM((rows, width), BF16),
                pltpu.VMEM((rows, 2 * feats), BF16),
                pltpu.SemaphoreType.DMA,
            ],
        ),
        out_shape=[
            pltpu.HBM((rows, 2 * feats), BF16),
            pltpu.HBM((rows, HEAD), F32),
            pltpu.HBM((rows, width), BF16),
        ]
        + [pltpu.HBM((2, 256, 2 * feats), BF16)] * 4,
        compiler_params=params(56),
        cost_estimate=pl.CostEstimate(flops=10000 * MIB, bytes_accessed=20 * MIB, transcendentals=0),
        name="norm_and_terms",
    )(order, in_hbm(tokens), gain, in_hbm(key_cot), in_hbm(value_cot), cosine, sine, in_hbm(after))


def own_kernel(order_ref, n0_ref, n1_ref, both_ref, terms_ref):
    for j, n_ref in enumerate((n0_ref, n1_ref)):
        term = lax.dot_general(n_ref[...], both_ref[...], COLUMNS, preferred_element_type=F32)
        terms_ref[j] = term.astype(BF16)


def own_terms(order, normed, both):
    rows, feats = both.shape
    block = lambda j: pl.BlockSpec((rows, 256), lambda g, order: (0, order[2 * g + j]))
    return pl.pallas_call(
        own_kernel,
        grid_spec=pltpu.PrefetchScalarGridSpec(
            num_scalar_prefetch=1,
            grid=(4,),
            in_specs=[block(0), block(1), pl.BlockSpec((rows, feats), lambda g, order: (0, 0))],
            out_specs=pl.BlockSpec((2, 256, feats), lambda g, order: (g, 0, 0)),
        ),
        out_shape=pltpu.HBM((8, 256, feats), BF16),
        compiler_params=params(56),
        cost_estimate=pl.CostEstimate(flops=0, bytes_accessed=0, transcendentals=0),
        name="own_terms",
    )(order, in_hbm(normed), in_hbm(normed), in_hbm(both))


def add_kernel(own_ref, *refs):
    got_refs, out_ref = refs[:4], refs[-1]
    for p, got_ref in enumerate(got_refs):

        @pl.when(pl.program_id(0) == p)
        def _():
            out_ref[...] = (own_ref[...].astype(F32) + got_ref[...].astype(F32)).astype(BF16)


def add(own, got, after):
    block = pl.BlockSpec((2, *own.shape[1:]), lambda g: (g, 0, 0))
    fixed = pl.BlockSpec((2, *own.shape[1:]), lambda g: (0, 0, 0))
    return pl.pallas_call(
        add_kernel,
        grid=(4,),
        in_specs=[block] + [fixed] * 4 + [UNREAD],
        out_specs=block,
        out_shape=pltpu.HBM(own.shape, BF16),
        compiler_params=params(56),
        cost_estimate=pl.CostEstimate(flops=0, bytes_accessed=0, transcendentals=0),
        name="add",
    )(in_hbm(own), *(in_hbm(g) for g in got), in_hbm(after))


def pick_kernel(half_ref, value_ref, after_ref, same_ref, half_out_ref, done):
    rows = half_out_ref.shape[0]
    copy = pltpu.make_async_copy(value_ref.at[pl.ds(half_ref[0] * rows, rows)], half_out_ref, done)
    copy.start()
    copy.wait()


def pick(half, value, after):
    return pl.pallas_call(
        pick_kernel,
        in_specs=[pl.BlockSpec(memory_space=pltpu.SMEM), UNREAD, UNREAD],
        out_specs=[pl.BlockSpec(memory_space=pltpu.HBM)] * 2,
        out_shape=[pltpu.HBM(value.shape, BF16), pltpu.HBM((value.shape[0] // 2, *value.shape[1:]), BF16)],
        scratch_shapes=[pltpu.SemaphoreType.DMA],
        input_output_aliases={1: 0},
        cost_estimate=pl.CostEstimate(flops=0, bytes_accessed=2 * MIB, transcendentals=0),
        name="pick",
    )(half.reshape(1), in_hbm(value), in_hbm(after))


def forward_kernel(
    place_ref, normed_ref, both_ref, inv_ref, cos_ref, sin_ref, *refs
):
    w_refs, (key_ref, value_ref, coef_ref, held_ref, done) = refs[:6], refs[7:]
    feats = key_ref.shape[1]
    zh, core, zl = place_ref[0], place_ref[1], place_ref[2]
    first_step = pl.program_id(0) == 0
    copies = []
    for p, w_ref in enumerate(w_refs):
        c = lax.rem(core + p % 2, 2)
        if p < 2:
            to = held_ref.at[:, zh, c]
        else:
            to = held_ref.at[pl.ds(2 * lax.rem(zl + p // 2 - 1, 2), 2), 1 - zh, c]
        copies.append(pltpu.make_async_copy(w_ref, to, done.at[p]))

    @pl.when(first_step)
    def _():
        for copy in copies:
            copy.start()

    pre = None
    for z in range(2):
        for copy in copies[:2] if z == 0 else copies[2:]:
            pl.when(first_step)(copy.wait)
        at = lax.rem(zh + z, 2)
        for x in range(4):
            columns = pl.ds(pl.multiple_of(x * 1024 + at * 512, 512), 512)
            w = held_ref[x, at].reshape(512, 2 * feats)
            term = jnp.dot(normed_ref[:, columns], w, preferred_element_type=F32)
            pre = term if pre is None else pre + term
    key_pre, value_pre = pre[:, :feats], pre[:, feats:]
    key_ref[...] = turn(key_pre, cos_ref[...], sin_ref[...], 1.0).astype(BF16)
    value_ref[...] = value_pre.astype(BF16)
    inner = jnp.sum(
        key_pre * both_ref[:, :feats].astype(F32) + value_pre * both_ref[:, feats:].astype(F32), axis=1, keepdims=True
    )
    inv = inv_ref[...]
    coef_ref[...] = inv * inv * (inner * (1.0 / normed_ref.shape[1]))


def forward(place, normed, both, inv, cosine, sine, weights, after):
    rows, width = normed.shape
    feats = both.shape[1] // 2
    tb = 256
    by_rows = lambda n: pl.BlockSpec((tb, n), lambda i, place: (i, 0))
    return pl.pallas_call(
        forward_kernel,
        grid_spec=pltpu.PrefetchScalarGridSpec(
            num_scalar_prefetch=1,
            grid=(rows // tb,),
            in_specs=[by_rows(width), by_rows(2 * feats), by_rows(HEAD), by_rows(HEAD), by_rows(HEAD)] + [UNREAD] * 7,
            out_specs=[by_rows(feats), by_rows(feats), by_rows(HEAD)],
            scratch_shapes=[pltpu.VMEM((4, 2, 2, 256, 2 * feats), BF16), pltpu.SemaphoreType.DMA((6,))],
        ),
        out_shape=[
            pltpu.HBM((rows, feats), BF16),
            pltpu.HBM((rows, feats), BF16),
            pltpu.HBM((rows, HEAD), F32),
        ],
        compiler_params=params(56),
        cost_estimate=pl.CostEstimate(flops=4 * rows * width * feats, bytes_accessed=20 * MIB, transcendentals=0),
        name="forward",
    )(place, in_hbm(normed), in_hbm(both), in_hbm(inv), cosine, sine, *(in_hbm(w) for w in weights), in_hbm(after))


def backward_kernel(place_ref, tok_ref, both_ref, inv_ref, coef_ref, gain_ref, *refs):
    w_refs, out_ref = refs[:6], refs[6]

    def part(pair):
        for c, w_ref in enumerate(pair):
            s = pl.ds(pl.multiple_of(lax.rem(place_ref[8] + c, 2) * 256, 256), 256)
            grad = lax.dot_general(both_ref[...], w_ref[0], (((1,), (1,)), ((), ())), preferred_element_type=F32)
            out = inv_ref[:, :1] * (grad * gain_ref[:, s]) - tok_ref[:, s].astype(F32) * coef_ref[:, :1]
            out_ref[:, s] = out.astype(BF16)

    i = pl.program_id(0)
    pl.when(i < 4)(lambda: part(w_refs[:2]))
    pl.when((i >= 4) & (i < 6))(lambda: part(w_refs[2:4]))
    pl.when(i >= 6)(lambda: part(w_refs[4:]))


def backward(place, tokens, both, inv, coef, gain, weights):
    rows, width = tokens.shape
    feats = both.shape[1] // 2
    cb = 512
    whole = lambda n: pl.BlockSpec((rows, n), lambda i, place: (0, 0))
    columns = pl.BlockSpec((rows, cb), lambda i, place: (0, place[i]))
    block = lambda first, size: pl.BlockSpec(
        (1, 256, 2 * feats), lambda i, place: (jnp.clip(i - first, 0, size - 1), 0, 0)
    )
    return pl.pallas_call(
        backward_kernel,
        grid_spec=pltpu.PrefetchScalarGridSpec(
            num_scalar_prefetch=1,
            grid=(width // cb,),
            in_specs=[
                columns,
                whole(2 * feats),
                whole(HEAD),
                whole(HEAD),
                pl.BlockSpec((1, cb), lambda i, place: (0, place[i])),
                block(0, 4),
                block(0, 4),
                block(4, 2),
                block(4, 2),
                block(6, 2),
                block(6, 2),
            ],
            out_specs=columns,
        ),
        out_shape=pltpu.HBM((rows, width), BF16),
        compiler_params=params(56),
        cost_estimate=pl.CostEstimate(flops=4 * rows * width * feats, bytes_accessed=28 * MIB, transcendentals=0),
        name="backward",
    )(place, in_hbm(tokens), in_hbm(both), in_hbm(inv), in_hbm(coef), gain, *(in_hbm(w) for w in weights))


def total_kernel(count, got_ref, kw_ref, vw_ref, gain_ref, after_ref, out_ref, gain_out_ref, sum_ref):
    g = pl.program_id(0)
    feats = kw_ref.shape[1]
    part = got_ref[0].astype(F32)
    for j in range(1, got_ref.shape[0]):
        part += got_ref[j].astype(F32)

    @pl.when(g == 0)
    def _():
        sum_ref[...] = part

    @pl.when(g > 0)
    def _():
        sum_ref[...] += part

    @pl.when(g == pl.num_programs(0) - 1)
    def _():
        mean = sum_ref[...] * (1.0 / count)
        out_ref[...] = jnp.broadcast_to(mean.astype(BF16)[None], out_ref.shape)
        products = mean[:, :feats] * kw_ref[...].astype(F32) + mean[:, feats:] * vw_ref[...].astype(F32)
        sums = jnp.broadcast_to(jnp.sum(products, axis=1, keepdims=True), (products.shape[0], HEAD)).T
        line = jnp.concatenate([sums[:1]] * (HEAD // sums.shape[1]), axis=1) / gain_ref[...]
        gain_out_ref[...] = jnp.broadcast_to(line, gain_out_ref.shape)


def total(count, got, key_rows, value_rows, gain_rows, after):
    sources, rows, width = got.shape
    feats = key_rows.shape[1]
    fixed = lambda shape: pl.BlockSpec(shape, lambda g: (0,) * len(shape))
    return pl.pallas_call(
        lambda *refs: total_kernel(count, *refs),
        grid=(4,),
        in_specs=[
            pl.BlockSpec((sources // 4, rows, width), lambda g: (g, 0, 0)),
            fixed((rows, feats)),
            fixed((rows, feats)),
            fixed((1, HEAD)),
            UNREAD,
        ],
        out_specs=[fixed((8, rows, width)), fixed((count, HEAD))],
        out_shape=[pltpu.HBM((8, rows, width), BF16), pltpu.HBM((count, HEAD), F32)],
        scratch_shapes=[pltpu.VMEM((rows, width), F32)],
        compiler_params=params(56),
        cost_estimate=pl.CostEstimate(flops=2 * MIB, bytes_accessed=5 * MIB, transcendentals=0),
        name="total",
    )(in_hbm(got), key_rows, value_rows, gain_rows, in_hbm(after))


def finish_kernel(got_ref, key_ref, value_ref):
    feats = key_ref.shape[1]
    rows = got_ref[...].reshape(key_ref.shape[0], 2 * feats).astype(F32)
    key_ref[...] = rows[:, :feats]
    value_ref[...] = rows[:, feats:]


def finish(got):
    pieces, rows, width = got.shape
    vmem = pl.BlockSpec(memory_space=pltpu.VMEM)
    return pl.pallas_call(
        finish_kernel,
        in_specs=[vmem],
        out_specs=[vmem] * 2,
        out_shape=[pltpu.HBM((pieces * rows, width // 2), F32)] * 2,
        compiler_params=params(56),
        cost_estimate=pl.CostEstimate(flops=MIB, bytes_accessed=2 * MIB, transcendentals=0),
        name="finish",
    )(got)


def shards(tokens, norm_gain, key_weight, value_weight, key_cotangent, value_cotangent):
    length, width = tokens.shape
    feats = key_weight.shape[1]
    count = math.prod(SIZES)
    x, zh, core, y, zl = (lax.axis_index(a).astype(jnp.int32) for a in AXES)
    half = HEAD // 2
    angles = np.arange(length)[:, None] * np.exp(-(2.0 * np.arange(half) / HEAD) * math.log(500000.0))[None, :]
    cosine = jnp.asarray(np.concatenate([np.cos(angles), np.cos(angles)], 1).astype(np.float32))
    sine = jnp.asarray(np.concatenate([-np.sin(angles), np.sin(angles)], 1).astype(np.float32))
    gain = norm_gain.reshape(1, width)

    shard = jnp.concatenate([key_weight, value_weight], axis=1)
    spread = jnp.broadcast_to(shard[None], (4, 256, 2 * feats))
    near = lax.all_to_all(spread, "x", 0, 0, tiled=True)

    blocks = jnp.arange(8, dtype=jnp.int32) * 2
    both, inv, normed, *sibling = norm_and_terms(
        blocks + 1 - core, tokens, gain, key_cotangent, value_cotangent, cosine, sine, spread
    )
    sibling = [to_core(s) for s in sibling]
    terms = add(own_terms(blocks + core, normed, both), sibling, near)
    got = lax.all_to_all(terms.reshape(64, 32, 2 * feats), ("x", "zh", "y", "zl"), 0, 0, tiled=True)

    near, half_near = pick(1 - zl, near, terms)
    first = send(half_near, lambda x, y, z, c: (x, y, 3 - z, c))
    second = send(first, lambda x, y, z, c: (x, y, z ^ 1, c))
    weights = [near, to_core(near), first, to_core(first), second, to_core(second)]
    rotated_keys, value_rows, coef = forward(
        jnp.stack([zh, core, zl]), normed, both, inv, cosine, sine, weights, terms
    )
    i4, i2 = jnp.arange(4, dtype=jnp.int32), jnp.arange(2, dtype=jnp.int32)
    place = jnp.concatenate(
        [i4 * 2 + zh, (2 * zl + i2) * 2 + 1 - zh, (2 - 2 * zl + i2) * 2 + 1 - zh, core.reshape(1)]
    )
    input_grad = backward(place, tokens, both, inv, coef, gain, weights)

    row = (y * 2 + zl) * 32
    key_rows, value_rows_of = (lax.dynamic_slice(w, (row, 0), (32, feats)) for w in (key_weight, value_weight))
    own_gain = lax.dynamic_slice(norm_gain, ((x * 4 + zh * 2 + core) * 256 + row,), (32,))
    mean, gain_rows = total(count, got, key_rows, value_rows_of, jnp.tile(own_gain, 4).reshape(1, HEAD), input_grad)
    got = lax.all_to_all(mean, ("y", "zl"), 0, 0, tiled=True)
    gain_rows = lax.all_to_all(gain_rows, AXES, 0, 0, tiled=True)
    key_grad, value_grad = finish(got)
    return rotated_keys, value_rows, input_grad, key_grad, value_grad, gain_rows[:, :32].reshape(width)


def solution(mesh):
    fine = Mesh(mesh.devices.reshape(SIZES), AXES)
    fsdp, replica = ("x", "zh", "c"), ("y", "zl")
    in_specs = (P(fsdp + replica, None), P(), P(fsdp, None), P(fsdp, None), P(fsdp + replica, None), P(fsdp + replica, None))
    out_specs = (P(fsdp + replica, None), P(fsdp + replica, None), P(fsdp + replica, None), P(fsdp, None), P(fsdp, None), P())
    return jax.shard_map(shards, mesh=fine, in_specs=in_specs, out_specs=out_specs, check_vma=False)
```

time: 200 us -> 253 us (1.26)
  waiting for transfers between devices: 60.2 us -> 92 us
  Pallas kernels: 79.7 us -> 106 us
  blocking collectives: 0 us -> 18 us
  between operations: 14.3 us -> 0.77 us
  starting transfers between devices: 32 us -> 22.4 us
  local copies, waits for them, and re-layouts: 11.2 us -> 8.11 us
  other arithmetic: 0.69 us -> 3.38 us
    pallas_call x10 -> x7, Pallas kernels: 55.6 us -> 88.8 us  [the longest x1 32.9 us: pick(): pl.pallas_call(pick_kernel, in_specs=[pl.BlockSpec(memory_space=pltpu.SME...]
    ppermute x17 -> x9, waiting for transfers between devices: 60.1 us -> 83 us  [send(): return lax.ppermute(value, AXES, pairs)]
    ppermute x17 -> x9, starting transfers between devices: 24.7 us -> 5.82 us  [send(): return lax.ppermute(value, AXES, pairs)]
    all_to_all x0 -> x1, blocking collectives: none -> 18 us  [shards(): gain_rows = lax.all_to_all(gain_rows, AXES, 0, 0, tiled=True)]
    all_to_all x1 -> x3, starting transfers between devices: 7.27 us -> 16.6 us  [the longest x1 8.3 us: shards(): lax.all_to_all(terms.reshape(64, 32, 2 * feats), ('x', 'zh', 'y', 'zl'),...]
    all_to_all x1 -> x3, waiting for transfers between devices: 0.01 us -> 8.99 us  [the longest x1 8.99 us: shards(): got = lax.all_to_all(mean, ('y', 'zl'), 0, 0, tiled=True)]
    pallas_call x1, Pallas kernels: 24 us -> 17.3 us  [norm_and_terms(): pl.pallas_call(norm_kernel, grid_spec=pltpu.PrefetchScalarGridSpec(num_sc...]
    unnamed x42 -> x10, local copies, waits for them, and re-layouts: 7.42 us -> 3.04 us
  transfers between devices with their start and end apart: 19 -> 12, of which waited for: 8 -> 3; matrix products, arithmetic and copies ran while one was open for 1% -> 2% of each run, Pallas kernels for 37% -> 24%
where the time goes in v3:
time: 253 us; the launch traced here: 251 us
  Pallas kernels  106 us (42%)
  waiting for transfers between devices  92 us (36%)
  starting transfers between devices  22.4 us (9%)
  blocking collectives  18 us (7%)
  local copies, waits for them, and re-layouts  8.11 us (3%)
  other arithmetic  3.38 us (1%)
    ppermute x9, waiting for transfers between devices, send(): return lax.ppermute(value, AXES, pairs)  83 us
    pallas_call x1, Pallas kernels, pick(): pl.pallas_call(pick_kernel, in_specs=[pl.BlockSpec(memory_space=pltpu.SME...  32.9 us
    all_to_all x1, blocking collectives, shards(): gain_rows = lax.all_to_all(gain_rows, AXES, 0, 0, tiled=True)  18 us
    pallas_call x1, Pallas kernels, backward(): pl.pallas_call(backward_kernel, grid_spec=pltpu.PrefetchScalarGridSpec(nu...  17.8 us
    pallas_call x1, Pallas kernels, norm_and_terms(): pl.pallas_call(norm_kernel, grid_spec=pltpu.PrefetchScalarGridSpec(num_sc...  17.3 us
    pallas_call x1, Pallas kernels, forward(): pl.pallas_call(forward_kernel, grid_spec=pltpu.PrefetchScalarGridSpec(num...  16.2 us
    pallas_call x1, Pallas kernels, own_terms(): pl.pallas_call(own_kernel, grid_spec=pltpu.PrefetchScalarGridSpec(num_sca...  9.27 us
    all_to_all x1, waiting for transfers between devices, shards(): got = lax.all_to_all(mean, ('y', 'zl'), 0, 0, tiled=True)  8.99 us
  transfers between devices with their start and end apart: 12, of which 3 were waited for; matrix products, arithmetic and copies ran while one was open for 2% of the time, Pallas kernels for 24%

profile of v3, /device:TPU:2, one launch (start us, length us, event | category | flops | bytes accessed | tf_op | source)
XLA Modules:
  0.0 250.8 jit_solution(3143338020792663877)
XLA Ops:
  0.6 1.1 pad_maximum_fusion
  1.7 1.6 broadcast_in_dim.2.after_ref
  3.3 4.8 %all-to-all-start = ((bf16[4,256,1024]{2,1,0:T(8,128)(2,1)}), bf16[4,256,1024]{2,1,0:T(8,128)(2,1)S(1)}, u32[]{:S(2)}, u32[]{:S(2)}) async-start(bf16[4,256,1024]{2,1,0:T(8,128)(2,1)} %broadcast_in_dim.2.after_ref), calls=%async_computation | async-start | bytes 4194304 | tf_op jit(solution)/shard_map/all_to_all | solution.py:412
  8.2 0.5 add_subtract_fusion.2.order_ref
  8.7 17.3 %norm_and_terms.1 = (bf16[1024,1024]{1,0:T(8,128)(2,1)}, f32[1024,128]{1,0:T(8,128)}, bf16[1024,4096]{1,0:T(8,128)(2,1)}, bf16[2,256,1024]{2,1,0:T(8,128)(2,1)},...) custom-call(s32[8]{0:T(128)} %add_subtract_fusion.2.order_ref, ...), custom_call_target="tpu_custom_call" | custom-call | flops 10485760000 | bytes 20971520 | tf_op jit(solution)/shard_map/norm_and_terms/pallas_call | solution.py:106
  26.1 0.5 collective-permute-start.1
  26.7 0.4 collective-permute-start.3
  27.1 0.5 fusion.order_ref
  27.6 9.3 %own_terms.1.own_ref = bf16[8,256,1024]{2,1,0:T(8,128)(2,1)} custom-call(s32[8]{0:T(128)} %fusion.order_ref, bf16[1024,4096]{1,0:T(8,128)(2,1)} %get-tuple-element.22.n0_ref.n1_ref.normed_ref, bf16[1024,4096]{1,0:T(8,128)(2,1)} %get-tuple-element.22.n0_ref.n1_ref.normed_ref, bf16[1024,1024]{1,0:T(8,128)(2,1)} %get-tuple-element.23.both_ref), custom_call_target="tpu_custom_call" | custom-call | tf_op jit(solution)/shard_map/own_terms/pallas_call | solution.py:153
  36.9 0.9 copy-done.3
  37.9 1.3 copy-done
  39.2 6.3 %add.87.after_ref.refs_6_ = bf16[8,256,1024]{2,1,0:T(8,128)(2,1)} custom-call(bf16[8,256,1024]{2,1,0:T(8,128)(2,1)} %own_terms.1.own_ref, bf16[2,256,1024]{2,1,0:T(8,128)(2,1)} %copy-done.3, bf16[2,256,1024]{2,1,0:T(8,128)(2,1)} %collective-permute-done.1.refs_1_, bf16[2,256,1024]{2,1,0:T(8,128)(2,1)} %collective-permute-done.2.refs_2_, ...), custom_call_target="tpu_custom_call" | custom-call | tf_op jit(solution)/shard_map/add/pallas_call | solution.py:180
  45.5 32.9 %pick.1 = (bf16[4,256,1024]{2,1,0:T(8,128)(2,1)}, bf16[2,256,1024]{2,1,0:T(8,128)(2,1)}) custom-call(s32[1]{0:T(128)} %bitcast.4.half_ref, bf16[4,256,1024]{2,1,0:T(8,128)(2,1)} %copy-done, bf16[8,256,1024]{2,1,0:T(8,128)(2,1)} %add.87.after_ref.refs_6_), custom_call_target="tpu_custom_call", output_to_operand_aliasing={{0}: (1, {})} | custom-call | bytes 2097152 | tf_op jit(solution)/shard_map/pick/pallas_call | solution.py:200
  78.4 4.1 %collective-permute-start.5 = (bf16[2,256,1024]{2,1,0:T(8,128)(2,1)}, bf16[2,256,1024]{2,1,0:T(8,128)(2,1)S(1)}, u32[]{:S(2)}, u32[]{:S(2)}) collective-permute-start(bf16[2,256,1024]{2,1,0:T(8,128)(2,1)} %get-tuple-element.30), channel_id=1, source_target_pairs={{0,17},{1,16},{2,19},{3,18},{4,21},{5,20},{6,23},{7,22},{8,25},{9,... | collective-permute-start | bytes 3145736 | tf_op jit(solution)/shard_map/ppermute | solution.py:26
  82.5 8.3 %all-to-all-start.1 = ((bf16[64,32,1024]{2,1,0:T(8,128)(2,1)}), bf16[64,32,1024]{2,1,0:T(8,128)(2,1)}, u32[]{:S(2)}, u32[]{:S(2)}) async-start(bf16[64,32,1024]{2,1,0:T(8,128)(2,1)} %bitcast.11), calls=%async_computation.1 | async-start | bytes 8388608 | tf_op jit(solution)/shard_map/all_to_all | solution.py:420
  90.8 59.4 %collective-permute-done.5.refs_2_ = bf16[2,256,1024]{2,1,0:T(8,128)(2,1)S(1)} collective-permute-done((bf16[2,256,1024]{2,1,0:T(8,128)(2,1)}, bf16[2,256,1024]{2,1,0:T(8,128)(2,1)S(1)}, u32[]{:S(2)}, u32[]{:S(2)}) %collective-permute-start.5) | collective-permute-done | bytes 1048608 | tf_op jit(solution)/shard_map/ppermute | solution.py:26
  150.3 0.5 collective-permute-start.6
  150.8 23.6 %collective-permute-done.7.refs_4_ = bf16[2,256,1024]{2,1,0:T(8,128)(2,1)} collective-permute-done((bf16[2,256,1024]{2,1,0:T(8,128)(2,1)S(1)}, bf16[2,256,1024]{2,1,0:T(8,128)(2,1)}, u32[]{:S(2)}, u32[]{:S(2)}) %collective-permute-start.7) | collective-permute-done | bytes 1048608 | tf_op jit(solution)/shard_map/ppermute | solution.py:26
  174.4 0.8 dynamic_slice.11
  175.2 0.6 reshape_tile.3.refs_3_
  175.8 0.7 pad_add_fusion.place_ref
  176.4 0.6 pad_add_fusion.1.place_ref
  177.0 1.4 constant_dynamic-slice_fusion
  178.5 16.2 %forward.1 = (bf16[1024,512]{1,0:T(8,128)(2,1)}, bf16[1024,512]{1,0:T(8,128)(2,1)}, f32[1024,128]{1,0:T(8,128)}) custom-call(s32[3]{0:T(128)} %pad_add_fusion.place_ref, bf16[1024,4096]{1,0:T(8,128)(2,1)} %get-tuple-element.22.n0_ref.n1_ref.normed_ref, bf16[1024,1024]{1,0:T(8,128)(2,1)} %get-tuple-element.23.both_ref, ...), custom_call_target="tpu_custom_call" | custom-call | flops 8589934592 | bytes 20971520 | tf_op jit(solution)/shard_map/forward/pallas_call | solution.py:258
  194.6 17.8 %backward.1.refs_4_ = bf16[1024,4096]{1,0:T(8,128)(2,1)} custom-call(s32[9]{0:T(128)} %pad_add_fusion.1.place_ref, bf16[1024,4096]{1,0:T(8,128)(2,1)} %tok_ref.3, bf16[1024,1024]{1,0:T(8,128)(2,1)} %get-tuple-element.23.both_ref, f32[1024,128]{1,0:T(8,128)} %get-tuple-element.24.inv_ref, f32[1024,128]{1,0:T(8,128)} %get-tuple-element.33.coef_ref, ...), custom_call_target="tpu_custom_call" | custom-call | flops 8589934592 | bytes 29360128 | tf_op jit(solution)/shard_map/backward/pallas_call | solution.py:303
  212.5 4.3 %total.1 = (bf16[8,32,1024]{2,1,0:T(8,128)(2,1)}, f32[128,128]{1,0:T(8,128)}) custom-call(bf16[64,32,1024]{2,1,0:T(8,128)(2,1)} %all-to-all-done.1.refs_0_, bf16[32,512]{1,0:T(8,128)(2,1)} %get-tuple-element.41.refs_1_, bf16[32,512]{1,0:T(8,128)(2,1)} %get-tuple-element.40.refs_2_, f32[1,128]{1,0:T(1,128)} %reshape_tile.3.refs_3_, ...), custom_call_target="tpu_custom_call" | custom-call | flops 2097152 | bytes 5242880 | tf_op jit(solution)/shard_map/total/pallas_call | solution.py:359
  216.8 18.0 %all_to_all.27 = f32[128,1,128]{2,1,0:T(1,128)S(1)} all-to-all(f32[128,1,128]{2,1,0:T(1,128)} %bitcast.13), channel_id=1, replica_groups=mesh['x'=4,'zh'=2,'c'=2,'y'=4,'zl'=2] {'x','zh','c','y','zl'}, dimensions={0} | all-to-all | bytes 131072 | tf_op jit(solution)/shard_map/all_to_all | solution.py:440
  234.8 3.5 %all-to-all-start.2 = ((bf16[8,32,1024]{2,1,0:T(8,128)(2,1)}), bf16[8,32,1024]{2,1,0:T(8,128)(2,1)S(1)}, u32[]{:S(2)}, u32[]{:S(2)}) async-start(bf16[8,32,1024]{2,1,0:T(8,128)(2,1)} %get-tuple-element.34), calls=%async_computation.2 | async-start | bytes 1048576 | tf_op jit(solution)/shard_map/all_to_all | solution.py:439
  238.3 0.7 reshape.32
  239.0 9.0 %all-to-all-done.2.got_ref = bf16[8,32,1024]{2,1,0:T(8,128)(2,1)S(1)} async-done(((bf16[8,32,1024]{2,1,0:T(8,128)(2,1)}), bf16[8,32,1024]{2,1,0:T(8,128)(2,1)S(1)}, u32[]{:S(2)}, u32[]{:S(2)}) %all-to-all-start.2) | async-done | bytes 524320 | tf_op jit(solution)/shard_map/all_to_all | solution.py:439
  248.0 0.8 copy-done.2
  248.8 2.0 finish.1
  (24 shorter events, 0.3 us)
Async XLA Ops:
  3.3 33.6 %all-to-all-start = ((bf16[4,256,1024]{2,1,0:T(8,128)(2,1)}), bf16[4,256,1024]{2,1,0:T(8,128)(2,1)S(1)}, u32[]{:S(2)}, u32[]{:S(2)}) async-start(bf16[4,256,1024]{2,1,0:T(8,128)(2,1)} %broadcast_in_dim.2.after_ref), calls=%async_computation | async-start | bytes 4194304 | tf_op jit(solution)/shard_map/all_to_all | solution.py:412
  26.0 10.9 %collective-permute-start = (bf16[2,256,1024]{2,1,0:T(8,128)(2,1)}, bf16[2,256,1024]{2,1,0:T(8,128)(2,1)S(1)}, u32[]{:S(2)}, u32[]{:S(2)}) collective-permute-start(bf16[2,256,1024]{2,1,0:T(8,128)(2,1)} %get-tuple-element.25), channel_id=1, source_target_pairs={{0,8},{1,9},{2,10},{3,11},{4,12},{5,13},{6,14},{7,15},{8,0},{9,1},... | collective-permute-start | bytes 3145736 | tf_op jit(solution)/shard_map/ppermute | solution.py:26
  26.1 10.8 %collective-permute-start.1 = (bf16[2,256,1024]{2,1,0:T(8,128)(2,1)}, bf16[2,256,1024]{2,1,0:T(8,128)(2,1)}, u32[]{:S(2)}, u32[]{:S(2)}) collective-permute-start(bf16[2,256,1024]{2,1,0:T(8,128)(2,1)} %get-tuple-element.26), channel_id=1, source_target_pairs={{0,8},{1,9},{2,10},{3,11},{4,12},{5,13},{6,14},{7,15},{8,0},{9,1},... | collective-permute-start | bytes 3145736 | tf_op jit(solution)/shard_map/ppermute | solution.py:26
  26.6 10.3 %collective-permute-start.2 = (bf16[2,256,1024]{2,1,0:T(8,128)(2,1)}, bf16[2,256,1024]{2,1,0:T(8,128)(2,1)}, u32[]{:S(2)}, u32[]{:S(2)}) collective-permute-start(bf16[2,256,1024]{2,1,0:T(8,128)(2,1)} %get-tuple-element.27), channel_id=1, source_target_pairs={{0,8},{1,9},{2,10},{3,11},{4,12},{5,13},{6,14},{7,15},{8,0},{9,1},... | collective-permute-start | bytes 3145736 | tf_op jit(solution)/shard_map/ppermute | solution.py:26
  26.7 10.3 %collective-permute-start.3 = (bf16[2,256,1024]{2,1,0:T(8,128)(2,1)}, bf16[2,256,1024]{2,1,0:T(8,128)(2,1)}, u32[]{:S(2)}, u32[]{:S(2)}) collective-permute-start(bf16[2,256,1024]{2,1,0:T(8,128)(2,1)} %get-tuple-element.28), channel_id=1, source_target_pairs={{0,8},{1,9},{2,10},{3,11},{4,12},{5,13},{6,14},{7,15},{8,0},{9,1},... | collective-permute-start | bytes 3145736 | tf_op jit(solution)/shard_map/ppermute | solution.py:26
  36.9 1.0 copy-start.3
  37.9 1.3 copy-start
  78.4 71.8 %collective-permute-start.5 = (bf16[2,256,1024]{2,1,0:T(8,128)(2,1)}, bf16[2,256,1024]{2,1,0:T(8,128)(2,1)S(1)}, u32[]{:S(2)}, u32[]{:S(2)}) collective-permute-start(bf16[2,256,1024]{2,1,0:T(8,128)(2,1)} %get-tuple-element.30), channel_id=1, source_target_pairs={{0,17},{1,16},{2,19},{3,18},{4,21},{5,20},{6,23},{7,22},{8,25},{9,... | collective-permute-start | bytes 3145736 | tf_op jit(solution)/shard_map/ppermute | solution.py:26
  82.5 67.7 %copy-start.1 = (bf16[4,256,1024]{2,1,0:T(8,128)(2,1)S(1)}, bf16[4,256,1024]{2,1,0:T(8,128)(2,1)}, u32[]{:S(2)}) copy-start(bf16[4,256,1024]{2,1,0:T(8,128)(2,1)} %get-tuple-element.29.refs_0_) | copy-start | bytes 6291460
  82.5 130.0 %all-to-all-start.1 = ((bf16[64,32,1024]{2,1,0:T(8,128)(2,1)}), bf16[64,32,1024]{2,1,0:T(8,128)(2,1)}, u32[]{:S(2)}, u32[]{:S(2)}) async-start(bf16[64,32,1024]{2,1,0:T(8,128)(2,1)} %bitcast.11), calls=%async_computation.1 | async-start | bytes 8388608 | tf_op jit(solution)/shard_map/all_to_all | solution.py:420
  150.2 28.3 %copy-start.4 = (bf16[2,256,1024]{2,1,0:T(8,128)(2,1)}, bf16[2,256,1024]{2,1,0:T(8,128)(2,1)S(1)}, u32[]{:S(2)}) copy-start(bf16[2,256,1024]{2,1,0:T(8,128)(2,1)S(1)} %collective-permute-done.5.refs_2_) | copy-start | bytes 3145732
  150.2 24.2 %collective-permute-start.7 = (bf16[2,256,1024]{2,1,0:T(8,128)(2,1)S(1)}, bf16[2,256,1024]{2,1,0:T(8,128)(2,1)}, u32[]{:S(2)}, u32[]{:S(2)}) collective-permute-start(bf16[2,256,1024]{2,1,0:T(8,128)(2,1)S(1)} %collective-permute-done.5.refs_2_), channel_id=1, source_target_pairs={{0,1},{1,0},{2,3},{3,2},{4,5},{5,4},{6,7},{7,6},{8,9},{9,8},{10,11... | collective-permute-start | bytes 3145736 | tf_op jit(solution)/shard_map/ppermute | solution.py:26
  150.2 28.2 %collective-permute-start.4 = (bf16[4,256,1024]{2,1,0:T(8,128)(2,1)S(1)}, bf16[4,256,1024]{2,1,0:T(8,128)(2,1)}, u32[]{:S(2)}, u32[]{:S(2)}) collective-permute-start(bf16[4,256,1024]{2,1,0:T(8,128)(2,1)S(1)} %copy-done.1), channel_id=1, source_target_pairs={{0,8},{1,9},{2,10},{3,11},{4,12},{5,13},{6,14},{7,15},{8,0},{9,1},... | collective-permute-start | bytes 6291464 | tf_op jit(solution)/shard_map/ppermute | solution.py:26
  150.3 28.2 %collective-permute-start.6 = (bf16[2,256,1024]{2,1,0:T(8,128)(2,1)S(1)}, bf16[2,256,1024]{2,1,0:T(8,128)(2,1)}, u32[]{:S(2)}, u32[]{:S(2)}) collective-permute-start(bf16[2,256,1024]{2,1,0:T(8,128)(2,1)S(1)} %collective-permute-done.5.refs_2_), channel_id=1, source_target_pairs={{0,8},{1,9},{2,10},{3,11},{4,12},{5,13},{6,14},{7,15},{8,0},{9,1},... | collective-permute-start | bytes 3145736 | tf_op jit(solution)/shard_map/ppermute | solution.py:26
  174.4 4.0 %collective-permute-start.8 = (bf16[2,256,1024]{2,1,0:T(8,128)(2,1)}, bf16[2,256,1024]{2,1,0:T(8,128)(2,1)}, u32[]{:S(2)}, u32[]{:S(2)}) collective-permute-start(bf16[2,256,1024]{2,1,0:T(8,128)(2,1)} %collective-permute-done.7.refs_4_), channel_id=1, source_target_pairs={{0,8},{1,9},{2,10},{3,11},{4,12},{5,13},{6,14},{7,15},{8,0},{9,1},... | collective-permute-start | bytes 3145736 | tf_op jit(solution)/shard_map/ppermute | solution.py:26
  234.8 13.2 %all-to-all-start.2 = ((bf16[8,32,1024]{2,1,0:T(8,128)(2,1)}), bf16[8,32,1024]{2,1,0:T(8,128)(2,1)S(1)}, u32[]{:S(2)}, u32[]{:S(2)}) async-start(bf16[8,32,1024]{2,1,0:T(8,128)(2,1)} %get-tuple-element.34), calls=%async_computation.2 | async-start | bytes 1048576 | tf_op jit(solution)/shard_map/all_to_all | solution.py:439
  248.0 0.8 copy-start.2

commit v4 on v3

--- a/solution.py
+++ b/solution.py
@@ -189,41 +189,29 @@
     )(in_hbm(own), *(in_hbm(g) for g in got), in_hbm(after))
 
 
-def pick_kernel(half_ref, value_ref, after_ref, same_ref, half_out_ref, done):
-    rows = half_out_ref.shape[0]
-    copy = pltpu.make_async_copy(value_ref.at[pl.ds(half_ref[0] * rows, rows)], half_out_ref, done)
-    copy.start()
-    copy.wait()
-
-
-def pick(half, value, after):
-    return pl.pallas_call(
-        pick_kernel,
-        in_specs=[pl.BlockSpec(memory_space=pltpu.SMEM), UNREAD, UNREAD],
-        out_specs=[pl.BlockSpec(memory_space=pltpu.HBM)] * 2,
-        out_shape=[pltpu.HBM(value.shape, BF16), pltpu.HBM((value.shape[0] // 2, *value.shape[1:]), BF16)],
-        scratch_shapes=[pltpu.SemaphoreType.DMA],
-        input_output_aliases={1: 0},
-        cost_estimate=pl.CostEstimate(flops=0, bytes_accessed=2 * MIB, transcendentals=0),
-        name="pick",
-    )(half.reshape(1), in_hbm(value), in_hbm(after))
+def release(value, after):
+    return pl.pallas_call(
+        lambda *refs: None,
+        in_specs=[UNREAD] * 2,
+        out_specs=pl.BlockSpec(memory_space=pltpu.HBM),
+        out_shape=pltpu.HBM(value.shape, value.dtype),
+        input_output_aliases={0: 0},
+        cost_estimate=pl.CostEstimate(flops=0, bytes_accessed=0, transcendentals=0),
+        name="release",
+    )(in_hbm(value), in_hbm(after))
 
 
 def forward_kernel(
-    place_ref, normed_ref, both_ref, inv_ref, cos_ref, sin_ref, *refs
+    core_ref, normed_ref, both_ref, inv_ref, cos_ref, sin_ref, own_ref, other_ref, after_ref,
+    key_ref, value_ref, coef_ref, held_ref, done,
 ):
-    w_refs, (key_ref, value_ref, coef_ref, held_ref, done) = refs[:6], refs[7:]
     feats = key_ref.shape[1]
-    zh, core, zl = place_ref[0], place_ref[1], place_ref[2]
     first_step = pl.program_id(0) == 0
     copies = []
-    for p, w_ref in enumerate(w_refs):
-        c = lax.rem(core + p % 2, 2)
-        if p < 2:
-            to = held_ref.at[:, zh, c]
-        else:
-            to = held_ref.at[pl.ds(2 * lax.rem(zl + p // 2 - 1, 2), 2), 1 - zh, c]
-        copies.append(pltpu.make_async_copy(w_ref, to, done.at[p]))
+    for p in range(4):
+        for c, w_ref in enumerate((own_ref, other_ref)):
+            to = held_ref.at[pl.ds(2 * p, 2), lax.rem(core_ref[0] + c, 2)]
+            copies.append(pltpu.make_async_copy(w_ref.at[pl.ds(2 * p, 2)], to, done.at[2 * p + c]))
 
     @pl.when(first_step)
     def _():
@@ -231,15 +219,12 @@
             copy.start()
 
     pre = None
-    for z in range(2):
-        for copy in copies[:2] if z == 0 else copies[2:]:
-            pl.when(first_step)(copy.wait)
-        at = lax.rem(zh + z, 2)
-        for x in range(4):
-            columns = pl.ds(pl.multiple_of(x * 1024 + at * 512, 512), 512)
-            w = held_ref[x, at].reshape(512, 2 * feats)
-            term = jnp.dot(normed_ref[:, columns], w, preferred_element_type=F32)
-            pre = term if pre is None else pre + term
+    for p in range(4):
+        pl.when(first_step)(copies[2 * p].wait)
+        pl.when(first_step)(copies[2 * p + 1].wait)
+        w = held_ref[2 * p : 2 * p + 2].reshape(1024, 2 * feats)
+        term = jnp.dot(normed_ref[:, p * 1024 : p * 1024 + 1024], w, preferred_element_type=F32)
+        pre = term if pre is None else pre + term
     key_pre, value_pre = pre[:, :feats], pre[:, feats:]
     key_ref[...] = turn(key_pre, cos_ref[...], sin_ref[...], 1.0).astype(BF16)
     value_ref[...] = value_pre.astype(BF16)
@@ -250,19 +235,19 @@
     coef_ref[...] = inv * inv * (inner * (1.0 / normed_ref.shape[1]))
 
 
-def forward(place, normed, both, inv, cosine, sine, weights, after):
+def forward(core, normed, both, inv, cosine, sine, own, other, after):
     rows, width = normed.shape
     feats = both.shape[1] // 2
     tb = 256
-    by_rows = lambda n: pl.BlockSpec((tb, n), lambda i, place: (i, 0))
+    by_rows = lambda n: pl.BlockSpec((tb, n), lambda i, core: (i, 0))
     return pl.pallas_call(
         forward_kernel,
         grid_spec=pltpu.PrefetchScalarGridSpec(
             num_scalar_prefetch=1,
             grid=(rows // tb,),
-            in_specs=[by_rows(width), by_rows(2 * feats), by_rows(HEAD), by_rows(HEAD), by_rows(HEAD)] + [UNREAD] * 7,
+            in_specs=[by_rows(width), by_rows(2 * feats), by_rows(HEAD), by_rows(HEAD), by_rows(HEAD)] + [UNREAD] * 3,
             out_specs=[by_rows(feats), by_rows(feats), by_rows(HEAD)],
-            scratch_shapes=[pltpu.VMEM((4, 2, 2, 256, 2 * feats), BF16), pltpu.SemaphoreType.DMA((6,))],
+            scratch_shapes=[pltpu.VMEM((8, 2, 256, 2 * feats), BF16), pltpu.SemaphoreType.DMA((8,))],
         ),
         out_shape=[
             pltpu.HBM((rows, feats), BF16),
@@ -272,34 +257,24 @@
         compiler_params=params(56),
         cost_estimate=pl.CostEstimate(flops=4 * rows * width * feats, bytes_accessed=20 * MIB, transcendentals=0),
         name="forward",
-    )(place, in_hbm(normed), in_hbm(both), in_hbm(inv), cosine, sine, *(in_hbm(w) for w in weights), in_hbm(after))
-
-
-def backward_kernel(place_ref, tok_ref, both_ref, inv_ref, coef_ref, gain_ref, *refs):
-    w_refs, out_ref = refs[:6], refs[6]
-
-    def part(pair):
-        for c, w_ref in enumerate(pair):
-            s = pl.ds(pl.multiple_of(lax.rem(place_ref[8] + c, 2) * 256, 256), 256)
-            grad = lax.dot_general(both_ref[...], w_ref[0], (((1,), (1,)), ((), ())), preferred_element_type=F32)
-            out = inv_ref[:, :1] * (grad * gain_ref[:, s]) - tok_ref[:, s].astype(F32) * coef_ref[:, :1]
-            out_ref[:, s] = out.astype(BF16)
-
-    i = pl.program_id(0)
-    pl.when(i < 4)(lambda: part(w_refs[:2]))
-    pl.when((i >= 4) & (i < 6))(lambda: part(w_refs[2:4]))
-    pl.when(i >= 6)(lambda: part(w_refs[4:]))
-
-
-def backward(place, tokens, both, inv, coef, gain, weights):
+    )(core, in_hbm(normed), in_hbm(both), in_hbm(inv), cosine, sine, in_hbm(own), in_hbm(other), in_hbm(after))
+
+
+def backward_kernel(core_ref, tok_ref, both_ref, inv_ref, coef_ref, gain_ref, own_ref, other_ref, out_ref):
+    for c, w_ref in enumerate((own_ref, other_ref)):
+        s = pl.ds(pl.multiple_of(lax.rem(core_ref[0] + c, 2) * 256, 256), 256)
+        grad = lax.dot_general(both_ref[...], w_ref[0], (((1,), (1,)), ((), ())), preferred_element_type=F32)
+        out = inv_ref[:, :1] * (grad * gain_ref[:, s]) - tok_ref[:, s].astype(F32) * coef_ref[:, :1]
+        out_ref[:, s] = out.astype(BF16)
+
+
+def backward(core, tokens, both, inv, coef, gain, own, other):
     rows, width = tokens.shape
     feats = both.shape[1] // 2
     cb = 512
-    whole = lambda n: pl.BlockSpec((rows, n), lambda i, place: (0, 0))
-    columns = pl.BlockSpec((rows, cb), lambda i, place: (0, place[i]))
-    block = lambda first, size: pl.BlockSpec(
-        (1, 256, 2 * feats), lambda i, place: (jnp.clip(i - first, 0, size - 1), 0, 0)
-    )
+    whole = lambda n: pl.BlockSpec((rows, n), lambda i, core: (0, 0))
+    columns = pl.BlockSpec((rows, cb), lambda i, core: (0, i))
+    weights = pl.BlockSpec((1, 256, 2 * feats), lambda i, core: (i, 0, 0))
     return pl.pallas_call(
         backward_kernel,
         grid_spec=pltpu.PrefetchScalarGridSpec(
@@ -310,13 +285,9 @@
                 whole(2 * feats),
                 whole(HEAD),
                 whole(HEAD),
-                pl.BlockSpec((1, cb), lambda i, place: (0, place[i])),
-                block(0, 4),
-                block(0, 4),
-                block(4, 2),
-                block(4, 2),
-                block(6, 2),
-                block(6, 2),
+                pl.BlockSpec((1, cb), lambda i, core: (0, i)),
+                weights,
+                weights,
             ],
             out_specs=columns,
         ),
@@ -324,7 +295,7 @@
         compiler_params=params(56),
         cost_estimate=pl.CostEstimate(flops=4 * rows * width * feats, bytes_accessed=28 * MIB, transcendentals=0),
         name="backward",
-    )(place, in_hbm(tokens), in_hbm(both), in_hbm(inv), in_hbm(coef), gain, *(in_hbm(w) for w in weights))
+    )(core, in_hbm(tokens), in_hbm(both), in_hbm(inv), in_hbm(coef), gain, in_hbm(own), in_hbm(other))
 
 
 def total_kernel(count, got_ref, kw_ref, vw_ref, gain_ref, after_ref, out_ref, gain_out_ref, sum_ref):
@@ -345,7 +316,7 @@
     @pl.when(g == pl.num_programs(0) - 1)
     def _():
         mean = sum_ref[...] * (1.0 / count)
-        out_ref[...] = jnp.broadcast_to(mean.astype(BF16)[None], out_ref.shape)
+        out_ref[...] = mean.astype(BF16)
         products = mean[:, :feats] * kw_ref[...].astype(F32) + mean[:, feats:] * vw_ref[...].astype(F32)
         sums = jnp.broadcast_to(jnp.sum(products, axis=1, keepdims=True), (products.shape[0], HEAD)).T
         line = jnp.concatenate([sums[:1]] * (HEAD // sums.shape[1]), axis=1) / gain_ref[...]
@@ -366,8 +337,8 @@
             fixed((1, HEAD)),
             UNREAD,
         ],
-        out_specs=[fixed((8, rows, width)), fixed((count, HEAD))],
-        out_shape=[pltpu.HBM((8, rows, width), BF16), pltpu.HBM((count, HEAD), F32)],
+        out_specs=[fixed((rows, width)), fixed((count, HEAD))],
+        out_shape=[pltpu.HBM((rows, width), BF16), pltpu.HBM((count, HEAD), F32)],
         scratch_shapes=[pltpu.VMEM((rows, width), F32)],
         compiler_params=params(56),
         cost_estimate=pl.CostEstimate(flops=2 * MIB, bytes_accessed=5 * MIB, transcendentals=0),
@@ -375,25 +346,46 @@
     )(in_hbm(got), key_rows, value_rows, gain_rows, in_hbm(after))
 
 
-def finish_kernel(got_ref, key_ref, value_ref):
+def pair_kernel(zl_ref, mine_ref, got_ref, out_ref):
+    out_ref[zl_ref[0]] = mine_ref[...]
+    out_ref[1 - zl_ref[0]] = got_ref[...]
+
+
+def pair(zl, mine, got):
+    vmem = pl.BlockSpec(memory_space=pltpu.VMEM)
+    return pl.pallas_call(
+        pair_kernel,
+        in_specs=[pl.BlockSpec(memory_space=pltpu.SMEM), vmem, vmem],
+        out_specs=vmem,
+        out_shape=jax.ShapeDtypeStruct((2, *mine.shape), BF16),
+        compiler_params=params(8),
+        cost_estimate=pl.CostEstimate(flops=0, bytes_accessed=0, transcendentals=0),
+        name="pair",
+    )(zl.reshape(1), mine, got)
+
+
+def finish_kernel(y_ref, p0_ref, p1_ref, p2_ref, p3_ref, key_ref, value_ref):
     feats = key_ref.shape[1]
-    rows = got_ref[...].reshape(key_ref.shape[0], 2 * feats).astype(F32)
-    key_ref[...] = rows[:, :feats]
-    value_ref[...] = rows[:, feats:]
-
-
-def finish(got):
-    pieces, rows, width = got.shape
+    for d, p_ref in enumerate((p0_ref, p1_ref, p2_ref, p3_ref)):
+        for z in range(2):
+            first = lax.rem(y_ref[0] + 4 - d, 4) * 64 + z * 32
+            at = pl.ds(pl.multiple_of(first, 32), 32)
+            key_ref[at, :] = p_ref[z, :, :feats].astype(F32)
+            value_ref[at, :] = p_ref[z, :, feats:].astype(F32)
+
+
+def finish(y, pieces):
+    pairs, rows, width = pieces[0].shape
     vmem = pl.BlockSpec(memory_space=pltpu.VMEM)
     return pl.pallas_call(
         finish_kernel,
-        in_specs=[vmem],
+        in_specs=[pl.BlockSpec(memory_space=pltpu.SMEM)] + [vmem] * 4,
         out_specs=[vmem] * 2,
-        out_shape=[pltpu.HBM((pieces * rows, width // 2), F32)] * 2,
-        compiler_params=params(56),
+        out_shape=[pltpu.HBM((4 * pairs * rows, width // 2), F32)] * 2,
+        compiler_params=params(8),
         cost_estimate=pl.CostEstimate(flops=MIB, bytes_accessed=2 * MIB, transcendentals=0),
         name="finish",
-    )(got)
+    )(y.reshape(1), *pieces)
 
 
 def shards(tokens, norm_gain, key_weight, value_weight, key_cotangent, value_cotangent):
@@ -408,37 +400,33 @@
     gain = norm_gain.reshape(1, width)
 
     shard = jnp.concatenate([key_weight, value_weight], axis=1)
-    spread = jnp.broadcast_to(shard[None], (4, 256, 2 * feats))
-    near = lax.all_to_all(spread, "x", 0, 0, tiled=True)
+    spread = jnp.broadcast_to(shard[None], (8, 256, 2 * feats))
+    own_weights = lax.all_to_all(spread, ("x", "zh"), 0, 0, tiled=True)
 
     blocks = jnp.arange(8, dtype=jnp.int32) * 2
     both, inv, normed, *sibling = norm_and_terms(
         blocks + 1 - core, tokens, gain, key_cotangent, value_cotangent, cosine, sine, spread
     )
     sibling = [to_core(s) for s in sibling]
-    terms = add(own_terms(blocks + core, normed, both), sibling, near)
+    terms = add(own_terms(blocks + core, normed, both), sibling, inv)
     got = lax.all_to_all(terms.reshape(64, 32, 2 * feats), ("x", "zh", "y", "zl"), 0, 0, tiled=True)
 
-    near, half_near = pick(1 - zl, near, terms)
-    first = send(half_near, lambda x, y, z, c: (x, y, 3 - z, c))
-    second = send(first, lambda x, y, z, c: (x, y, z ^ 1, c))
-    weights = [near, to_core(near), first, to_core(first), second, to_core(second)]
+    own_weights = release(own_weights, terms)
+    other_weights = to_core(own_weights)
+    at = core.reshape(1)
     rotated_keys, value_rows, coef = forward(
-        jnp.stack([zh, core, zl]), normed, both, inv, cosine, sine, weights, terms
+        at, normed, both, inv, cosine, sine, own_weights, other_weights, terms
     )
-    i4, i2 = jnp.arange(4, dtype=jnp.int32), jnp.arange(2, dtype=jnp.int32)
-    place = jnp.concatenate(
-        [i4 * 2 + zh, (2 * zl + i2) * 2 + 1 - zh, (2 - 2 * zl + i2) * 2 + 1 - zh, core.reshape(1)]
-    )
-    input_grad = backward(place, tokens, both, inv, coef, gain, weights)
+    input_grad = backward(at, tokens, both, inv, coef, gain, own_weights, other_weights)
 
     row = (y * 2 + zl) * 32
     key_rows, value_rows_of = (lax.dynamic_slice(w, (row, 0), (32, feats)) for w in (key_weight, value_weight))
     own_gain = lax.dynamic_slice(norm_gain, ((x * 4 + zh * 2 + core) * 256 + row,), (32,))
     mean, gain_rows = total(count, got, key_rows, value_rows_of, jnp.tile(own_gain, 4).reshape(1, HEAD), input_grad)
-    got = lax.all_to_all(mean, ("y", "zl"), 0, 0, tiled=True)
     gain_rows = lax.all_to_all(gain_rows, AXES, 0, 0, tiled=True)
-    key_grad, value_grad = finish(got)
+    pieces = pair(zl, mean, send(mean, lambda x, y, z, c: (x, y, z ^ 1, c)))
+    pieces = [pieces] + [send(pieces, lambda x, y, z, c, d=d: (x, y + d, z, c)) for d in (1, 2, 3)]
+    key_grad, value_grad = finish(y, pieces)
     return rotated_keys, value_rows, input_grad, key_grad, value_grad, gain_rows[:, :32].reshape(width)
 
 

time: 253 us -> 171 us (0.68)
  waiting for transfers between devices: 92 us -> 40.3 us
  Pallas kernels: 106 us -> 70.2 us
  starting transfers between devices: 22.4 us -> 29.2 us
    ppermute x9, waiting for transfers between devices: 83 us -> 2.56 us  [send(): return lax.ppermute(value, AXES, pairs)]
    pallas_call x2 -> x3, Pallas kernels: 34.9 us -> 1.05 us  [the longest x1 1.04 us: finish(): pl.pallas_call(finish_kernel, in_specs=[pl.BlockSpec(memory_space=pltpu.S...]
    all_to_all x1, waiting for transfers between devices: 0.01 us -> 18.2 us  [shards(): lax.all_to_all(terms.reshape(64, 32, 2 * feats), ('x', 'zh', 'y', 'zl'),...]
    all_to_all x2 -> x1, waiting for transfers between devices: 8.99 us -> 19.6 us  [shards(): own_weights = lax.all_to_all(spread, ('x', 'zh'), 0, 0, tiled=True)]
    ppermute x9, starting transfers between devices: 5.82 us -> 9.6 us  [send(): return lax.ppermute(value, AXES, pairs)]
    all_to_all x1, starting transfers between devices: 8.3 us -> 11.5 us  [shards(): lax.all_to_all(terms.reshape(64, 32, 2 * feats), ('x', 'zh', 'y', 'zl'),...]
    all_to_all x2 -> x1, starting transfers between devices: 8.32 us -> 8.14 us  [shards(): own_weights = lax.all_to_all(spread, ('x', 'zh'), 0, 0, tiled=True)]
  transfers between devices with their start and end apart: 12 -> 11, of which waited for: 3 -> 3; matrix products, arithmetic and copies ran while one was open for 2% -> 3% of each run, Pallas kernels for 24% -> 39%
where the time goes in v4:
time: 171 us; the launch traced here: 168 us
  Pallas kernels  70.2 us (41%)
  waiting for transfers between devices  40.3 us (24%)
  starting transfers between devices  29.2 us (17%)
  blocking collectives  16.9 us (10%)
  local copies, waits for them, and re-layouts  8.79 us (5%)
  other arithmetic  2.11 us (1%)
    all_to_all x1, waiting for transfers between devices, shards(): own_weights = lax.all_to_all(spread, ('x', 'zh'), 0, 0, tiled=True)  19.6 us
    all_to_all x1, waiting for transfers between devices, shards(): lax.all_to_all(terms.reshape(64, 32, 2 * feats), ('x', 'zh', 'y', 'zl'),...  18.2 us
    pallas_call x1, Pallas kernels, norm_and_terms(): pl.pallas_call(norm_kernel, grid_spec=pltpu.PrefetchScalarGridSpec(num_sc...  17.4 us
    all_to_all x1, blocking collectives, shards(): gain_rows = lax.all_to_all(gain_rows, AXES, 0, 0, tiled=True)  16.9 us
    pallas_call x1, Pallas kernels, backward(): pl.pallas_call(backward_kernel, grid_spec=pltpu.PrefetchScalarGridSpec(nu...  16.4 us
    pallas_call x1, Pallas kernels, forward(): pl.pallas_call(forward_kernel, grid_spec=pltpu.PrefetchScalarGridSpec(num...  15.7 us
    all_to_all x1, starting transfers between devices, shards(): lax.all_to_all(terms.reshape(64, 32, 2 * feats), ('x', 'zh', 'y', 'zl'),...  11.5 us
    ppermute x9, starting transfers between devices, send(): return lax.ppermute(value, AXES, pairs)  9.6 us
  transfers between devices with their start and end apart: 11, of which 3 were waited for; matrix products, arithmetic and copies ran while one was open for 3% of the time, Pallas kernels for 39%

profile of v4, /device:TPU:2, one launch (start us, length us, event | category | flops | bytes accessed | tf_op | source)
XLA Modules:
  0.0 168.3 jit_solution(8709390789665661695)
XLA Ops:
  0.6 1.1 pad_maximum_fusion
  1.7 2.5 %broadcast_in_dim.2.after_ref = bf16[8,256,1024]{2,1,0:T(8,128)(2,1)} broadcast(bf16[256,1024]{1,0:T(8,128)(2,1)S(1)} %pad_maximum_fusion), dimensions={1,2} | broadcast | bytes 4718592 | tf_op jit(solution)/shard_map/broadcast_in_dim | solution.py:403
  4.2 8.1 %all-to-all-start = ((bf16[8,256,1024]{2,1,0:T(8,128)(2,1)}), bf16[8,256,1024]{2,1,0:T(8,128)(2,1)}, u32[]{:S(2)}, u32[]{:S(2)}) async-start(bf16[8,256,1024]{2,1,0:T(8,128)(2,1)} %broadcast_in_dim.2.after_ref), calls=%async_computation | async-start | bytes 8388608 | tf_op jit(solution)/shard_map/all_to_all | solution.py:404
  12.4 0.5 add_subtract_fusion.order_ref
  12.9 17.4 %norm_and_terms.1 = (bf16[1024,1024]{1,0:T(8,128)(2,1)}, f32[1024,128]{1,0:T(8,128)}, bf16[1024,4096]{1,0:T(8,128)(2,1)}, bf16[2,256,1024]{2,1,0:T(8,128)(2,1)},...) custom-call(s32[8]{0:T(128)} %add_subtract_fusion.order_ref, ...), custom_call_target="tpu_custom_call" | custom-call | flops 10485760000 | bytes 20971520 | tf_op jit(solution)/shard_map/norm_and_terms/pallas_call | solution.py:106
  30.4 0.5 collective-permute-start.1
  31.0 0.4 collective-permute-start.3
  31.4 0.5 fusion.order_ref
  31.9 9.2 %own_terms.1.own_ref = bf16[8,256,1024]{2,1,0:T(8,128)(2,1)} custom-call(s32[8]{0:T(128)} %fusion.order_ref, bf16[1024,4096]{1,0:T(8,128)(2,1)} %get-tuple-element.20.n0_ref.n1_ref.normed_ref, bf16[1024,4096]{1,0:T(8,128)(2,1)} %get-tuple-element.20.n0_ref.n1_ref.normed_ref, bf16[1024,1024]{1,0:T(8,128)(2,1)} %get-tuple-element.21.both_ref), custom_call_target="tpu_custom_call" | custom-call | tf_op jit(solution)/shard_map/own_terms/pallas_call | solution.py:153
  41.1 0.9 copy-done.1
  42.0 0.3 copy-done.2
  42.4 0.4 copy-done.3
  42.7 0.3 copy-done.4
  43.1 6.3 %add.37.refs_1_.after_ref = bf16[8,256,1024]{2,1,0:T(8,128)(2,1)} custom-call(bf16[8,256,1024]{2,1,0:T(8,128)(2,1)} %own_terms.1.own_ref, bf16[2,256,1024]{2,1,0:T(8,128)(2,1)} %copy-done.1, bf16[2,256,1024]{2,1,0:T(8,128)(2,1)} %copy-done.2, bf16[2,256,1024]{2,1,0:T(8,128)(2,1)} %copy-done.3, bf16[2,256,1024]{2,1,0:T(8,128)(2,1)} %copy-done.4, ...), custom_call_target="tpu_custom_call" | custom-call | tf_op jit(solution)/shard_map/add/pallas_call | solution.py:180
  49.4 19.6 %all-to-all-done.refs_0_ = bf16[8,256,1024]{2,1,0:T(8,128)(2,1)} async-done(((bf16[8,256,1024]{2,1,0:T(8,128)(2,1)}), bf16[8,256,1024]{2,1,0:T(8,128)(2,1)}, u32[]{:S(2)}, u32[]{:S(2)}) %all-to-all-start) | async-done | bytes 4194336 | tf_op jit(solution)/shard_map/all_to_all | solution.py:404
  69.0 11.5 %all-to-all-start.1 = ((bf16[64,32,1024]{2,1,0:T(8,128)(2,1)}), bf16[64,32,1024]{2,1,0:T(8,128)(2,1)}, u32[]{:S(2)}, u32[]{:S(2)}) async-start(bf16[64,32,1024]{2,1,0:T(8,128)(2,1)} %bitcast.10), calls=%async_computation.1 | async-start | bytes 8388608 | tf_op jit(solution)/shard_map/all_to_all | solution.py:412
  80.5 0.8 dynamic_slice.11
  81.2 0.6 reshape_tile.3.refs_3_
  81.9 1.4 constant_dynamic-slice_fusion
  83.3 15.7 %forward.1 = (bf16[1024,512]{1,0:T(8,128)(2,1)}, bf16[1024,512]{1,0:T(8,128)(2,1)}, f32[1024,128]{1,0:T(8,128)}) custom-call(s32[1]{0:T(128)} %bitcast.core_ref, bf16[1024,4096]{1,0:T(8,128)(2,1)} %get-tuple-element.20.n0_ref.n1_ref.normed_ref, bf16[1024,1024]{1,0:T(8,128)(2,1)} %get-tuple-element.21.both_ref, ...), custom_call_target="tpu_custom_call" | custom-call | flops 8589934592 | bytes 20971520 | tf_op jit(solution)/shard_map/forward/pallas_call | solution.py:243
  99.0 16.4 %backward.1.refs_4_ = bf16[1024,4096]{1,0:T(8,128)(2,1)} custom-call(s32[1]{0:T(128)} %bitcast.core_ref, bf16[1024,4096]{1,0:T(8,128)(2,1)} %tok_ref.3, bf16[1024,1024]{1,0:T(8,128)(2,1)} %get-tuple-element.21.both_ref, f32[1024,128]{1,0:T(8,128)} %get-tuple-element.22.refs_4_.inv_ref, f32[1024,128]{1,0:T(8,128)} %get-tuple-element.29.coef_ref, ...), custom_call_target="tpu_custom_call" | custom-call | flops 8589934592 | bytes 29360128 | tf_op jit(solution)/shard_map/backward/pallas_call | solution.py:278
  115.5 18.2 %all-to-all-done.1.refs_0_ = bf16[64,32,1024]{2,1,0:T(8,128)(2,1)} async-done(((bf16[64,32,1024]{2,1,0:T(8,128)(2,1)}), bf16[64,32,1024]{2,1,0:T(8,128)(2,1)}, u32[]{:S(2)}, u32[]{:S(2)}) %all-to-all-start.1) | async-done | bytes 4194336 | tf_op jit(solution)/shard_map/all_to_all | solution.py:412
  133.6 4.1 %total.1 = (bf16[32,1024]{1,0:T(8,128)(2,1)}, f32[128,128]{1,0:T(8,128)}) custom-call(bf16[64,32,1024]{2,1,0:T(8,128)(2,1)} %all-to-all-done.1.refs_0_, bf16[32,512]{1,0:T(8,128)(2,1)} %get-tuple-element.35.refs_1_, bf16[32,512]{1,0:T(8,128)(2,1)} %get-tuple-element.34.refs_2_, f32[1,128]{1,0:T(1,128)} %reshape_tile.3.refs_3_, ...), custom_call_target="tpu_custom_call" | custom-call | flops 2097152 | bytes 5242880 | tf_op jit(solution)/shard_map/total/pallas_call | solution.py:330
  137.8 1.9 %collective-permute-start.5 = (bf16[32,1024]{1,0:T(8,128)(2,1)}, bf16[32,1024]{1,0:T(8,128)(2,1)S(1)}, u32[]{:S(2)}, u32[]{:S(2)}) collective-permute-start(bf16[32,1024]{1,0:T(8,128)(2,1)} %get-tuple-element.30.mine_ref), channel_id=1, source_target_pairs={{0,1},{1,0},{2,3},{3,2},{4,5},{5,4},{6,7},{7,6},{8,9},{9,8},{10,11... | collective-permute-start | bytes 196616 | tf_op jit(solution)/shard_map/ppermute | solution.py:26
  139.7 2.5 %collective-permute-done.5.got_ref = bf16[32,1024]{1,0:T(8,128)(2,1)S(1)} collective-permute-done((bf16[32,1024]{1,0:T(8,128)(2,1)}, bf16[32,1024]{1,0:T(8,128)(2,1)S(1)}, u32[]{:S(2)}, u32[]{:S(2)}) %collective-permute-start.5) | collective-permute-done | bytes 65568 | tf_op jit(solution)/shard_map/ppermute | solution.py:26
  142.3 0.8 copy-done
  143.1 0.4 collective-permute-start.6
  143.5 3.6 %collective-permute-start.7 = (bf16[2,32,1024]{2,1,0:T(8,128)(2,1)S(1)}, bf16[2,32,1024]{2,1,0:T(8,128)(2,1)S(1)}, u32[]{:S(2)}, u32[]{:S(2)}) collective-permute-start(bf16[2,32,1024]{2,1,0:T(8,128)(2,1)S(1)} %pair.1.p0_ref), channel_id=1, source_target_pairs={{0,4},{1,5},{2,6},{3,7},{4,0},{5,1},{6,2},{7,3},{8,12},{9,13},{10,... | collective-permute-start | bytes 393224 | tf_op jit(solution)/shard_map/ppermute | solution.py:26
  147.1 2.5 %collective-permute-start.8 = (bf16[2,32,1024]{2,1,0:T(8,128)(2,1)S(1)}, bf16[2,32,1024]{2,1,0:T(8,128)(2,1)S(1)}, u32[]{:S(2)}, u32[]{:S(2)}) collective-permute-start(bf16[2,32,1024]{2,1,0:T(8,128)(2,1)S(1)} %pair.1.p0_ref), channel_id=1, source_target_pairs={{0,6},{1,7},{2,0},{3,1},{4,2},{5,3},{6,4},{7,5},{8,14},{9,15},{10,... | collective-permute-start | bytes 393224 | tf_op jit(solution)/shard_map/ppermute | solution.py:26
  149.7 16.9 %all_to_all.22 = f32[128,1,128]{2,1,0:T(1,128)S(1)} all-to-all(f32[128,1,128]{2,1,0:T(1,128)} %bitcast.12), channel_id=1, replica_groups=mesh['x'=4,'zh'=2,'c'=2,'y'=4,'zl'=2] {'x','zh','c','y','zl'}, dimensions={0} | all-to-all | bytes 131072 | tf_op jit(solution)/shard_map/all_to_all | solution.py:426
  166.5 0.7 reshape.39
  167.2 1.0 finish.1
  (19 shorter events, 0.2 us)
Async XLA Ops:
  4.2 64.7 %all-to-all-start = ((bf16[8,256,1024]{2,1,0:T(8,128)(2,1)}), bf16[8,256,1024]{2,1,0:T(8,128)(2,1)}, u32[]{:S(2)}, u32[]{:S(2)}) async-start(bf16[8,256,1024]{2,1,0:T(8,128)(2,1)} %broadcast_in_dim.2.after_ref), calls=%async_computation | async-start | bytes 8388608 | tf_op jit(solution)/shard_map/all_to_all | solution.py:404
  30.3 10.8 %collective-permute-start = (bf16[2,256,1024]{2,1,0:T(8,128)(2,1)}, bf16[2,256,1024]{2,1,0:T(8,128)(2,1)S(1)}, u32[]{:S(2)}, u32[]{:S(2)}) collective-permute-start(bf16[2,256,1024]{2,1,0:T(8,128)(2,1)} %get-tuple-element.23), channel_id=1, source_target_pairs={{0,8},{1,9},{2,10},{3,11},{4,12},{5,13},{6,14},{7,15},{8,0},{9,1},... | collective-permute-start | bytes 3145736 | tf_op jit(solution)/shard_map/ppermute | solution.py:26
  30.4 10.7 %collective-permute-start.1 = (bf16[2,256,1024]{2,1,0:T(8,128)(2,1)}, bf16[2,256,1024]{2,1,0:T(8,128)(2,1)S(1)}, u32[]{:S(2)}, u32[]{:S(2)}) collective-permute-start(bf16[2,256,1024]{2,1,0:T(8,128)(2,1)} %get-tuple-element.24), channel_id=1, source_target_pairs={{0,8},{1,9},{2,10},{3,11},{4,12},{5,13},{6,14},{7,15},{8,0},{9,1},... | collective-permute-start | bytes 3145736 | tf_op jit(solution)/shard_map/ppermute | solution.py:26
  30.9 10.2 %collective-permute-start.2 = (bf16[2,256,1024]{2,1,0:T(8,128)(2,1)}, bf16[2,256,1024]{2,1,0:T(8,128)(2,1)S(1)}, u32[]{:S(2)}, u32[]{:S(2)}) collective-permute-start(bf16[2,256,1024]{2,1,0:T(8,128)(2,1)} %get-tuple-element.25), channel_id=1, source_target_pairs={{0,8},{1,9},{2,10},{3,11},{4,12},{5,13},{6,14},{7,15},{8,0},{9,1},... | collective-permute-start | bytes 3145736 | tf_op jit(solution)/shard_map/ppermute | solution.py:26
  31.0 10.1 %collective-permute-start.3 = (bf16[2,256,1024]{2,1,0:T(8,128)(2,1)}, bf16[2,256,1024]{2,1,0:T(8,128)(2,1)S(1)}, u32[]{:S(2)}, u32[]{:S(2)}) collective-permute-start(bf16[2,256,1024]{2,1,0:T(8,128)(2,1)} %get-tuple-element.26), channel_id=1, source_target_pairs={{0,8},{1,9},{2,10},{3,11},{4,12},{5,13},{6,14},{7,15},{8,0},{9,1},... | collective-permute-start | bytes 3145736 | tf_op jit(solution)/shard_map/ppermute | solution.py:26
  41.1 1.0 copy-start.1
  41.1 1.3 copy-start.2
  41.1 1.6 copy-start.3
  41.1 2.0 %copy-start.4 = (bf16[2,256,1024]{2,1,0:T(8,128)(2,1)}, bf16[2,256,1024]{2,1,0:T(8,128)(2,1)S(1)}, u32[]{:S(2)}) copy-start(bf16[2,256,1024]{2,1,0:T(8,128)(2,1)S(1)} %collective-permute-done.3.refs_3_) | copy-start | bytes 3145732
  69.0 14.3 %collective-permute-start.4 = (bf16[8,256,1024]{2,1,0:T(8,128)(2,1)}, bf16[8,256,1024]{2,1,0:T(8,128)(2,1)}, u32[]{:S(2)}, u32[]{:S(2)}) collective-permute-start(bf16[8,256,1024]{2,1,0:T(8,128)(2,1)} %release.1.own_ref), channel_id=1, source_target_pairs={{0,8},{1,9},{2,10},{3,11},{4,12},{5,13},{6,14},{7,15},{8,0},{9,1},... | collective-permute-start | bytes 12582920 | tf_op jit(solution)/shard_map/ppermute | solution.py:26
  69.0 64.7 %all-to-all-start.1 = ((bf16[64,32,1024]{2,1,0:T(8,128)(2,1)}), bf16[64,32,1024]{2,1,0:T(8,128)(2,1)}, u32[]{:S(2)}, u32[]{:S(2)}) async-start(bf16[64,32,1024]{2,1,0:T(8,128)(2,1)} %bitcast.10), calls=%async_computation.1 | async-start | bytes 8388608 | tf_op jit(solution)/shard_map/all_to_all | solution.py:412
  137.8 4.5 %collective-permute-start.5 = (bf16[32,1024]{1,0:T(8,128)(2,1)}, bf16[32,1024]{1,0:T(8,128)(2,1)S(1)}, u32[]{:S(2)}, u32[]{:S(2)}) collective-permute-start(bf16[32,1024]{1,0:T(8,128)(2,1)} %get-tuple-element.30.mine_ref), channel_id=1, source_target_pairs={{0,1},{1,0},{2,3},{3,2},{4,5},{5,4},{6,7},{7,6},{8,9},{9,8},{10,11... | collective-permute-start | bytes 196616 | tf_op jit(solution)/shard_map/ppermute | solution.py:26
  142.3 0.8 copy-start
  143.1 24.1 %collective-permute-start.6 = (bf16[2,32,1024]{2,1,0:T(8,128)(2,1)S(1)}, bf16[2,32,1024]{2,1,0:T(8,128)(2,1)S(1)}, u32[]{:S(2)}, u32[]{:S(2)}) collective-permute-start(bf16[2,32,1024]{2,1,0:T(8,128)(2,1)S(1)} %pair.1.p0_ref), channel_id=1, source_target_pairs={{0,2},{1,3},{2,4},{3,5},{4,6},{5,7},{6,0},{7,1},{8,10},{9,11},{10,... | collective-permute-start | bytes 393224 | tf_op jit(solution)/shard_map/ppermute | solution.py:26
  143.5 23.7 %collective-permute-start.7 = (bf16[2,32,1024]{2,1,0:T(8,128)(2,1)S(1)}, bf16[2,32,1024]{2,1,0:T(8,128)(2,1)S(1)}, u32[]{:S(2)}, u32[]{:S(2)}) collective-permute-start(bf16[2,32,1024]{2,1,0:T(8,128)(2,1)S(1)} %pair.1.p0_ref), channel_id=1, source_target_pairs={{0,4},{1,5},{2,6},{3,7},{4,0},{5,1},{6,2},{7,3},{8,12},{9,13},{10,... | collective-permute-start | bytes 393224 | tf_op jit(solution)/shard_map/ppermute | solution.py:26
  147.1 20.1 %collective-permute-start.8 = (bf16[2,32,1024]{2,1,0:T(8,128)(2,1)S(1)}, bf16[2,32,1024]{2,1,0:T(8,128)(2,1)S(1)}, u32[]{:S(2)}, u32[]{:S(2)}) collective-permute-start(bf16[2,32,1024]{2,1,0:T(8,128)(2,1)S(1)} %pair.1.p0_ref), channel_id=1, source_target_pairs={{0,6},{1,7},{2,0},{3,1},{4,2},{5,3},{6,4},{7,5},{8,14},{9,15},{10,... | collective-permute-start | bytes 393224 | tf_op jit(solution)/shard_map/ppermute | solution.py:26

commit v5 on v4

--- a/solution.py
+++ b/solution.py
@@ -55,7 +55,7 @@
 
 def norm_kernel(
     order_ref, tok_ref, gain_ref, kc_ref, vc_ref, cos_ref, sin_ref, after_ref,
-    both_out_ref, inv_ref, stored_ref, t0_ref, t1_ref, t2_ref, t3_ref, normed_ref, both_ref, done,
+    both_out_ref, inv_ref, stored_ref, t0_ref, t1_ref, normed_ref, both_ref, done,
 ):
     i = pl.program_id(0)
     tb, feats = kc_ref.shape
@@ -88,10 +88,10 @@
         for j in range(2):
             columns = pl.ds(pl.multiple_of(order_ref[p * 2 + j] * 256, 256), 256)
             term = lax.dot_general(normed_ref[:, columns], both_ref[...], COLUMNS, preferred_element_type=F32)
-            terms_ref[j] = term.astype(BF16)
-
-    for p, terms_ref in enumerate((t0_ref, t1_ref, t2_ref, t3_ref)):
-        pl.when(i == 4 + p)(lambda p=p, terms_ref=terms_ref: part(p, terms_ref))
+            terms_ref[p % 2 * 2 + j] = term.astype(BF16)
+
+    for p in range(4):
+        pl.when(i == 4 + p)(lambda p=p: part(p, (t0_ref, t1_ref)[p // 2]))
 
     @pl.when(i == 7)
     def _():
@@ -122,7 +122,7 @@
                 by_rows(HEAD),
                 pl.BlockSpec(memory_space=pltpu.HBM),
             ]
-            + [pl.BlockSpec((2, 256, 2 * feats), lambda i, order: (0, 0, 0))] * 4,
+            + [pl.BlockSpec((4, 256, 2 * feats), lambda i, order: (0, 0, 0))] * 2,
             scratch_shapes=[
                 pltpu.VMEM((rows, width), BF16),
                 pltpu.VMEM((rows, 2 * feats), BF16),
@@ -134,20 +134,20 @@
             pltpu.HBM((rows, HEAD), F32),
             pltpu.HBM((rows, width), BF16),
         ]
-        + [pltpu.HBM((2, 256, 2 * feats), BF16)] * 4,
+        + [pltpu.HBM((4, 256, 2 * feats), BF16)] * 2,
         compiler_params=params(56),
         cost_estimate=pl.CostEstimate(flops=10000 * MIB, bytes_accessed=20 * MIB, transcendentals=0),
         name="norm_and_terms",
     )(order, in_hbm(tokens), gain, in_hbm(key_cot), in_hbm(value_cot), cosine, sine, in_hbm(after))
 
 
-def own_kernel(order_ref, n0_ref, n1_ref, both_ref, terms_ref):
+def own_kernel(order_ref, n0_ref, n1_ref, both_ref, after_ref, terms_ref):
     for j, n_ref in enumerate((n0_ref, n1_ref)):
         term = lax.dot_general(n_ref[...], both_ref[...], COLUMNS, preferred_element_type=F32)
         terms_ref[j] = term.astype(BF16)
 
 
-def own_terms(order, normed, both):
+def own_terms(order, normed, both, after):
     rows, feats = both.shape
     block = lambda j: pl.BlockSpec((rows, 256), lambda g, order: (0, order[2 * g + j]))
     return pl.pallas_call(
@@ -155,33 +155,36 @@
         grid_spec=pltpu.PrefetchScalarGridSpec(
             num_scalar_prefetch=1,
             grid=(4,),
-            in_specs=[block(0), block(1), pl.BlockSpec((rows, feats), lambda g, order: (0, 0))],
+            in_specs=[block(0), block(1), pl.BlockSpec((rows, feats), lambda g, order: (0, 0)), UNREAD],
             out_specs=pl.BlockSpec((2, 256, feats), lambda g, order: (g, 0, 0)),
         ),
         out_shape=pltpu.HBM((8, 256, feats), BF16),
         compiler_params=params(56),
-        cost_estimate=pl.CostEstimate(flops=0, bytes_accessed=0, transcendentals=0),
+        cost_estimate=pl.CostEstimate(flops=30000 * MIB, bytes_accessed=0, transcendentals=0),
         name="own_terms",
-    )(order, in_hbm(normed), in_hbm(normed), in_hbm(both))
-
-
-def add_kernel(own_ref, *refs):
-    got_refs, out_ref = refs[:4], refs[-1]
-    for p, got_ref in enumerate(got_refs):
-
-        @pl.when(pl.program_id(0) == p)
-        def _():
-            out_ref[...] = (own_ref[...].astype(F32) + got_ref[...].astype(F32)).astype(BF16)
+    )(order, in_hbm(normed), in_hbm(normed), in_hbm(both), in_hbm(after))
+
+
+def add_kernel(own_ref, got0_ref, got1_ref, after_ref, out_ref):
+    def part(got_ref):
+        out_ref[...] = (own_ref[...].astype(F32) + got_ref[...].astype(F32)).astype(BF16)
+
+    pl.when(pl.program_id(0) < 2)(lambda: part(got0_ref))
+    pl.when(pl.program_id(0) >= 2)(lambda: part(got1_ref))
 
 
 def add(own, got, after):
-    block = pl.BlockSpec((2, *own.shape[1:]), lambda g: (g, 0, 0))
-    fixed = pl.BlockSpec((2, *own.shape[1:]), lambda g: (0, 0, 0))
+    block = lambda place: pl.BlockSpec((2, *own.shape[1:]), lambda g: (place(g), 0, 0))
     return pl.pallas_call(
         add_kernel,
         grid=(4,),
-        in_specs=[block] + [fixed] * 4 + [UNREAD],
-        out_specs=block,
+        in_specs=[
+            block(lambda g: g),
+            block(lambda g: jnp.minimum(g, 1)),
+            block(lambda g: jnp.maximum(g - 2, 0)),
+            UNREAD,
+        ],
+        out_specs=block(lambda g: g),
         out_shape=pltpu.HBM(own.shape, BF16),
         compiler_params=params(56),
         cost_estimate=pl.CostEstimate(flops=0, bytes_accessed=0, transcendentals=0),
@@ -189,29 +192,34 @@
     )(in_hbm(own), *(in_hbm(g) for g in got), in_hbm(after))
 
 
-def release(value, after):
+def release(values, after):
+    n = len(values)
     return pl.pallas_call(
         lambda *refs: None,
-        in_specs=[UNREAD] * 2,
-        out_specs=pl.BlockSpec(memory_space=pltpu.HBM),
-        out_shape=pltpu.HBM(value.shape, value.dtype),
-        input_output_aliases={0: 0},
+        in_specs=[UNREAD] * (n + 1),
+        out_specs=[pl.BlockSpec(memory_space=pltpu.HBM)] * n,
+        out_shape=[pltpu.HBM(v.shape, v.dtype) for v in values],
+        input_output_aliases={k: k for k in range(n)},
         cost_estimate=pl.CostEstimate(flops=0, bytes_accessed=0, transcendentals=0),
         name="release",
-    )(in_hbm(value), in_hbm(after))
+    )(*(in_hbm(v) for v in values), in_hbm(after))
 
 
 def forward_kernel(
-    core_ref, normed_ref, both_ref, inv_ref, cos_ref, sin_ref, own_ref, other_ref, after_ref,
-    key_ref, value_ref, coef_ref, held_ref, done,
+    place_ref, normed_ref, both_ref, inv_ref, cos_ref, sin_ref, *refs
 ):
+    w_refs, (key_ref, value_ref, coef_ref, held_ref, done) = refs[:10], refs[11:]
     feats = key_ref.shape[1]
+    zh, core, x_here = place_ref[0], place_ref[1], place_ref[2]
     first_step = pl.program_id(0) == 0
     copies = []
-    for p in range(4):
-        for c, w_ref in enumerate((own_ref, other_ref)):
-            to = held_ref.at[pl.ds(2 * p, 2), lax.rem(core_ref[0] + c, 2)]
-            copies.append(pltpu.make_async_copy(w_ref.at[pl.ds(2 * p, 2)], to, done.at[2 * p + c]))
+    for p, w_ref in enumerate(w_refs):
+        c = lax.rem(core + p % 2, 2)
+        if p < 2:
+            to = held_ref.at[:, zh, c]
+        else:
+            to = held_ref.at[lax.rem(x_here + 5 - p // 2, 4), 1 - zh, c]
+        copies.append(pltpu.make_async_copy(w_ref, to, done.at[p]))
 
     @pl.when(first_step)
     def _():
@@ -219,12 +227,15 @@
             copy.start()
 
     pre = None
-    for p in range(4):
-        pl.when(first_step)(copies[2 * p].wait)
-        pl.when(first_step)(copies[2 * p + 1].wait)
-        w = held_ref[2 * p : 2 * p + 2].reshape(1024, 2 * feats)
-        term = jnp.dot(normed_ref[:, p * 1024 : p * 1024 + 1024], w, preferred_element_type=F32)
-        pre = term if pre is None else pre + term
+    for z in range(2):
+        for copy in copies[:2] if z == 0 else copies[2:]:
+            pl.when(first_step)(copy.wait)
+        at = lax.rem(zh + z, 2)
+        for x in range(4):
+            columns = pl.ds(pl.multiple_of(x * 1024 + at * 512, 512), 512)
+            w = held_ref[x, at].reshape(512, 2 * feats)
+            term = jnp.dot(normed_ref[:, columns], w, preferred_element_type=F32)
+            pre = term if pre is None else pre + term
     key_pre, value_pre = pre[:, :feats], pre[:, feats:]
     key_ref[...] = turn(key_pre, cos_ref[...], sin_ref[...], 1.0).astype(BF16)
     value_ref[...] = value_pre.astype(BF16)
@@ -235,19 +246,19 @@
     coef_ref[...] = inv * inv * (inner * (1.0 / normed_ref.shape[1]))
 
 
-def forward(core, normed, both, inv, cosine, sine, own, other, after):
+def forward(place, normed, both, inv, cosine, sine, weights, after):
     rows, width = normed.shape
     feats = both.shape[1] // 2
     tb = 256
-    by_rows = lambda n: pl.BlockSpec((tb, n), lambda i, core: (i, 0))
+    by_rows = lambda n: pl.BlockSpec((tb, n), lambda i, place: (i, 0))
     return pl.pallas_call(
         forward_kernel,
         grid_spec=pltpu.PrefetchScalarGridSpec(
             num_scalar_prefetch=1,
             grid=(rows // tb,),
-            in_specs=[by_rows(width), by_rows(2 * feats), by_rows(HEAD), by_rows(HEAD), by_rows(HEAD)] + [UNREAD] * 3,
+            in_specs=[by_rows(width), by_rows(2 * feats), by_rows(HEAD), by_rows(HEAD), by_rows(HEAD)] + [UNREAD] * 11,
             out_specs=[by_rows(feats), by_rows(feats), by_rows(HEAD)],
-            scratch_shapes=[pltpu.VMEM((8, 2, 256, 2 * feats), BF16), pltpu.SemaphoreType.DMA((8,))],
+            scratch_shapes=[pltpu.VMEM((4, 2, 2, 256, 2 * feats), BF16), pltpu.SemaphoreType.DMA((10,))],
         ),
         out_shape=[
             pltpu.HBM((rows, feats), BF16),
@@ -257,24 +268,33 @@
         compiler_params=params(56),
         cost_estimate=pl.CostEstimate(flops=4 * rows * width * feats, bytes_accessed=20 * MIB, transcendentals=0),
         name="forward",
-    )(core, in_hbm(normed), in_hbm(both), in_hbm(inv), cosine, sine, in_hbm(own), in_hbm(other), in_hbm(after))
-
-
-def backward_kernel(core_ref, tok_ref, both_ref, inv_ref, coef_ref, gain_ref, own_ref, other_ref, out_ref):
-    for c, w_ref in enumerate((own_ref, other_ref)):
-        s = pl.ds(pl.multiple_of(lax.rem(core_ref[0] + c, 2) * 256, 256), 256)
-        grad = lax.dot_general(both_ref[...], w_ref[0], (((1,), (1,)), ((), ())), preferred_element_type=F32)
-        out = inv_ref[:, :1] * (grad * gain_ref[:, s]) - tok_ref[:, s].astype(F32) * coef_ref[:, :1]
-        out_ref[:, s] = out.astype(BF16)
-
-
-def backward(core, tokens, both, inv, coef, gain, own, other):
+    )(place, in_hbm(normed), in_hbm(both), in_hbm(inv), cosine, sine, *(in_hbm(w) for w in weights), in_hbm(after))
+
+
+def backward_kernel(place_ref, tok_ref, both_ref, inv_ref, coef_ref, gain_ref, *refs):
+    w_refs, out_ref = refs[:10], refs[10]
+
+    def part(pair):
+        for c, w_ref in enumerate(pair):
+            s = pl.ds(pl.multiple_of(lax.rem(place_ref[8] + c, 2) * 256, 256), 256)
+            w = w_ref[...].reshape(256, both_ref.shape[1])
+            grad = lax.dot_general(both_ref[...], w, (((1,), (1,)), ((), ())), preferred_element_type=F32)
+            out = inv_ref[:, :1] * (grad * gain_ref[:, s]) - tok_ref[:, s].astype(F32) * coef_ref[:, :1]
+            out_ref[:, s] = out.astype(BF16)
+
+    i = pl.program_id(0)
+    pl.when(i < 4)(lambda: part(w_refs[:2]))
+    for d in range(4):
+        pl.when(i == 4 + d)(lambda d=d: part(w_refs[2 + 2 * d : 4 + 2 * d]))
+
+
+def backward(place, tokens, both, inv, coef, gain, weights):
     rows, width = tokens.shape
     feats = both.shape[1] // 2
     cb = 512
-    whole = lambda n: pl.BlockSpec((rows, n), lambda i, core: (0, 0))
-    columns = pl.BlockSpec((rows, cb), lambda i, core: (0, i))
-    weights = pl.BlockSpec((1, 256, 2 * feats), lambda i, core: (i, 0, 0))
+    whole = lambda n: pl.BlockSpec((rows, n), lambda i, place: (0, 0))
+    columns = pl.BlockSpec((rows, cb), lambda i, place: (0, place[i]))
+    block = pl.BlockSpec((1, 256, 2 * feats), lambda i, place: (jnp.minimum(i, 3), 0, 0))
     return pl.pallas_call(
         backward_kernel,
         grid_spec=pltpu.PrefetchScalarGridSpec(
@@ -285,17 +305,18 @@
                 whole(2 * feats),
                 whole(HEAD),
                 whole(HEAD),
-                pl.BlockSpec((1, cb), lambda i, core: (0, i)),
-                weights,
-                weights,
-            ],
+                pl.BlockSpec((1, cb), lambda i, place: (0, place[i])),
+                block,
+                block,
+            ]
+            + [pl.BlockSpec((256, 2 * feats), lambda i, place: (0, 0))] * 8,
             out_specs=columns,
         ),
         out_shape=pltpu.HBM((rows, width), BF16),
         compiler_params=params(56),
         cost_estimate=pl.CostEstimate(flops=4 * rows * width * feats, bytes_accessed=28 * MIB, transcendentals=0),
         name="backward",
-    )(core, in_hbm(tokens), in_hbm(both), in_hbm(inv), in_hbm(coef), gain, in_hbm(own), in_hbm(other))
+    )(place, in_hbm(tokens), in_hbm(both), in_hbm(inv), in_hbm(coef), gain, *(in_hbm(w) for w in weights))
 
 
 def total_kernel(count, got_ref, kw_ref, vw_ref, gain_ref, after_ref, out_ref, gain_out_ref, sum_ref):
@@ -400,24 +421,29 @@
     gain = norm_gain.reshape(1, width)
 
     shard = jnp.concatenate([key_weight, value_weight], axis=1)
-    spread = jnp.broadcast_to(shard[None], (8, 256, 2 * feats))
-    own_weights = lax.all_to_all(spread, ("x", "zh"), 0, 0, tiled=True)
+    spread = jnp.broadcast_to(shard[None], (4, 256, 2 * feats))
+    near = lax.all_to_all(spread, "x", 0, 0, tiled=True)
+    far = send(shard, lambda x, y, z, c: (x, y, z + 2, c))
+    far = [far] + [send(far, lambda x, y, z, c, d=d: (x + d, y, z, c)) for d in (1, 2, 3)]
 
     blocks = jnp.arange(8, dtype=jnp.int32) * 2
     both, inv, normed, *sibling = norm_and_terms(
         blocks + 1 - core, tokens, gain, key_cotangent, value_cotangent, cosine, sine, spread
     )
     sibling = [to_core(s) for s in sibling]
-    terms = add(own_terms(blocks + core, normed, both), sibling, inv)
+    terms = add(own_terms(blocks + core, normed, both, near), sibling, inv)
+    terms, near, *far = release([terms, near, *far], inv)
     got = lax.all_to_all(terms.reshape(64, 32, 2 * feats), ("x", "zh", "y", "zl"), 0, 0, tiled=True)
 
-    own_weights = release(own_weights, terms)
-    other_weights = to_core(own_weights)
-    at = core.reshape(1)
+    weights = [near, to_core(near)]
+    for w in far:
+        weights += [w, to_core(w)]
     rotated_keys, value_rows, coef = forward(
-        at, normed, both, inv, cosine, sine, own_weights, other_weights, terms
+        jnp.stack([zh, core, x]), normed, both, inv, cosine, sine, weights, terms
     )
-    input_grad = backward(at, tokens, both, inv, coef, gain, own_weights, other_weights)
+    i4 = jnp.arange(4, dtype=jnp.int32)
+    place = jnp.concatenate([i4 * 2 + zh, (x + 4 - i4) % 4 * 2 + 1 - zh, core.reshape(1)])
+    input_grad = backward(place, tokens, both, inv, coef, gain, weights)
 
     row = (y * 2 + zl) * 32
     key_rows, value_rows_of = (lax.dynamic_slice(w, (row, 0), (32, feats)) for w in (key_weight, value_weight))

time: 171 us -> 161 us (0.942)
  waiting for transfers between devices: 40.3 us -> 21.2 us
  blocking collectives: 16.9 us -> 22.6 us
    all_to_all x1, waiting for transfers between devices: 19.6 us -> 0.01 us  [shards(): near = lax.all_to_all(spread, 'x', 0, 0, tiled=True)]
    ppermute x9 -> x15, waiting for transfers between devices: 2.56 us -> 10.8 us  [send(): return lax.ppermute(value, AXES, pairs)]
    all_to_all x1, waiting for transfers between devices: 18.2 us -> 10.4 us  [shards(): lax.all_to_all(terms.reshape(64, 32, 2 * feats), ('x', 'zh', 'y', 'zl'),...]
    ppermute x9 -> x15, starting transfers between devices: 9.6 us -> 16.8 us  [send(): return lax.ppermute(value, AXES, pairs)]
    all_to_all x1, blocking collectives: 16.9 us -> 22.6 us  [shards(): gain_rows = lax.all_to_all(gain_rows, AXES, 0, 0, tiled=True)]
    all_to_all x1, starting transfers between devices: 8.14 us -> 4.82 us  [shards(): near = lax.all_to_all(spread, 'x', 0, 0, tiled=True)]
    all_to_all x1, starting transfers between devices: 11.5 us -> 8.87 us  [shards(): lax.all_to_all(terms.reshape(64, 32, 2 * feats), ('x', 'zh', 'y', 'zl'),...]
  transfers between devices with their start and end apart: 11 -> 17, of which waited for: 3 -> 6; matrix products, arithmetic and copies ran while one was open for 3% -> 4% of each run, Pallas kernels for 39% -> 42%
where the time goes in v5:
time: 161 us; the launch traced here: 158 us
  Pallas kernels  71.6 us (44%)
  starting transfers between devices  30.5 us (19%)
  blocking collectives  22.6 us (14%)
  waiting for transfers between devices  21.2 us (13%)
  local copies, waits for them, and re-layouts  9.38 us (6%)
  other arithmetic  2.19 us (1%)
    all_to_all x1, blocking collectives, shards(): gain_rows = lax.all_to_all(gain_rows, AXES, 0, 0, tiled=True)  22.6 us
    pallas_call x1, Pallas kernels, backward(): pl.pallas_call(backward_kernel, grid_spec=pltpu.PrefetchScalarGridSpec(nu...  17.7 us
    pallas_call x1, Pallas kernels, norm_and_terms(): pl.pallas_call(norm_kernel, grid_spec=pltpu.PrefetchScalarGridSpec(num_sc...  17.3 us
    ppermute x15, starting transfers between devices, send(): return lax.ppermute(value, AXES, pairs)  16.8 us
    pallas_call x1, Pallas kernels, forward(): pl.pallas_call(forward_kernel, grid_spec=pltpu.PrefetchScalarGridSpec(num...  16.2 us
    ppermute x15, waiting for transfers between devices, send(): return lax.ppermute(value, AXES, pairs)  10.8 us
    all_to_all x1, waiting for transfers between devices, shards(): lax.all_to_all(terms.reshape(64, 32, 2 * feats), ('x', 'zh', 'y', 'zl'),...  10.4 us
    pallas_call x1, Pallas kernels, own_terms(): pl.pallas_call(own_kernel, grid_spec=pltpu.PrefetchScalarGridSpec(num_sca...  9.16 us
  transfers between devices with their start and end apart: 17, of which 6 were waited for; matrix products, arithmetic and copies ran while one was open for 4% of the time, Pallas kernels for 42%

profile of v5, /device:TPU:2, one launch (start us, length us, event | category | flops | bytes accessed | tf_op | source)
XLA Modules:
  0.0 158.2 jit_solution(15209513847730462212)
XLA Ops:
  0.6 1.0 constant_dynamic-update-slice_fusion.1
  1.6 1.0 constant_dynamic-update-slice_fusion
  2.6 1.7 %broadcast_in_dim.2.after_ref = bf16[4,256,1024]{2,1,0:T(8,128)(2,1)} broadcast(bf16[256,1024]{1,0:T(8,128)(2,1)S(1)} %constant_dynamic-update-slice_fusion), dimensions={1,2} | broadcast | bytes 2621440 | tf_op jit(solution)/shard_map/broadcast_in_dim | solution.py:424
  4.3 4.8 %all-to-all-start = ((bf16[4,256,1024]{2,1,0:T(8,128)(2,1)}), bf16[4,256,1024]{2,1,0:T(8,128)(2,1)S(1)}, u32[]{:S(2)}, u32[]{:S(2)}) async-start(bf16[4,256,1024]{2,1,0:T(8,128)(2,1)} %broadcast_in_dim.2.after_ref), calls=%async_computation | async-start | bytes 4194304 | tf_op jit(solution)/shard_map/all_to_all | solution.py:425
  9.1 3.9 %collective-permute-start.2 = (bf16[256,1024]{1,0:T(8,128)(2,1)S(1)}, bf16[256,1024]{1,0:T(8,128)(2,1)S(1)}, u32[]{:S(2)}, u32[]{:S(2)}) collective-permute-start(bf16[256,1024]{1,0:T(8,128)(2,1)S(1)} %constant_dynamic-update-slice_fusion), channel_id=1, source_target_pairs={{0,16},{1,17},{2,18},{3,19},{4,20},{5,21},{6,22},{7,23},{8,24},{9,... | collective-permute-start | bytes 1572872 | tf_op jit(solution)/shard_map/ppermute | solution.py:26
  13.5 17.3 %norm_and_terms.1 = (bf16[1024,1024]{1,0:T(8,128)(2,1)}, f32[1024,128]{1,0:T(8,128)}, bf16[1024,4096]{1,0:T(8,128)(2,1)}, bf16[4,256,1024]{2,1,0:T(8,128)(2,1)}, bf16[4,256,1024]{2,1,0:T(8,128)(2,1)}) custom-call(s32[8]{0:T(128)} %add_subtract_fusion.order_ref, bf16[1024,4096]{1,0:T(8,128)(2,1)} %tok_ref.3, f32[1,4096]{1,0:T(1,128)} %bitcast.15, ...), custom_call_target="tpu_custom_call" | custom-call | flops 10485760000 | bytes 20971520 | tf_op jit(solution)/shard_map/norm_and_terms/pallas_call | solution.py:106
  31.9 1.5 collective-permute-start.3
  33.4 0.7 collective-permute-start.4
  34.1 2.5 %collective-permute-start.5 = (bf16[256,1024]{1,0:T(8,128)(2,1)S(1)}, bf16[256,1024]{1,0:T(8,128)(2,1)}, u32[]{:S(2)}, u32[]{:S(2)}) collective-permute-start(bf16[256,1024]{1,0:T(8,128)(2,1)S(1)} %collective-permute-done.2.refs_2_), channel_id=1, source_target_pairs={{0,96},{1,97},{2,98},{3,99},{4,100},{5,101},{6,102},{7,103},{8,104... | collective-permute-start | bytes 1572872 | tf_op jit(solution)/shard_map/ppermute | solution.py:26
  36.6 1.4 copy-done.1
  38.0 9.2 %own_terms.1.own_ref = bf16[8,256,1024]{2,1,0:T(8,128)(2,1)} custom-call(s32[8]{0:T(128)} %fusion.4.order_ref, bf16[1024,4096]{1,0:T(8,128)(2,1)} %get-tuple-element.24.n0_ref.n1_ref.normed_ref, bf16[1024,4096]{1,0:T(8,128)(2,1)} %get-tuple-element.24.n0_ref.n1_ref.normed_ref, bf16[1024,1024]{1,0:T(8,128)(2,1)} %get-tuple-element.25.both_ref, ...), custom_call_target="tpu_custom_call" | custom-call | flops 31457280000 | tf_op jit(solution)/shard_map/own_terms/pallas_call | solution.py:153
  47.2 6.0 %add.81.refs_0_ = bf16[8,256,1024]{2,1,0:T(8,128)(2,1)} custom-call(bf16[8,256,1024]{2,1,0:T(8,128)(2,1)} %own_terms.1.own_ref, bf16[4,256,1024]{2,1,0:T(8,128)(2,1)} %collective-permute-done.got0_ref, bf16[4,256,1024]{2,1,0:T(8,128)(2,1)} %collective-permute-done.1.got1_ref, f32[1024,128]{1,0:T(8,128)} %get-tuple-element.26.after_ref.refs_6_.inv_ref), custom_call_target="tpu_custom_call" | custom-call | tf_op jit(solution)/shard_map/add/pallas_call | solution.py:178
  53.2 5.8 %collective-permute-done.5.refs_5_ = bf16[256,1024]{1,0:T(8,128)(2,1)} collective-permute-done((bf16[256,1024]{1,0:T(8,128)(2,1)S(1)}, bf16[256,1024]{1,0:T(8,128)(2,1)}, u32[]{:S(2)}, u32[]{:S(2)}) %collective-permute-start.5) | collective-permute-done | bytes 524320 | tf_op jit(solution)/shard_map/ppermute | solution.py:26
  59.1 8.9 %all-to-all-start.1 = ((bf16[64,32,1024]{2,1,0:T(8,128)(2,1)}), bf16[64,32,1024]{2,1,0:T(8,128)(2,1)}, u32[]{:S(2)}, u32[]{:S(2)}) async-start(bf16[64,32,1024]{2,1,0:T(8,128)(2,1)} %bitcast.12), calls=%async_computation.1 | async-start | bytes 8388608 | tf_op jit(solution)/shard_map/all_to_all | solution.py:436
  69.2 0.8 dynamic_slice.11
  69.9 0.7 reshape_tile.3.refs_3_
  71.2 0.6 pad_add_fusion.1.place_ref
  71.8 1.4 constant_dynamic-slice_fusion
  73.7 0.9 collective-permute-done.7.refs_3_
  74.6 0.7 collective-permute-done.8.refs_5_
  75.4 16.2 %forward.1 = (bf16[1024,512]{1,0:T(8,128)(2,1)}, bf16[1024,512]{1,0:T(8,128)(2,1)}, f32[1024,128]{1,0:T(8,128)}) custom-call(s32[3]{0:T(128)} %pad_add_fusion.place_ref, bf16[1024,4096]{1,0:T(8,128)(2,1)} %get-tuple-element.24.n0_ref.n1_ref.normed_ref, bf16[1024,1024]{1,0:T(8,128)(2,1)} %get-tuple-element.25.both_ref, ...), custom_call_target="tpu_custom_call" | custom-call | flops 8589934592 | bytes 20971520 | tf_op jit(solution)/shard_map/forward/pallas_call | solution.py:254
  91.5 17.7 %backward.1.refs_4_ = bf16[1024,4096]{1,0:T(8,128)(2,1)} custom-call(s32[9]{0:T(128)} %pad_add_fusion.1.place_ref, bf16[1024,4096]{1,0:T(8,128)(2,1)} %tok_ref.3, bf16[1024,1024]{1,0:T(8,128)(2,1)} %get-tuple-element.25.both_ref, f32[1024,128]{1,0:T(8,128)} %get-tuple-element.26.after_ref.refs_6_.inv_ref, f32[1024,128]{1,0:T(8,128)} %get-tuple-element.37.coef_ref, ...), custom_call_target="tpu_custom_call" | custom-call | flops 8589934592 | bytes 29360128 | tf_op jit(solution)/shard_map/backward/pallas_call | solution.py:298
  109.2 10.4 %all-to-all-done.1.refs_0_ = bf16[64,32,1024]{2,1,0:T(8,128)(2,1)} async-done(((bf16[64,32,1024]{2,1,0:T(8,128)(2,1)}), bf16[64,32,1024]{2,1,0:T(8,128)(2,1)}, u32[]{:S(2)}, u32[]{:S(2)}) %all-to-all-start.1) | async-done | bytes 4194336 | tf_op jit(solution)/shard_map/all_to_all | solution.py:436
  119.6 4.1 %total.1 = (bf16[32,1024]{1,0:T(8,128)(2,1)}, f32[128,128]{1,0:T(8,128)}) custom-call(bf16[64,32,1024]{2,1,0:T(8,128)(2,1)} %all-to-all-done.1.refs_0_, bf16[32,512]{1,0:T(8,128)(2,1)} %get-tuple-element.45.refs_1_, bf16[32,512]{1,0:T(8,128)(2,1)} %get-tuple-element.44.refs_2_, f32[1,128]{1,0:T(1,128)} %reshape_tile.3.refs_3_, ...), custom_call_target="tpu_custom_call" | custom-call | flops 2097152 | bytes 5242880 | tf_op jit(solution)/shard_map/total/pallas_call | solution.py:351
  123.8 1.7 %collective-permute-start.11 = (bf16[32,1024]{1,0:T(8,128)(2,1)}, bf16[32,1024]{1,0:T(8,128)(2,1)S(1)}, u32[]{:S(2)}, u32[]{:S(2)}) collective-permute-start(bf16[32,1024]{1,0:T(8,128)(2,1)} %get-tuple-element.38.mine_ref), channel_id=1, source_target_pairs={{0,1},{1,0},{2,3},{3,2},{4,5},{5,4},{6,7},{7,6},{8,9},{9,8},{10,11... | collective-permute-start | bytes 196616 | tf_op jit(solution)/shard_map/ppermute | solution.py:26
  125.5 2.7 %collective-permute-done.11.got_ref = bf16[32,1024]{1,0:T(8,128)(2,1)S(1)} collective-permute-done((bf16[32,1024]{1,0:T(8,128)(2,1)}, bf16[32,1024]{1,0:T(8,128)(2,1)S(1)}, u32[]{:S(2)}, u32[]{:S(2)}) %collective-permute-start.11) | collective-permute-done | bytes 65568 | tf_op jit(solution)/shard_map/ppermute | solution.py:26
  128.3 0.8 copy-done
  129.3 2.2 %collective-permute-start.13 = (bf16[2,32,1024]{2,1,0:T(8,128)(2,1)S(1)}, bf16[2,32,1024]{2,1,0:T(8,128)(2,1)S(1)}, u32[]{:S(2)}, u32[]{:S(2)}) collective-permute-start(bf16[2,32,1024]{2,1,0:T(8,128)(2,1)S(1)} %pair.1.p0_ref), channel_id=1, source_target_pairs={{0,4},{1,5},{2,6},{3,7},{4,0},{5,1},{6,2},{7,3},{8,12},{9,13},{10,... | collective-permute-start | bytes 393224 | tf_op jit(solution)/shard_map/ppermute | solution.py:26
  131.5 2.3 %collective-permute-start.14 = (bf16[2,32,1024]{2,1,0:T(8,128)(2,1)S(1)}, bf16[2,32,1024]{2,1,0:T(8,128)(2,1)S(1)}, u32[]{:S(2)}, u32[]{:S(2)}) collective-permute-start(bf16[2,32,1024]{2,1,0:T(8,128)(2,1)S(1)} %pair.1.p0_ref), channel_id=1, source_target_pairs={{0,6},{1,7},{2,0},{3,1},{4,2},{5,3},{6,4},{7,5},{8,14},{9,15},{10,... | collective-permute-start | bytes 393224 | tf_op jit(solution)/shard_map/ppermute | solution.py:26
  133.9 22.6 %all_to_all.22 = f32[128,1,128]{2,1,0:T(1,128)S(1)} all-to-all(f32[128,1,128]{2,1,0:T(1,128)} %bitcast.14), channel_id=1, replica_groups=mesh['x'=4,'zh'=2,'c'=2,'y'=4,'zl'=2] {'x','zh','c','y','zl'}, dimensions={0} | all-to-all | bytes 131072 | tf_op jit(solution)/shard_map/all_to_all | solution.py:452
  156.4 0.7 reshape.36
  157.1 1.0 finish.1
  (39 shorter events, 4.1 us)
Async XLA Ops:
  4.3 32.4 %all-to-all-start = ((bf16[4,256,1024]{2,1,0:T(8,128)(2,1)}), bf16[4,256,1024]{2,1,0:T(8,128)(2,1)S(1)}, u32[]{:S(2)}, u32[]{:S(2)}) async-start(bf16[4,256,1024]{2,1,0:T(8,128)(2,1)} %broadcast_in_dim.2.after_ref), calls=%async_computation | async-start | bytes 4194304 | tf_op jit(solution)/shard_map/all_to_all | solution.py:425
  9.1 22.8 %collective-permute-start.2 = (bf16[256,1024]{1,0:T(8,128)(2,1)S(1)}, bf16[256,1024]{1,0:T(8,128)(2,1)S(1)}, u32[]{:S(2)}, u32[]{:S(2)}) collective-permute-start(bf16[256,1024]{1,0:T(8,128)(2,1)S(1)} %constant_dynamic-update-slice_fusion), channel_id=1, source_target_pairs={{0,16},{1,17},{2,18},{3,19},{4,20},{5,21},{6,22},{7,23},{8,24},{9,... | collective-permute-start | bytes 1572872 | tf_op jit(solution)/shard_map/ppermute | solution.py:26
  30.8 16.4 %collective-permute-start = (bf16[4,256,1024]{2,1,0:T(8,128)(2,1)}, bf16[4,256,1024]{2,1,0:T(8,128)(2,1)}, u32[]{:S(2)}, u32[]{:S(2)}) collective-permute-start(bf16[4,256,1024]{2,1,0:T(8,128)(2,1)} %get-tuple-element.27), channel_id=1, source_target_pairs={{0,8},{1,9},{2,10},{3,11},{4,12},{5,13},{6,14},{7,15},{8,0},{9,1},... | collective-permute-start | bytes 6291464 | tf_op jit(solution)/shard_map/ppermute | solution.py:26
  30.9 16.3 %collective-permute-start.1 = (bf16[4,256,1024]{2,1,0:T(8,128)(2,1)}, bf16[4,256,1024]{2,1,0:T(8,128)(2,1)}, u32[]{:S(2)}, u32[]{:S(2)}) collective-permute-start(bf16[4,256,1024]{2,1,0:T(8,128)(2,1)} %get-tuple-element.28), channel_id=1, source_target_pairs={{0,8},{1,9},{2,10},{3,11},{4,12},{5,13},{6,14},{7,15},{8,0},{9,1},... | collective-permute-start | bytes 6291464 | tf_op jit(solution)/shard_map/ppermute | solution.py:26
  31.9 15.3 %copy-start.3 = (bf16[256,1024]{1,0:T(8,128)(2,1)}, bf16[256,1024]{1,0:T(8,128)(2,1)S(1)}, u32[]{:S(2)}) copy-start(bf16[256,1024]{1,0:T(8,128)(2,1)S(1)} %collective-permute-done.2.refs_2_) | copy-start | bytes 1572868
  31.9 21.3 %collective-permute-start.3 = (bf16[256,1024]{1,0:T(8,128)(2,1)S(1)}, bf16[256,1024]{1,0:T(8,128)(2,1)S(1)}, u32[]{:S(2)}, u32[]{:S(2)}) collective-permute-start(bf16[256,1024]{1,0:T(8,128)(2,1)S(1)} %collective-permute-done.2.refs_2_), channel_id=1, source_target_pairs={{0,32},{1,33},{2,34},{3,35},{4,36},{5,37},{6,38},{7,39},{8,40},{9,... | collective-permute-start | bytes 1572872 | tf_op jit(solution)/shard_map/ppermute | solution.py:26
  33.4 19.8 %collective-permute-start.4 = (bf16[256,1024]{1,0:T(8,128)(2,1)S(1)}, bf16[256,1024]{1,0:T(8,128)(2,1)}, u32[]{:S(2)}, u32[]{:S(2)}) collective-permute-start(bf16[256,1024]{1,0:T(8,128)(2,1)S(1)} %collective-permute-done.2.refs_2_), channel_id=1, source_target_pairs={{0,64},{1,65},{2,66},{3,67},{4,68},{5,69},{6,70},{7,71},{8,72},{9,... | collective-permute-start | bytes 1572872 | tf_op jit(solution)/shard_map/ppermute | solution.py:26
  34.1 25.0 %collective-permute-start.5 = (bf16[256,1024]{1,0:T(8,128)(2,1)S(1)}, bf16[256,1024]{1,0:T(8,128)(2,1)}, u32[]{:S(2)}, u32[]{:S(2)}) collective-permute-start(bf16[256,1024]{1,0:T(8,128)(2,1)S(1)} %collective-permute-done.2.refs_2_), channel_id=1, source_target_pairs={{0,96},{1,97},{2,98},{3,99},{4,100},{5,101},{6,102},{7,103},{8,104... | collective-permute-start | bytes 1572872 | tf_op jit(solution)/shard_map/ppermute | solution.py:26
  36.6 1.4 copy-start.1
  53.2 5.8 %copy-start.5 = (bf16[256,1024]{1,0:T(8,128)(2,1)}, bf16[256,1024]{1,0:T(8,128)(2,1)S(1)}, u32[]{:S(2)}) copy-start(bf16[256,1024]{1,0:T(8,128)(2,1)S(1)} %collective-permute-done.3.refs_3_) | copy-start | bytes 1572868
  59.1 8.9 %copy-start.2 = (bf16[4,256,1024]{2,1,0:T(8,128)(2,1)S(1)}, bf16[4,256,1024]{2,1,0:T(8,128)(2,1)}, u32[]{:S(2)}) copy-start(bf16[4,256,1024]{2,1,0:T(8,128)(2,1)} %get-tuple-element.29.refs_0_) | copy-start | bytes 6291460
  59.1 9.5 %copy-start.4 = (bf16[256,1024]{1,0:T(8,128)(2,1)S(1)}, bf16[256,1024]{1,0:T(8,128)(2,1)}, u32[]{:S(2)}) copy-start(bf16[256,1024]{1,0:T(8,128)(2,1)} %get-tuple-element.30.refs_2_) | copy-start | bytes 1572868
  59.1 9.6 %copy-start.6 = (bf16[256,1024]{1,0:T(8,128)(2,1)S(1)}, bf16[256,1024]{1,0:T(8,128)(2,1)}, u32[]{:S(2)}) copy-start(bf16[256,1024]{1,0:T(8,128)(2,1)} %get-tuple-element.31.refs_4_) | copy-start | bytes 1572868
  59.1 60.6 %all-to-all-start.1 = ((bf16[64,32,1024]{2,1,0:T(8,128)(2,1)}), bf16[64,32,1024]{2,1,0:T(8,128)(2,1)}, u32[]{:S(2)}, u32[]{:S(2)}) async-start(bf16[64,32,1024]{2,1,0:T(8,128)(2,1)} %bitcast.12), calls=%async_computation.1 | async-start | bytes 8388608 | tf_op jit(solution)/shard_map/all_to_all | solution.py:436
  68.0 7.4 %collective-permute-start.6 = (bf16[4,256,1024]{2,1,0:T(8,128)(2,1)S(1)}, bf16[4,256,1024]{2,1,0:T(8,128)(2,1)}, u32[]{:S(2)}, u32[]{:S(2)}) collective-permute-start(bf16[4,256,1024]{2,1,0:T(8,128)(2,1)S(1)} %copy-done.2), channel_id=1, source_target_pairs={{0,8},{1,9},{2,10},{3,11},{4,12},{5,13},{6,14},{7,15},{8,0},{9,1},... | collective-permute-start | bytes 6291464 | tf_op jit(solution)/shard_map/ppermute | solution.py:26
  68.1 5.6 %collective-permute-start.10 = (bf16[256,1024]{1,0:T(8,128)(2,1)}, bf16[256,1024]{1,0:T(8,128)(2,1)}, u32[]{:S(2)}, u32[]{:S(2)}) collective-permute-start(bf16[256,1024]{1,0:T(8,128)(2,1)} %get-tuple-element.33.refs_8_), channel_id=1, source_target_pairs={{0,8},{1,9},{2,10},{3,11},{4,12},{5,13},{6,14},{7,15},{8,0},{9,1},... | collective-permute-start | bytes 1572872 | tf_op jit(solution)/shard_map/ppermute | solution.py:26
  68.6 6.0 %collective-permute-start.7 = (bf16[256,1024]{1,0:T(8,128)(2,1)S(1)}, bf16[256,1024]{1,0:T(8,128)(2,1)}, u32[]{:S(2)}, u32[]{:S(2)}) collective-permute-start(bf16[256,1024]{1,0:T(8,128)(2,1)S(1)} %copy-done.4), channel_id=1, source_target_pairs={{0,8},{1,9},{2,10},{3,11},{4,12},{5,13},{6,14},{7,15},{8,0},{9,1},... | collective-permute-start | bytes 1572872 | tf_op jit(solution)/shard_map/ppermute | solution.py:26
  68.7 6.7 %collective-permute-start.8 = (bf16[256,1024]{1,0:T(8,128)(2,1)S(1)}, bf16[256,1024]{1,0:T(8,128)(2,1)}, u32[]{:S(2)}, u32[]{:S(2)}) collective-permute-start(bf16[256,1024]{1,0:T(8,128)(2,1)S(1)} %copy-done.6), channel_id=1, source_target_pairs={{0,8},{1,9},{2,10},{3,11},{4,12},{5,13},{6,14},{7,15},{8,0},{9,1},... | collective-permute-start | bytes 1572872 | tf_op jit(solution)/shard_map/ppermute | solution.py:26
  69.1 6.3 %collective-permute-start.9 = (bf16[256,1024]{1,0:T(8,128)(2,1)}, bf16[256,1024]{1,0:T(8,128)(2,1)}, u32[]{:S(2)}, u32[]{:S(2)}) collective-permute-start(bf16[256,1024]{1,0:T(8,128)(2,1)} %get-tuple-element.32.refs_6_), channel_id=1, source_target_pairs={{0,8},{1,9},{2,10},{3,11},{4,12},{5,13},{6,14},{7,15},{8,0},{9,1},... | collective-permute-start | bytes 1572872 | tf_op jit(solution)/shard_map/ppermute | solution.py:26
  123.8 4.5 %collective-permute-start.11 = (bf16[32,1024]{1,0:T(8,128)(2,1)}, bf16[32,1024]{1,0:T(8,128)(2,1)S(1)}, u32[]{:S(2)}, u32[]{:S(2)}) collective-permute-start(bf16[32,1024]{1,0:T(8,128)(2,1)} %get-tuple-element.38.mine_ref), channel_id=1, source_target_pairs={{0,1},{1,0},{2,3},{3,2},{4,5},{5,4},{6,7},{7,6},{8,9},{9,8},{10,11... | collective-permute-start | bytes 196616 | tf_op jit(solution)/shard_map/ppermute | solution.py:26
  128.3 0.8 copy-start
  129.1 28.0 %collective-permute-start.12 = (bf16[2,32,1024]{2,1,0:T(8,128)(2,1)S(1)}, bf16[2,32,1024]{2,1,0:T(8,128)(2,1)S(1)}, u32[]{:S(2)}, u32[]{:S(2)}) collective-permute-start(bf16[2,32,1024]{2,1,0:T(8,128)(2,1)S(1)} %pair.1.p0_ref), channel_id=1, source_target_pairs={{0,2},{1,3},{2,4},{3,5},{4,6},{5,7},{6,0},{7,1},{8,10},{9,11},{10,... | collective-permute-start | bytes 393224 | tf_op jit(solution)/shard_map/ppermute | solution.py:26
  129.3 27.8 %collective-permute-start.13 = (bf16[2,32,1024]{2,1,0:T(8,128)(2,1)S(1)}, bf16[2,32,1024]{2,1,0:T(8,128)(2,1)S(1)}, u32[]{:S(2)}, u32[]{:S(2)}) collective-permute-start(bf16[2,32,1024]{2,1,0:T(8,128)(2,1)S(1)} %pair.1.p0_ref), channel_id=1, source_target_pairs={{0,4},{1,5},{2,6},{3,7},{4,0},{5,1},{6,2},{7,3},{8,12},{9,13},{10,... | collective-permute-start | bytes 393224 | tf_op jit(solution)/shard_map/ppermute | solution.py:26
  131.5 25.6 %collective-permute-start.14 = (bf16[2,32,1024]{2,1,0:T(8,128)(2,1)S(1)}, bf16[2,32,1024]{2,1,0:T(8,128)(2,1)S(1)}, u32[]{:S(2)}, u32[]{:S(2)}) collective-permute-start(bf16[2,32,1024]{2,1,0:T(8,128)(2,1)S(1)} %pair.1.p0_ref), channel_id=1, source_target_pairs={{0,6},{1,7},{2,0},{3,1},{4,2},{5,3},{6,4},{7,5},{8,14},{9,15},{10,... | collective-permute-start | bytes 393224 | tf_op jit(solution)/shard_map/ppermute | solution.py:26

commit v6 on v5

--- a/solution.py
+++ b/solution.py
@@ -63,16 +63,10 @@
 
     @pl.when(i < 4)
     def _():
-        def rows(r, carry):
-            at = pl.ds(pl.multiple_of(r * 16, 16), 16)
-            v = tok_ref[at, :].astype(F32)
-            inv = lax.rsqrt(jnp.mean(v * v, axis=1, keepdims=True) + 1e-05)
-            inv_ref[at, :] = jnp.broadcast_to(inv, (16, HEAD))
-            to = pl.ds(pl.multiple_of(i * tb + r * 16, 16), 16)
-            normed_ref[to, :] = (tok_ref[at, :].astype(F32) * inv * gain_ref[...]).astype(BF16)
-            return carry
-
-        lax.fori_loop(0, tb // 16, rows, 0, unroll=2)
+        v = tok_ref[...].astype(F32)
+        inv = lax.rsqrt(jnp.mean(v * v, axis=1, keepdims=True) + 1e-05)
+        inv_ref[...] = jnp.broadcast_to(inv, inv_ref.shape)
+        normed_ref[pl.ds(pl.multiple_of(i * tb, tb), tb), :] = (v * inv * gain_ref[...]).astype(BF16)
         here = pl.ds(pl.multiple_of(i * tb, tb), tb)
         back = turn(kc_ref[...].astype(F32), cos_ref[...], sin_ref[...], -1.0).astype(BF16)
         both_ref[here, :feats] = back
@@ -344,7 +338,7 @@
         gain_out_ref[...] = jnp.broadcast_to(line, gain_out_ref.shape)
 
 
-def total(count, got, key_rows, value_rows, gain_rows, after):
+def total(count, copies, got, key_rows, value_rows, gain_rows, after):
     sources, rows, width = got.shape
     feats = key_rows.shape[1]
     fixed = lambda shape: pl.BlockSpec(shape, lambda g: (0,) * len(shape))
@@ -358,8 +352,8 @@
             fixed((1, HEAD)),
             UNREAD,
         ],
-        out_specs=[fixed((rows, width)), fixed((count, HEAD))],
-        out_shape=[pltpu.HBM((rows, width), BF16), pltpu.HBM((count, HEAD), F32)],
+        out_specs=[fixed((rows, width)), fixed((copies, HEAD))],
+        out_shape=[pltpu.HBM((rows, width), BF16), pltpu.HBM((copies, HEAD), F32)],
         scratch_shapes=[pltpu.VMEM((rows, width), F32)],
         compiler_params=params(56),
         cost_estimate=pl.CostEstimate(flops=2 * MIB, bytes_accessed=5 * MIB, transcendentals=0),
@@ -448,12 +442,16 @@
     row = (y * 2 + zl) * 32
     key_rows, value_rows_of = (lax.dynamic_slice(w, (row, 0), (32, feats)) for w in (key_weight, value_weight))
     own_gain = lax.dynamic_slice(norm_gain, ((x * 4 + zh * 2 + core) * 256 + row,), (32,))
-    mean, gain_rows = total(count, got, key_rows, value_rows_of, jnp.tile(own_gain, 4).reshape(1, HEAD), input_grad)
-    gain_rows = lax.all_to_all(gain_rows, AXES, 0, 0, tiled=True)
+    mean, gain_rows = total(count, count // 2, got, key_rows, value_rows_of, jnp.tile(own_gain, 4).reshape(1, HEAD), input_grad)
+    gain_rows = lax.all_to_all(gain_rows, ("x", "zh", "y", "zl"), 0, 0, tiled=True)
+    gain_rows = gain_rows.reshape(4, 2, 8, HEAD)[..., :32]
+    gain_other = to_core(gain_rows)
+    by_core = lambda mine: jnp.where(core == mine, gain_rows, gain_other)
+    gain_grad = jnp.stack([by_core(0), by_core(1)], axis=2).reshape(width)
     pieces = pair(zl, mean, send(mean, lambda x, y, z, c: (x, y, z ^ 1, c)))
     pieces = [pieces] + [send(pieces, lambda x, y, z, c, d=d: (x, y + d, z, c)) for d in (1, 2, 3)]
     key_grad, value_grad = finish(y, pieces)
-    return rotated_keys, value_rows, input_grad, key_grad, value_grad, gain_rows[:, :32].reshape(width)
+    return rotated_keys, value_rows, input_grad, key_grad, value_grad, gain_grad
 
 
 def solution(mesh):

time: 161 us -> 159 us (0.988)
  blocking collectives: 22.6 us -> 18.1 us
  waiting for transfers between devices: 21.2 us -> 24.2 us
  Pallas kernels: 71.6 us -> 69.9 us
    all_to_all x1, blocking collectives: 22.6 us -> 18.1 us  [shards(): lax.all_to_all(gain_rows, ('x', 'zh', 'y', 'zl'), 0, 0, tiled=True)]
    ppermute x15 -> x16, waiting for transfers between devices: 10.8 us -> 13.9 us  [send(): return lax.ppermute(value, AXES, pairs)]
    pallas_call x1, Pallas kernels: 17.3 us -> 15.6 us  [norm_and_terms(): pl.pallas_call(norm_kernel, grid_spec=pltpu.PrefetchScalarGridSpec(num_sc...]
    ppermute x15 -> x16, starting transfers between devices: 16.8 us -> 16.8 us  [send(): return lax.ppermute(value, AXES, pairs)]
  transfers between devices with their start and end apart: 17 -> 18, of which waited for: 6 -> 7; matrix products, arithmetic and copies ran while one was open for 4% -> 4% of each run, Pallas kernels for 42% -> 41%
where the time goes in v6:
time: 159 us; the launch traced here: 156 us
  Pallas kernels  69.9 us (44%)
  starting transfers between devices  31.9 us (20%)
  waiting for transfers between devices  24.2 us (15%)
  blocking collectives  18.1 us (11%)
  local copies, waits for them, and re-layouts  9.42 us (6%)
  other arithmetic  2.31 us (1%)
    all_to_all x1, blocking collectives, shards(): lax.all_to_all(gain_rows, ('x', 'zh', 'y', 'zl'), 0, 0, tiled=True)  18.1 us
    pallas_call x1, Pallas kernels, backward(): pl.pallas_call(backward_kernel, grid_spec=pltpu.PrefetchScalarGridSpec(nu...  17.7 us
    ppermute x16, starting transfers between devices, send(): return lax.ppermute(value, AXES, pairs)  16.8 us
    pallas_call x1, Pallas kernels, forward(): pl.pallas_call(forward_kernel, grid_spec=pltpu.PrefetchScalarGridSpec(num...  16.2 us
    pallas_call x1, Pallas kernels, norm_and_terms(): pl.pallas_call(norm_kernel, grid_spec=pltpu.PrefetchScalarGridSpec(num_sc...  15.6 us
    ppermute x16, waiting for transfers between devices, send(): return lax.ppermute(value, AXES, pairs)  13.9 us
    all_to_all x1, starting transfers between devices, shards(): lax.all_to_all(terms.reshape(64, 32, 2 * feats), ('x', 'zh', 'y', 'zl'),...  10.3 us
    all_to_all x1, waiting for transfers between devices, shards(): lax.all_to_all(terms.reshape(64, 32, 2 * feats), ('x', 'zh', 'y', 'zl'),...  10.3 us
  transfers between devices with their start and end apart: 18, of which 7 were waited for; matrix products, arithmetic and copies ran while one was open for 4% of the time, Pallas kernels for 41%

profile of v6, /device:TPU:2, one launch (start us, length us, event | category | flops | bytes accessed | tf_op | source)
XLA Modules:
  0.0 156.5 jit_solution(10639816989156441002)
XLA Ops:
  0.6 1.0 constant_dynamic-update-slice_fusion.1
  1.6 1.0 constant_dynamic-update-slice_fusion
  2.6 1.7 %broadcast_in_dim.2.after_ref = bf16[4,256,1024]{2,1,0:T(8,128)(2,1)} broadcast(bf16[256,1024]{1,0:T(8,128)(2,1)S(1)} %constant_dynamic-update-slice_fusion), dimensions={1,2} | broadcast | bytes 2621440 | tf_op jit(solution)/shard_map/broadcast_in_dim | solution.py:418
  4.3 4.8 %all-to-all-start = ((bf16[4,256,1024]{2,1,0:T(8,128)(2,1)}), bf16[4,256,1024]{2,1,0:T(8,128)(2,1)S(1)}, u32[]{:S(2)}, u32[]{:S(2)}) async-start(bf16[4,256,1024]{2,1,0:T(8,128)(2,1)} %broadcast_in_dim.2.after_ref), calls=%async_computation | async-start | bytes 4194304 | tf_op jit(solution)/shard_map/all_to_all | solution.py:419
  9.1 3.9 %collective-permute-start.2 = (bf16[256,1024]{1,0:T(8,128)(2,1)S(1)}, bf16[256,1024]{1,0:T(8,128)(2,1)S(1)}, u32[]{:S(2)}, u32[]{:S(2)}) collective-permute-start(bf16[256,1024]{1,0:T(8,128)(2,1)S(1)} %constant_dynamic-update-slice_fusion), channel_id=1, source_target_pairs={{0,16},{1,17},{2,18},{3,19},{4,20},{5,21},{6,22},{7,23},{8,24},{9,... | collective-permute-start | bytes 1572872 | tf_op jit(solution)/shard_map/ppermute | solution.py:26
  13.5 15.6 %norm_and_terms.1 = (bf16[1024,1024]{1,0:T(8,128)(2,1)}, f32[1024,128]{1,0:T(8,128)}, bf16[1024,4096]{1,0:T(8,128)(2,1)}, bf16[4,256,1024]{2,1,0:T(8,128)(2,1)}, bf16[4,256,1024]{2,1,0:T(8,128)(2,1)}) custom-call(s32[8]{0:T(128)} %add_subtract_fusion.order_ref, bf16[1024,4096]{1,0:T(8,128)(2,1)} %tok_ref.3, f32[1,4096]{1,0:T(1,128)} %bitcast.24, ...), custom_call_target="tpu_custom_call" | custom-call | flops 10485760000 | bytes 20971520 | tf_op jit(solution)/shard_map/norm_and_terms/pallas_call | solution.py:100
  30.2 1.5 collective-permute-start.3
  31.7 0.7 collective-permute-start.4
  32.4 2.5 %collective-permute-start.5 = (bf16[256,1024]{1,0:T(8,128)(2,1)S(1)}, bf16[256,1024]{1,0:T(8,128)(2,1)}, u32[]{:S(2)}, u32[]{:S(2)}) collective-permute-start(bf16[256,1024]{1,0:T(8,128)(2,1)S(1)} %collective-permute-done.2.refs_2_), channel_id=1, source_target_pairs={{0,96},{1,97},{2,98},{3,99},{4,100},{5,101},{6,102},{7,103},{8,104... | collective-permute-start | bytes 1572872 | tf_op jit(solution)/shard_map/ppermute | solution.py:26
  35.0 1.4 copy-done.1
  36.4 9.2 %own_terms.1.own_ref = bf16[8,256,1024]{2,1,0:T(8,128)(2,1)} custom-call(s32[8]{0:T(128)} %fusion.4.order_ref, bf16[1024,4096]{1,0:T(8,128)(2,1)} %get-tuple-element.24.n0_ref.n1_ref.normed_ref, bf16[1024,4096]{1,0:T(8,128)(2,1)} %get-tuple-element.24.n0_ref.n1_ref.normed_ref, bf16[1024,1024]{1,0:T(8,128)(2,1)} %get-tuple-element.25.both_ref, ...), custom_call_target="tpu_custom_call" | custom-call | flops 31457280000 | tf_op jit(solution)/shard_map/own_terms/pallas_call | solution.py:147
  45.6 6.0 %add.81.refs_0_ = bf16[8,256,1024]{2,1,0:T(8,128)(2,1)} custom-call(bf16[8,256,1024]{2,1,0:T(8,128)(2,1)} %own_terms.1.own_ref, bf16[4,256,1024]{2,1,0:T(8,128)(2,1)} %collective-permute-done.got0_ref, bf16[4,256,1024]{2,1,0:T(8,128)(2,1)} %collective-permute-done.1.got1_ref, f32[1024,128]{1,0:T(8,128)} %get-tuple-element.26.after_ref.refs_6_.inv_ref), custom_call_target="tpu_custom_call" | custom-call | tf_op jit(solution)/shard_map/add/pallas_call | solution.py:172
  51.6 5.8 %collective-permute-done.5.refs_5_ = bf16[256,1024]{1,0:T(8,128)(2,1)} collective-permute-done((bf16[256,1024]{1,0:T(8,128)(2,1)S(1)}, bf16[256,1024]{1,0:T(8,128)(2,1)}, u32[]{:S(2)}, u32[]{:S(2)}) %collective-permute-start.5) | collective-permute-done | bytes 524320 | tf_op jit(solution)/shard_map/ppermute | solution.py:26
  57.4 10.3 %all-to-all-start.1 = ((bf16[64,32,1024]{2,1,0:T(8,128)(2,1)}), bf16[64,32,1024]{2,1,0:T(8,128)(2,1)}, u32[]{:S(2)}, u32[]{:S(2)}) async-start(bf16[64,32,1024]{2,1,0:T(8,128)(2,1)} %bitcast.20), calls=%async_computation.1 | async-start | bytes 8388608 | tf_op jit(solution)/shard_map/all_to_all | solution.py:430
  68.9 0.8 dynamic_slice.11
  69.6 0.7 reshape_tile.3.refs_3_
  70.3 0.7 pad_add_fusion.place_ref
  71.6 1.4 constant_dynamic-slice_fusion
  73.4 0.9 collective-permute-done.7.refs_3_
  74.3 0.7 collective-permute-done.8.refs_5_
  75.1 16.2 %forward.1 = (bf16[1024,512]{1,0:T(8,128)(2,1)}, bf16[1024,512]{1,0:T(8,128)(2,1)}, f32[1024,128]{1,0:T(8,128)}) custom-call(s32[3]{0:T(128)} %pad_add_fusion.place_ref, bf16[1024,4096]{1,0:T(8,128)(2,1)} %get-tuple-element.24.n0_ref.n1_ref.normed_ref, bf16[1024,1024]{1,0:T(8,128)(2,1)} %get-tuple-element.25.both_ref, ...), custom_call_target="tpu_custom_call" | custom-call | flops 8589934592 | bytes 20971520 | tf_op jit(solution)/shard_map/forward/pallas_call | solution.py:248
  91.3 17.7 %backward.1.refs_4_ = bf16[1024,4096]{1,0:T(8,128)(2,1)} custom-call(s32[9]{0:T(128)} %pad_add_fusion.1.place_ref, bf16[1024,4096]{1,0:T(8,128)(2,1)} %tok_ref.3, bf16[1024,1024]{1,0:T(8,128)(2,1)} %get-tuple-element.25.both_ref, f32[1024,128]{1,0:T(8,128)} %get-tuple-element.26.after_ref.refs_6_.inv_ref, f32[1024,128]{1,0:T(8,128)} %get-tuple-element.37.coef_ref, ...), custom_call_target="tpu_custom_call" | custom-call | flops 8589934592 | bytes 29360128 | tf_op jit(solution)/shard_map/backward/pallas_call | solution.py:292
  108.9 10.3 %all-to-all-done.1.refs_0_ = bf16[64,32,1024]{2,1,0:T(8,128)(2,1)} async-done(((bf16[64,32,1024]{2,1,0:T(8,128)(2,1)}), bf16[64,32,1024]{2,1,0:T(8,128)(2,1)}, u32[]{:S(2)}, u32[]{:S(2)}) %all-to-all-start.1) | async-done | bytes 4194336 | tf_op jit(solution)/shard_map/all_to_all | solution.py:430
  119.2 4.1 %total.1 = (bf16[32,1024]{1,0:T(8,128)(2,1)}, f32[64,128]{1,0:T(8,128)}) custom-call(bf16[64,32,1024]{2,1,0:T(8,128)(2,1)} %all-to-all-done.1.refs_0_, bf16[32,512]{1,0:T(8,128)(2,1)} %get-tuple-element.47.refs_1_, bf16[32,512]{1,0:T(8,128)(2,1)} %get-tuple-element.46.refs_2_, f32[1,128]{1,0:T(1,128)} %reshape_tile.3.refs_3_, bf16[1024,4096]{1,0:T(8,128)(2,1)} %backward.1.refs_4_), custom_call_target="tpu_custom_call" | custom-call | flops 2097152 | bytes 5242880 | tf_op jit(solution)/shard_map/total/pallas_call | solution.py:345
  123.3 2.6 %collective-permute-start.11 = (bf16[32,1024]{1,0:T(8,128)(2,1)}, bf16[32,1024]{1,0:T(8,128)(2,1)S(1)}, u32[]{:S(2)}, u32[]{:S(2)}) collective-permute-start(bf16[32,1024]{1,0:T(8,128)(2,1)} %get-tuple-element.38.mine_ref), channel_id=1, source_target_pairs={{0,1},{1,0},{2,3},{3,2},{4,5},{5,4},{6,7},{7,6},{8,9},{9,8},{10,11... | collective-permute-start | bytes 196616 | tf_op jit(solution)/shard_map/ppermute | solution.py:26
  125.9 18.1 %all_to_all.19 = f32[64,1,128]{2,1,0:T(1,128)S(1)} all-to-all(f32[64,1,128]{2,1,0:T(1,128)} %bitcast.23), channel_id=1, replica_groups=mesh['x'=4,'zh'=2,'c'=2,'y'=4,'zl'=2] {'x','zh','y','zl'}, dimensions={0} | all-to-all | bytes 65536 | tf_op jit(solution)/shard_map/all_to_all | solution.py:446
  144.0 0.8 copy-done
  145.5 2.2 %collective-permute-start.13 = (bf16[2,32,1024]{2,1,0:T(8,128)(2,1)S(1)}, bf16[2,32,1024]{2,1,0:T(8,128)(2,1)S(1)}, u32[]{:S(2)}, u32[]{:S(2)}) collective-permute-start(bf16[2,32,1024]{2,1,0:T(8,128)(2,1)S(1)} %pair.1.p0_ref), channel_id=1, source_target_pairs={{0,4},{1,5},{2,6},{3,7},{4,0},{5,1},{6,2},{7,3},{8,12},{9,13},{10,... | collective-permute-start | bytes 393224 | tf_op jit(solution)/shard_map/ppermute | solution.py:26
  147.7 1.0 collective-permute-start.14
  148.7 0.7 reshape.41
  149.4 5.4 %collective-permute-done.12.p1_ref = bf16[2,32,1024]{2,1,0:T(8,128)(2,1)S(1)} collective-permute-done((bf16[2,32,1024]{2,1,0:T(8,128)(2,1)S(1)}, bf16[2,32,1024]{2,1,0:T(8,128)(2,1)S(1)}, u32[]{:S(2)}, u32[]{:S(2)}) %collective-permute-start.12) | collective-permute-done | bytes 131104 | tf_op jit(solution)/shard_map/ppermute | solution.py:26
  155.5 1.0 finish.1
  (43 shorter events, 5.2 us)
Async XLA Ops:
  4.3 30.7 %all-to-all-start = ((bf16[4,256,1024]{2,1,0:T(8,128)(2,1)}), bf16[4,256,1024]{2,1,0:T(8,128)(2,1)S(1)}, u32[]{:S(2)}, u32[]{:S(2)}) async-start(bf16[4,256,1024]{2,1,0:T(8,128)(2,1)} %broadcast_in_dim.2.after_ref), calls=%async_computation | async-start | bytes 4194304 | tf_op jit(solution)/shard_map/all_to_all | solution.py:419
  9.1 21.1 %collective-permute-start.2 = (bf16[256,1024]{1,0:T(8,128)(2,1)S(1)}, bf16[256,1024]{1,0:T(8,128)(2,1)S(1)}, u32[]{:S(2)}, u32[]{:S(2)}) collective-permute-start(bf16[256,1024]{1,0:T(8,128)(2,1)S(1)} %constant_dynamic-update-slice_fusion), channel_id=1, source_target_pairs={{0,16},{1,17},{2,18},{3,19},{4,20},{5,21},{6,22},{7,23},{8,24},{9,... | collective-permute-start | bytes 1572872 | tf_op jit(solution)/shard_map/ppermute | solution.py:26
  29.1 16.4 %collective-permute-start = (bf16[4,256,1024]{2,1,0:T(8,128)(2,1)}, bf16[4,256,1024]{2,1,0:T(8,128)(2,1)}, u32[]{:S(2)}, u32[]{:S(2)}) collective-permute-start(bf16[4,256,1024]{2,1,0:T(8,128)(2,1)} %get-tuple-element.27), channel_id=1, source_target_pairs={{0,8},{1,9},{2,10},{3,11},{4,12},{5,13},{6,14},{7,15},{8,0},{9,1},... | collective-permute-start | bytes 6291464 | tf_op jit(solution)/shard_map/ppermute | solution.py:26
  29.2 16.3 %collective-permute-start.1 = (bf16[4,256,1024]{2,1,0:T(8,128)(2,1)}, bf16[4,256,1024]{2,1,0:T(8,128)(2,1)}, u32[]{:S(2)}, u32[]{:S(2)}) collective-permute-start(bf16[4,256,1024]{2,1,0:T(8,128)(2,1)} %get-tuple-element.28), channel_id=1, source_target_pairs={{0,8},{1,9},{2,10},{3,11},{4,12},{5,13},{6,14},{7,15},{8,0},{9,1},... | collective-permute-start | bytes 6291464 | tf_op jit(solution)/shard_map/ppermute | solution.py:26
  30.2 15.3 %copy-start.3 = (bf16[256,1024]{1,0:T(8,128)(2,1)}, bf16[256,1024]{1,0:T(8,128)(2,1)S(1)}, u32[]{:S(2)}) copy-start(bf16[256,1024]{1,0:T(8,128)(2,1)S(1)} %collective-permute-done.2.refs_2_) | copy-start | bytes 1572868
  30.2 21.3 %collective-permute-start.3 = (bf16[256,1024]{1,0:T(8,128)(2,1)S(1)}, bf16[256,1024]{1,0:T(8,128)(2,1)S(1)}, u32[]{:S(2)}, u32[]{:S(2)}) collective-permute-start(bf16[256,1024]{1,0:T(8,128)(2,1)S(1)} %collective-permute-done.2.refs_2_), channel_id=1, source_target_pairs={{0,32},{1,33},{2,34},{3,35},{4,36},{5,37},{6,38},{7,39},{8,40},{9,... | collective-permute-start | bytes 1572872 | tf_op jit(solution)/shard_map/ppermute | solution.py:26
  31.7 19.9 %collective-permute-start.4 = (bf16[256,1024]{1,0:T(8,128)(2,1)S(1)}, bf16[256,1024]{1,0:T(8,128)(2,1)}, u32[]{:S(2)}, u32[]{:S(2)}) collective-permute-start(bf16[256,1024]{1,0:T(8,128)(2,1)S(1)} %collective-permute-done.2.refs_2_), channel_id=1, source_target_pairs={{0,64},{1,65},{2,66},{3,67},{4,68},{5,69},{6,70},{7,71},{8,72},{9,... | collective-permute-start | bytes 1572872 | tf_op jit(solution)/shard_map/ppermute | solution.py:26
  32.4 25.0 %collective-permute-start.5 = (bf16[256,1024]{1,0:T(8,128)(2,1)S(1)}, bf16[256,1024]{1,0:T(8,128)(2,1)}, u32[]{:S(2)}, u32[]{:S(2)}) collective-permute-start(bf16[256,1024]{1,0:T(8,128)(2,1)S(1)} %collective-permute-done.2.refs_2_), channel_id=1, source_target_pairs={{0,96},{1,97},{2,98},{3,99},{4,100},{5,101},{6,102},{7,103},{8,104... | collective-permute-start | bytes 1572872 | tf_op jit(solution)/shard_map/ppermute | solution.py:26
  35.0 1.4 copy-start.1
  51.6 5.8 %copy-start.5 = (bf16[256,1024]{1,0:T(8,128)(2,1)}, bf16[256,1024]{1,0:T(8,128)(2,1)S(1)}, u32[]{:S(2)}) copy-start(bf16[256,1024]{1,0:T(8,128)(2,1)S(1)} %collective-permute-done.3.refs_3_) | copy-start | bytes 1572868
  57.4 10.3 %copy-start.2 = (bf16[4,256,1024]{2,1,0:T(8,128)(2,1)S(1)}, bf16[4,256,1024]{2,1,0:T(8,128)(2,1)}, u32[]{:S(2)}) copy-start(bf16[4,256,1024]{2,1,0:T(8,128)(2,1)} %get-tuple-element.29.refs_0_) | copy-start | bytes 6291460
  57.4 10.9 %copy-start.4 = (bf16[256,1024]{1,0:T(8,128)(2,1)S(1)}, bf16[256,1024]{1,0:T(8,128)(2,1)}, u32[]{:S(2)}) copy-start(bf16[256,1024]{1,0:T(8,128)(2,1)} %get-tuple-element.30.refs_2_) | copy-start | bytes 1572868
  57.4 11.0 %copy-start.6 = (bf16[256,1024]{1,0:T(8,128)(2,1)S(1)}, bf16[256,1024]{1,0:T(8,128)(2,1)}, u32[]{:S(2)}) copy-start(bf16[256,1024]{1,0:T(8,128)(2,1)} %get-tuple-element.31.refs_4_) | copy-start | bytes 1572868
  57.4 61.8 %all-to-all-start.1 = ((bf16[64,32,1024]{2,1,0:T(8,128)(2,1)}), bf16[64,32,1024]{2,1,0:T(8,128)(2,1)}, u32[]{:S(2)}, u32[]{:S(2)}) async-start(bf16[64,32,1024]{2,1,0:T(8,128)(2,1)} %bitcast.20), calls=%async_computation.1 | async-start | bytes 8388608 | tf_op jit(solution)/shard_map/all_to_all | solution.py:430
  67.7 7.4 %collective-permute-start.6 = (bf16[4,256,1024]{2,1,0:T(8,128)(2,1)S(1)}, bf16[4,256,1024]{2,1,0:T(8,128)(2,1)}, u32[]{:S(2)}, u32[]{:S(2)}) collective-permute-start(bf16[4,256,1024]{2,1,0:T(8,128)(2,1)S(1)} %copy-done.2), channel_id=1, source_target_pairs={{0,8},{1,9},{2,10},{3,11},{4,12},{5,13},{6,14},{7,15},{8,0},{9,1},... | collective-permute-start | bytes 6291464 | tf_op jit(solution)/shard_map/ppermute | solution.py:26
  67.8 5.6 %collective-permute-start.10 = (bf16[256,1024]{1,0:T(8,128)(2,1)}, bf16[256,1024]{1,0:T(8,128)(2,1)}, u32[]{:S(2)}, u32[]{:S(2)}) collective-permute-start(bf16[256,1024]{1,0:T(8,128)(2,1)} %get-tuple-element.33.refs_8_), channel_id=1, source_target_pairs={{0,8},{1,9},{2,10},{3,11},{4,12},{5,13},{6,14},{7,15},{8,0},{9,1},... | collective-permute-start | bytes 1572872 | tf_op jit(solution)/shard_map/ppermute | solution.py:26
  68.3 6.0 %collective-permute-start.7 = (bf16[256,1024]{1,0:T(8,128)(2,1)S(1)}, bf16[256,1024]{1,0:T(8,128)(2,1)}, u32[]{:S(2)}, u32[]{:S(2)}) collective-permute-start(bf16[256,1024]{1,0:T(8,128)(2,1)S(1)} %copy-done.4), channel_id=1, source_target_pairs={{0,8},{1,9},{2,10},{3,11},{4,12},{5,13},{6,14},{7,15},{8,0},{9,1},... | collective-permute-start | bytes 1572872 | tf_op jit(solution)/shard_map/ppermute | solution.py:26
  68.4 6.7 %collective-permute-start.8 = (bf16[256,1024]{1,0:T(8,128)(2,1)S(1)}, bf16[256,1024]{1,0:T(8,128)(2,1)}, u32[]{:S(2)}, u32[]{:S(2)}) collective-permute-start(bf16[256,1024]{1,0:T(8,128)(2,1)S(1)} %copy-done.6), channel_id=1, source_target_pairs={{0,8},{1,9},{2,10},{3,11},{4,12},{5,13},{6,14},{7,15},{8,0},{9,1},... | collective-permute-start | bytes 1572872 | tf_op jit(solution)/shard_map/ppermute | solution.py:26
  68.8 6.3 %collective-permute-start.9 = (bf16[256,1024]{1,0:T(8,128)(2,1)}, bf16[256,1024]{1,0:T(8,128)(2,1)}, u32[]{:S(2)}, u32[]{:S(2)}) collective-permute-start(bf16[256,1024]{1,0:T(8,128)(2,1)} %get-tuple-element.32.refs_6_), channel_id=1, source_target_pairs={{0,8},{1,9},{2,10},{3,11},{4,12},{5,13},{6,14},{7,15},{8,0},{9,1},... | collective-permute-start | bytes 1572872 | tf_op jit(solution)/shard_map/ppermute | solution.py:26
  123.3 20.7 %collective-permute-start.11 = (bf16[32,1024]{1,0:T(8,128)(2,1)}, bf16[32,1024]{1,0:T(8,128)(2,1)S(1)}, u32[]{:S(2)}, u32[]{:S(2)}) collective-permute-start(bf16[32,1024]{1,0:T(8,128)(2,1)} %get-tuple-element.38.mine_ref), channel_id=1, source_target_pairs={{0,1},{1,0},{2,3},{3,2},{4,5},{5,4},{6,7},{7,6},{8,9},{9,8},{10,11... | collective-permute-start | bytes 196616 | tf_op jit(solution)/shard_map/ppermute | solution.py:26
  144.0 4.7 %collective-permute-start.15 = (f32[4,2,8,32]{3,2,1,0:T(8,128)S(1)}, f32[4,2,8,32]{3,2,1,0:T(8,128)S(1)}, u32[]{:S(2)}, u32[]{:S(2)}) collective-permute-start(f32[4,2,8,32]{3,2,1,0:T(8,128)S(1)} %bitcast.21), channel_id=1, source_target_pairs={{0,8},{1,9},{2,10},{3,11},{4,12},{5,13},{6,14},{7,15},{8,0},{9,1},... | collective-permute-start | bytes 24584 | tf_op jit(solution)/shard_map/ppermute | solution.py:26
  144.0 0.8 copy-start
  144.8 10.0 %collective-permute-start.12 = (bf16[2,32,1024]{2,1,0:T(8,128)(2,1)S(1)}, bf16[2,32,1024]{2,1,0:T(8,128)(2,1)S(1)}, u32[]{:S(2)}, u32[]{:S(2)}) collective-permute-start(bf16[2,32,1024]{2,1,0:T(8,128)(2,1)S(1)} %pair.1.p0_ref), channel_id=1, source_target_pairs={{0,2},{1,3},{2,4},{3,5},{4,6},{5,7},{6,0},{7,1},{8,10},{9,11},{10,... | collective-permute-start | bytes 393224 | tf_op jit(solution)/shard_map/ppermute | solution.py:26
  145.5 9.4 %collective-permute-start.13 = (bf16[2,32,1024]{2,1,0:T(8,128)(2,1)S(1)}, bf16[2,32,1024]{2,1,0:T(8,128)(2,1)S(1)}, u32[]{:S(2)}, u32[]{:S(2)}) collective-permute-start(bf16[2,32,1024]{2,1,0:T(8,128)(2,1)S(1)} %pair.1.p0_ref), channel_id=1, source_target_pairs={{0,4},{1,5},{2,6},{3,7},{4,0},{5,1},{6,2},{7,3},{8,12},{9,13},{10,... | collective-permute-start | bytes 393224 | tf_op jit(solution)/shard_map/ppermute | solution.py:26
  147.7 7.8 %collective-permute-start.14 = (bf16[2,32,1024]{2,1,0:T(8,128)(2,1)S(1)}, bf16[2,32,1024]{2,1,0:T(8,128)(2,1)S(1)}, u32[]{:S(2)}, u32[]{:S(2)}) collective-permute-start(bf16[2,32,1024]{2,1,0:T(8,128)(2,1)S(1)} %pair.1.p0_ref), channel_id=1, source_target_pairs={{0,6},{1,7},{2,0},{3,1},{4,2},{5,3},{6,4},{7,5},{8,14},{9,15},{10,... | collective-permute-start | bytes 393224 | tf_op jit(solution)/shard_map/ppermute | solution.py:26

commit v7 on v6

--- a/solution.py
+++ b/solution.py
@@ -426,7 +426,7 @@
     )
     sibling = [to_core(s) for s in sibling]
     terms = add(own_terms(blocks + core, normed, both, near), sibling, inv)
-    terms, near, *far = release([terms, near, *far], inv)
+    near, *far = release([near, *far], terms)
     got = lax.all_to_all(terms.reshape(64, 32, 2 * feats), ("x", "zh", "y", "zl"), 0, 0, tiled=True)
 
     weights = [near, to_core(near)]

time: 159 us -> 150 us (0.943)
  waiting for transfers between devices: 24.2 us -> 14.3 us
  local copies, waits for them, and re-layouts: 9.42 us -> 12 us
    ppermute x16, waiting for transfers between devices: 13.9 us -> 8.49 us  [send(): return lax.ppermute(value, AXES, pairs)]
    all_to_all x1, waiting for transfers between devices: 10.3 us -> 5.77 us  [shards(): lax.all_to_all(terms.reshape(64, 32, 2 * feats), ('x', 'zh', 'y', 'zl'),...]
    unnamed x15, local copies, waits for them, and re-layouts: 3.24 us -> 5.92 us
    ppermute x16, starting transfers between devices: 16.8 us -> 14.9 us  [send(): return lax.ppermute(value, AXES, pairs)]
  transfers between devices with their start and end apart: 18 -> 18, of which waited for: 7 -> 6; matrix products, arithmetic and copies ran while one was open for 4% -> 4% of each run, Pallas kernels for 41% -> 44%
where the time goes in v7:
time: 150 us; the launch traced here: 148 us
  Pallas kernels  70 us (47%)
  starting transfers between devices  31 us (21%)
  blocking collectives  17.2 us (11%)
  waiting for transfers between devices  14.3 us (10%)
  local copies, waits for them, and re-layouts  12 us (8%)
  other arithmetic  2.31 us (2%)
    pallas_call x1, Pallas kernels, backward(): pl.pallas_call(backward_kernel, grid_spec=pltpu.PrefetchScalarGridSpec(nu...  17.7 us
    all_to_all x1, blocking collectives, shards(): lax.all_to_all(gain_rows, ('x', 'zh', 'y', 'zl'), 0, 0, tiled=True)  17.2 us
    pallas_call x1, Pallas kernels, forward(): pl.pallas_call(forward_kernel, grid_spec=pltpu.PrefetchScalarGridSpec(num...  16.2 us
    pallas_call x1, Pallas kernels, norm_and_terms(): pl.pallas_call(norm_kernel, grid_spec=pltpu.PrefetchScalarGridSpec(num_sc...  15.6 us
    ppermute x16, starting transfers between devices, send(): return lax.ppermute(value, AXES, pairs)  14.9 us
    all_to_all x1, starting transfers between devices, shards(): lax.all_to_all(terms.reshape(64, 32, 2 * feats), ('x', 'zh', 'y', 'zl'),...  11.3 us
    pallas_call x1, Pallas kernels, own_terms(): pl.pallas_call(own_kernel, grid_spec=pltpu.PrefetchScalarGridSpec(num_sca...  9.28 us
    ppermute x16, waiting for transfers between devices, send(): return lax.ppermute(value, AXES, pairs)  8.49 us
  transfers between devices with their start and end apart: 18, of which 6 were waited for; matrix products, arithmetic and copies ran while one was open for 4% of the time, Pallas kernels for 44%

profile of v7, /device:TPU:2, one launch (start us, length us, event | category | flops | bytes accessed | tf_op | source)
XLA Modules:
  0.0 147.6 jit_solution(10579589866072362117)
XLA Ops:
  0.6 1.0 constant_dynamic-update-slice_fusion.1
  1.6 1.0 constant_dynamic-update-slice_fusion
  2.6 1.6 %broadcast_in_dim.2.after_ref = bf16[4,256,1024]{2,1,0:T(8,128)(2,1)} broadcast(bf16[256,1024]{1,0:T(8,128)(2,1)S(1)} %constant_dynamic-update-slice_fusion), dimensions={1,2} | broadcast | bytes 2621440 | tf_op jit(solution)/shard_map/broadcast_in_dim | solution.py:418
  4.2 4.8 %all-to-all-start = ((bf16[4,256,1024]{2,1,0:T(8,128)(2,1)}), bf16[4,256,1024]{2,1,0:T(8,128)(2,1)S(1)}, u32[]{:S(2)}, u32[]{:S(2)}) async-start(bf16[4,256,1024]{2,1,0:T(8,128)(2,1)} %broadcast_in_dim.2.after_ref), calls=%async_computation | async-start | bytes 4194304 | tf_op jit(solution)/shard_map/all_to_all | solution.py:419
  9.1 3.9 %collective-permute-start = (bf16[256,1024]{1,0:T(8,128)(2,1)S(1)}, bf16[256,1024]{1,0:T(8,128)(2,1)S(1)}, u32[]{:S(2)}, u32[]{:S(2)}) collective-permute-start(bf16[256,1024]{1,0:T(8,128)(2,1)S(1)} %constant_dynamic-update-slice_fusion), channel_id=1, source_target_pairs={{0,16},{1,17},{2,18},{3,19},{4,20},{5,21},{6,22},{7,23},{8,24},{9,... | collective-permute-start | bytes 1572872 | tf_op jit(solution)/shard_map/ppermute | solution.py:26
  13.4 15.6 %norm_and_terms.1 = (bf16[1024,1024]{1,0:T(8,128)(2,1)}, f32[1024,128]{1,0:T(8,128)}, bf16[1024,4096]{1,0:T(8,128)(2,1)}, bf16[4,256,1024]{2,1,0:T(8,128)(2,1)}, bf16[4,256,1024]{2,1,0:T(8,128)(2,1)}) custom-call(s32[8]{0:T(128)} %add_subtract_fusion.order_ref, bf16[1024,4096]{1,0:T(8,128)(2,1)} %tok_ref.3, f32[1,4096]{1,0:T(1,128)} %bitcast.24, ...), custom_call_target="tpu_custom_call" | custom-call | flops 10485760000 | bytes 20971520 | tf_op jit(solution)/shard_map/norm_and_terms/pallas_call | solution.py:100
  30.2 1.5 collective-permute-start.1
  31.7 0.7 collective-permute-start.2
  32.4 2.5 %collective-permute-start.3 = (bf16[256,1024]{1,0:T(8,128)(2,1)S(1)}, bf16[256,1024]{1,0:T(8,128)(2,1)}, u32[]{:S(2)}, u32[]{:S(2)}) collective-permute-start(bf16[256,1024]{1,0:T(8,128)(2,1)S(1)} %collective-permute-done.refs_1_), channel_id=1, source_target_pairs={{0,96},{1,97},{2,98},{3,99},{4,100},{5,101},{6,102},{7,103},{8,104... | collective-permute-start | bytes 1572872 | tf_op jit(solution)/shard_map/ppermute | solution.py:26
  34.9 1.4 copy-done.1
  36.3 9.3 %own_terms.1.own_ref = bf16[8,256,1024]{2,1,0:T(8,128)(2,1)} custom-call(s32[8]{0:T(128)} %fusion.4.order_ref, bf16[1024,4096]{1,0:T(8,128)(2,1)} %get-tuple-element.23.n0_ref.n1_ref.normed_ref, bf16[1024,4096]{1,0:T(8,128)(2,1)} %get-tuple-element.23.n0_ref.n1_ref.normed_ref, bf16[1024,1024]{1,0:T(8,128)(2,1)} %get-tuple-element.24.both_ref, ...), custom_call_target="tpu_custom_call" | custom-call | flops 31457280000 | tf_op jit(solution)/shard_map/own_terms/pallas_call | solution.py:147
  45.6 6.0 %add.81.refs_5_.refs_10_ = bf16[8,256,1024]{2,1,0:T(8,128)(2,1)} custom-call(bf16[8,256,1024]{2,1,0:T(8,128)(2,1)} %own_terms.1.own_ref, bf16[4,256,1024]{2,1,0:T(8,128)(2,1)} %collective-permute-done.4.got0_ref, bf16[4,256,1024]{2,1,0:T(8,128)(2,1)} %collective-permute-done.5.got1_ref, f32[1024,128]{1,0:T(8,128)} %get-tuple-element.25.after_ref.inv_ref), custom_call_target="tpu_custom_call" | custom-call | tf_op jit(solution)/shard_map/add/pallas_call | solution.py:172
  51.6 11.3 %all-to-all-start.1 = ((bf16[64,32,1024]{2,1,0:T(8,128)(2,1)}), bf16[64,32,1024]{2,1,0:T(8,128)(2,1)}, u32[]{:S(2)}, u32[]{:S(2)}) async-start(bf16[64,32,1024]{2,1,0:T(8,128)(2,1)} %bitcast.20), calls=%async_computation.1 | async-start | bytes 8388608 | tf_op jit(solution)/shard_map/all_to_all | solution.py:430
  63.0 0.8 copy-done.3
  64.8 0.8 dynamic_slice.11
  67.4 1.4 constant_dynamic-slice_fusion
  68.8 0.8 collective-permute-done.10.refs_9_
  69.6 1.5 %collective-permute-done.7.refs_3_ = bf16[256,1024]{1,0:T(8,128)(2,1)S(1)} collective-permute-done((bf16[256,1024]{1,0:T(8,128)(2,1)}, bf16[256,1024]{1,0:T(8,128)(2,1)S(1)}, u32[]{:S(2)}, u32[]{:S(2)}) %collective-permute-start.7) | collective-permute-done | bytes 524320 | tf_op jit(solution)/shard_map/ppermute | solution.py:26
  71.2 0.7 copy-done.6
  71.9 1.3 copy-done.4
  73.2 16.2 %forward.1 = (bf16[1024,512]{1,0:T(8,128)(2,1)}, bf16[1024,512]{1,0:T(8,128)(2,1)}, f32[1024,128]{1,0:T(8,128)}) custom-call(s32[3]{0:T(128)} %pad_add_fusion.place_ref, bf16[1024,4096]{1,0:T(8,128)(2,1)} %get-tuple-element.23.n0_ref.n1_ref.normed_ref, bf16[1024,1024]{1,0:T(8,128)(2,1)} %get-tuple-element.24.both_ref, ...), custom_call_target="tpu_custom_call" | custom-call | flops 8589934592 | bytes 20971520 | tf_op jit(solution)/shard_map/forward/pallas_call | solution.py:248
  89.4 17.7 %backward.1.refs_4_ = bf16[1024,4096]{1,0:T(8,128)(2,1)} custom-call(s32[9]{0:T(128)} %pad_add_fusion.1.place_ref, bf16[1024,4096]{1,0:T(8,128)(2,1)} %tok_ref.3, bf16[1024,1024]{1,0:T(8,128)(2,1)} %get-tuple-element.24.both_ref, f32[1024,128]{1,0:T(8,128)} %get-tuple-element.25.after_ref.inv_ref, f32[1024,128]{1,0:T(8,128)} %get-tuple-element.35.coef_ref, ...), custom_call_target="tpu_custom_call" | custom-call | flops 8589934592 | bytes 29360128 | tf_op jit(solution)/shard_map/backward/pallas_call | solution.py:292
  107.1 5.8 %all-to-all-done.1.refs_0_ = bf16[64,32,1024]{2,1,0:T(8,128)(2,1)} async-done(((bf16[64,32,1024]{2,1,0:T(8,128)(2,1)}), bf16[64,32,1024]{2,1,0:T(8,128)(2,1)}, u32[]{:S(2)}, u32[]{:S(2)}) %all-to-all-start.1) | async-done | bytes 4194336 | tf_op jit(solution)/shard_map/all_to_all | solution.py:430
  112.9 4.1 %total.1 = (bf16[32,1024]{1,0:T(8,128)(2,1)}, f32[64,128]{1,0:T(8,128)}) custom-call(bf16[64,32,1024]{2,1,0:T(8,128)(2,1)} %all-to-all-done.1.refs_0_, bf16[32,512]{1,0:T(8,128)(2,1)} %get-tuple-element.45.refs_1_, bf16[32,512]{1,0:T(8,128)(2,1)} %get-tuple-element.44.refs_2_, f32[1,128]{1,0:T(1,128)} %reshape_tile.3.refs_3_, bf16[1024,4096]{1,0:T(8,128)(2,1)} %backward.1.refs_4_), custom_call_target="tpu_custom_call" | custom-call | flops 2097152 | bytes 5242880 | tf_op jit(solution)/shard_map/total/pallas_call | solution.py:345
  117.0 0.8 collective-permute-start.11
  117.8 17.2 %all_to_all.19 = f32[64,1,128]{2,1,0:T(1,128)S(1)} all-to-all(f32[64,1,128]{2,1,0:T(1,128)} %bitcast.23), channel_id=1, replica_groups=mesh['x'=4,'zh'=2,'c'=2,'y'=4,'zl'=2] {'x','zh','y','zl'}, dimensions={0} | all-to-all | bytes 65536 | tf_op jit(solution)/shard_map/all_to_all | solution.py:446
  135.1 0.8 copy-done
  136.6 2.2 %collective-permute-start.13 = (bf16[2,32,1024]{2,1,0:T(8,128)(2,1)S(1)}, bf16[2,32,1024]{2,1,0:T(8,128)(2,1)S(1)}, u32[]{:S(2)}, u32[]{:S(2)}) collective-permute-start(bf16[2,32,1024]{2,1,0:T(8,128)(2,1)S(1)} %pair.1.p0_ref), channel_id=1, source_target_pairs={{0,4},{1,5},{2,6},{3,7},{4,0},{5,1},{6,2},{7,3},{8,12},{9,13},{10,... | collective-permute-start | bytes 393224 | tf_op jit(solution)/shard_map/ppermute | solution.py:26
  138.8 1.0 collective-permute-start.14
  139.8 0.7 reshape.41
  140.5 5.4 %collective-permute-done.12.p1_ref = bf16[2,32,1024]{2,1,0:T(8,128)(2,1)S(1)} collective-permute-done((bf16[2,32,1024]{2,1,0:T(8,128)(2,1)S(1)}, bf16[2,32,1024]{2,1,0:T(8,128)(2,1)S(1)}, u32[]{:S(2)}, u32[]{:S(2)}) %collective-permute-start.12) | collective-permute-done | bytes 131104 | tf_op jit(solution)/shard_map/ppermute | solution.py:26
  146.5 1.0 finish.1
  (43 shorter events, 6.0 us)
Async XLA Ops:
  4.2 30.7 %all-to-all-start = ((bf16[4,256,1024]{2,1,0:T(8,128)(2,1)}), bf16[4,256,1024]{2,1,0:T(8,128)(2,1)S(1)}, u32[]{:S(2)}, u32[]{:S(2)}) async-start(bf16[4,256,1024]{2,1,0:T(8,128)(2,1)} %broadcast_in_dim.2.after_ref), calls=%async_computation | async-start | bytes 4194304 | tf_op jit(solution)/shard_map/all_to_all | solution.py:419
  9.1 21.2 %collective-permute-start = (bf16[256,1024]{1,0:T(8,128)(2,1)S(1)}, bf16[256,1024]{1,0:T(8,128)(2,1)S(1)}, u32[]{:S(2)}, u32[]{:S(2)}) collective-permute-start(bf16[256,1024]{1,0:T(8,128)(2,1)S(1)} %constant_dynamic-update-slice_fusion), channel_id=1, source_target_pairs={{0,16},{1,17},{2,18},{3,19},{4,20},{5,21},{6,22},{7,23},{8,24},{9,... | collective-permute-start | bytes 1572872 | tf_op jit(solution)/shard_map/ppermute | solution.py:26
  29.1 16.5 %collective-permute-start.4 = (bf16[4,256,1024]{2,1,0:T(8,128)(2,1)}, bf16[4,256,1024]{2,1,0:T(8,128)(2,1)}, u32[]{:S(2)}, u32[]{:S(2)}) collective-permute-start(bf16[4,256,1024]{2,1,0:T(8,128)(2,1)} %get-tuple-element.26), channel_id=1, source_target_pairs={{0,8},{1,9},{2,10},{3,11},{4,12},{5,13},{6,14},{7,15},{8,0},{9,1},... | collective-permute-start | bytes 6291464 | tf_op jit(solution)/shard_map/ppermute | solution.py:26
  29.2 16.4 %collective-permute-start.5 = (bf16[4,256,1024]{2,1,0:T(8,128)(2,1)}, bf16[4,256,1024]{2,1,0:T(8,128)(2,1)}, u32[]{:S(2)}, u32[]{:S(2)}) collective-permute-start(bf16[4,256,1024]{2,1,0:T(8,128)(2,1)} %get-tuple-element.27), channel_id=1, source_target_pairs={{0,8},{1,9},{2,10},{3,11},{4,12},{5,13},{6,14},{7,15},{8,0},{9,1},... | collective-permute-start | bytes 6291464 | tf_op jit(solution)/shard_map/ppermute | solution.py:26
  30.2 15.3 %copy-start.2 = (bf16[256,1024]{1,0:T(8,128)(2,1)}, bf16[256,1024]{1,0:T(8,128)(2,1)S(1)}, u32[]{:S(2)}) copy-start(bf16[256,1024]{1,0:T(8,128)(2,1)S(1)} %collective-permute-done.refs_1_) | copy-start | bytes 1572868
  30.2 32.7 %collective-permute-start.1 = (bf16[256,1024]{1,0:T(8,128)(2,1)S(1)}, bf16[256,1024]{1,0:T(8,128)(2,1)S(1)}, u32[]{:S(2)}, u32[]{:S(2)}) collective-permute-start(bf16[256,1024]{1,0:T(8,128)(2,1)S(1)} %collective-permute-done.refs_1_), channel_id=1, source_target_pairs={{0,32},{1,33},{2,34},{3,35},{4,36},{5,37},{6,38},{7,39},{8,40},{9,... | collective-permute-start | bytes 1572872 | tf_op jit(solution)/shard_map/ppermute | solution.py:26
  31.7 31.3 %collective-permute-start.2 = (bf16[256,1024]{1,0:T(8,128)(2,1)S(1)}, bf16[256,1024]{1,0:T(8,128)(2,1)}, u32[]{:S(2)}, u32[]{:S(2)}) collective-permute-start(bf16[256,1024]{1,0:T(8,128)(2,1)S(1)} %collective-permute-done.refs_1_), channel_id=1, source_target_pairs={{0,64},{1,65},{2,66},{3,67},{4,68},{5,69},{6,70},{7,71},{8,72},{9,... | collective-permute-start | bytes 1572872 | tf_op jit(solution)/shard_map/ppermute | solution.py:26
  32.4 30.6 %collective-permute-start.3 = (bf16[256,1024]{1,0:T(8,128)(2,1)S(1)}, bf16[256,1024]{1,0:T(8,128)(2,1)}, u32[]{:S(2)}, u32[]{:S(2)}) collective-permute-start(bf16[256,1024]{1,0:T(8,128)(2,1)S(1)} %collective-permute-done.refs_1_), channel_id=1, source_target_pairs={{0,96},{1,97},{2,98},{3,99},{4,100},{5,101},{6,102},{7,103},{8,104... | collective-permute-start | bytes 1572872 | tf_op jit(solution)/shard_map/ppermute | solution.py:26
  34.9 1.4 copy-start.1
  51.6 61.3 %all-to-all-start.1 = ((bf16[64,32,1024]{2,1,0:T(8,128)(2,1)}), bf16[64,32,1024]{2,1,0:T(8,128)(2,1)}, u32[]{:S(2)}, u32[]{:S(2)}) async-start(bf16[64,32,1024]{2,1,0:T(8,128)(2,1)} %bitcast.20), calls=%async_computation.1 | async-start | bytes 8388608 | tf_op jit(solution)/shard_map/all_to_all | solution.py:430
  63.0 0.8 copy-start.3
  63.7 7.5 %collective-permute-start.6 = (bf16[4,256,1024]{2,1,0:T(8,128)(2,1)}, bf16[4,256,1024]{2,1,0:T(8,128)(2,1)S(1)}, u32[]{:S(2)}, u32[]{:S(2)}) collective-permute-start(bf16[4,256,1024]{2,1,0:T(8,128)(2,1)} %get-tuple-element.28.refs_0_), channel_id=1, source_target_pairs={{0,8},{1,9},{2,10},{3,11},{4,12},{5,13},{6,14},{7,15},{8,0},{9,1},... | collective-permute-start | bytes 6291464 | tf_op jit(solution)/shard_map/ppermute | solution.py:26
  63.7 5.9 %collective-permute-start.10 = (bf16[256,1024]{1,0:T(8,128)(2,1)}, bf16[256,1024]{1,0:T(8,128)(2,1)S(1)}, u32[]{:S(2)}, u32[]{:S(2)}) collective-permute-start(bf16[256,1024]{1,0:T(8,128)(2,1)} %get-tuple-element.32.refs_8_), channel_id=1, source_target_pairs={{0,8},{1,9},{2,10},{3,11},{4,12},{5,13},{6,14},{7,15},{8,0},{9,1},... | collective-permute-start | bytes 1572872 | tf_op jit(solution)/shard_map/ppermute | solution.py:26
  64.3 6.9 %collective-permute-start.7 = (bf16[256,1024]{1,0:T(8,128)(2,1)}, bf16[256,1024]{1,0:T(8,128)(2,1)S(1)}, u32[]{:S(2)}, u32[]{:S(2)}) collective-permute-start(bf16[256,1024]{1,0:T(8,128)(2,1)} %get-tuple-element.29.refs_2_), channel_id=1, source_target_pairs={{0,8},{1,9},{2,10},{3,11},{4,12},{5,13},{6,14},{7,15},{8,0},{9,1},... | collective-permute-start | bytes 1572872 | tf_op jit(solution)/shard_map/ppermute | solution.py:26
  64.3 6.9 %collective-permute-start.8 = (bf16[256,1024]{1,0:T(8,128)(2,1)}, bf16[256,1024]{1,0:T(8,128)(2,1)}, u32[]{:S(2)}, u32[]{:S(2)}) collective-permute-start(bf16[256,1024]{1,0:T(8,128)(2,1)} %get-tuple-element.30.refs_4_), channel_id=1, source_target_pairs={{0,8},{1,9},{2,10},{3,11},{4,12},{5,13},{6,14},{7,15},{8,0},{9,1},... | collective-permute-start | bytes 1572872 | tf_op jit(solution)/shard_map/ppermute | solution.py:26
  64.8 6.5 %collective-permute-start.9 = (bf16[256,1024]{1,0:T(8,128)(2,1)}, bf16[256,1024]{1,0:T(8,128)(2,1)}, u32[]{:S(2)}, u32[]{:S(2)}) collective-permute-start(bf16[256,1024]{1,0:T(8,128)(2,1)} %get-tuple-element.31.refs_6_), channel_id=1, source_target_pairs={{0,8},{1,9},{2,10},{3,11},{4,12},{5,13},{6,14},{7,15},{8,0},{9,1},... | collective-permute-start | bytes 1572872 | tf_op jit(solution)/shard_map/ppermute | solution.py:26
  69.6 1.6 %copy-start.5 = (bf16[256,1024]{1,0:T(8,128)(2,1)}, bf16[256,1024]{1,0:T(8,128)(2,1)S(1)}, u32[]{:S(2)}) copy-start(bf16[256,1024]{1,0:T(8,128)(2,1)S(1)} %collective-permute-done.10.refs_9_) | copy-start | bytes 1572868
  71.1 0.8 copy-start.6
  71.9 1.3 copy-start.4
  117.0 18.1 %collective-permute-start.11 = (bf16[32,1024]{1,0:T(8,128)(2,1)}, bf16[32,1024]{1,0:T(8,128)(2,1)S(1)}, u32[]{:S(2)}, u32[]{:S(2)}) collective-permute-start(bf16[32,1024]{1,0:T(8,128)(2,1)} %get-tuple-element.36.mine_ref), channel_id=1, source_target_pairs={{0,1},{1,0},{2,3},{3,2},{4,5},{5,4},{6,7},{7,6},{8,9},{9,8},{10,11... | collective-permute-start | bytes 196616 | tf_op jit(solution)/shard_map/ppermute | solution.py:26
  135.1 4.7 %collective-permute-start.15 = (f32[4,2,8,32]{3,2,1,0:T(8,128)S(1)}, f32[4,2,8,32]{3,2,1,0:T(8,128)S(1)}, u32[]{:S(2)}, u32[]{:S(2)}) collective-permute-start(f32[4,2,8,32]{3,2,1,0:T(8,128)S(1)} %bitcast.21), channel_id=1, source_target_pairs={{0,8},{1,9},{2,10},{3,11},{4,12},{5,13},{6,14},{7,15},{8,0},{9,1},... | collective-permute-start | bytes 24584 | tf_op jit(solution)/shard_map/ppermute | solution.py:26
  135.1 0.8 copy-start
  135.9 10.0 %collective-permute-start.12 = (bf16[2,32,1024]{2,1,0:T(8,128)(2,1)S(1)}, bf16[2,32,1024]{2,1,0:T(8,128)(2,1)S(1)}, u32[]{:S(2)}, u32[]{:S(2)}) collective-permute-start(bf16[2,32,1024]{2,1,0:T(8,128)(2,1)S(1)} %pair.1.p0_ref), channel_id=1, source_target_pairs={{0,2},{1,3},{2,4},{3,5},{4,6},{5,7},{6,0},{7,1},{8,10},{9,11},{10,... | collective-permute-start | bytes 393224 | tf_op jit(solution)/shard_map/ppermute | solution.py:26
  136.6 9.4 %collective-permute-start.13 = (bf16[2,32,1024]{2,1,0:T(8,128)(2,1)S(1)}, bf16[2,32,1024]{2,1,0:T(8,128)(2,1)S(1)}, u32[]{:S(2)}, u32[]{:S(2)}) collective-permute-start(bf16[2,32,1024]{2,1,0:T(8,128)(2,1)S(1)} %pair.1.p0_ref), channel_id=1, source_target_pairs={{0,4},{1,5},{2,6},{3,7},{4,0},{5,1},{6,2},{7,3},{8,12},{9,13},{10,... | collective-permute-start | bytes 393224 | tf_op jit(solution)/shard_map/ppermute | solution.py:26
  138.8 7.8 %collective-permute-start.14 = (bf16[2,32,1024]{2,1,0:T(8,128)(2,1)S(1)}, bf16[2,32,1024]{2,1,0:T(8,128)(2,1)S(1)}, u32[]{:S(2)}, u32[]{:S(2)}) collective-permute-start(bf16[2,32,1024]{2,1,0:T(8,128)(2,1)S(1)} %pair.1.p0_ref), channel_id=1, source_target_pairs={{0,6},{1,7},{2,0},{3,1},{4,2},{5,3},{6,4},{7,5},{8,14},{9,15},{10,... | collective-permute-start | bytes 393224 | tf_op jit(solution)/shard_map/ppermute | solution.py:26
